TPU v7x, 32 devices: a whole 2x2x4 slice. The times are simulated.
32 devices in a mesh: grp: 4 (over z), req: 8 (over y, x, core).
Axes of the slice: x: 2, y: 2, z: 4, core: 2. Of those that a mesh axis runs over, the one named last changes fastest.
Arguments:
- tokens: bfloat16 [4, 2048, 1024], P('grp', 'req'), may hold values from -6 to 6
- attn_gain: float32 [1024], replicated, may hold values from 0.5 to 1.5
- w_query: bfloat16 [1024, 1024], replicated, may hold values from -0.75 to 0.75
- w_key: bfloat16 [1024, 512], replicated, may hold values from -0.75 to 0.75
- w_value: bfloat16 [1024, 512], replicated, may hold values from -0.1875 to 0.1875
- w_out: bfloat16 [1024, 1024], replicated, may hold values from -0.1875 to 0.1875
- prefix_keys: bfloat16 [4, 2048, 512], P('grp', 'req'), may hold values from -1600 to 1600
- prefix_values: bfloat16 [4, 2048, 512], P('grp', 'req'), may hold values from -6 to 6
- lengths: int32 [4, 8], P('grp'), may hold values from 1 to 256, 1536 in all within a row
- assignment: int32 [4, 8], P('grp'), may hold values from 0 to 7, each once within a row
- moe_gain: float32 [1024], replicated, may hold values from 0.5 to 1.5
- expert_ids: int32 [4, 2048, 8], P('grp', 'req'), may hold values from 0 to 31, all different within a row; in each aligned block of 256 rows (0 to 255, 256 to 511, ..., all dimensions but the last counted through in order) at most 96 rows name the same one
- route_weights: float32 [4, 2048, 8], P('grp', 'req'), may hold values from 0.1 to 0.4
- w_gate: bfloat16 [32, 1024, 512], P('req'), may hold values from -0.1875 to 0.1875
- w_up: bfloat16 [32, 1024, 512], P('req'), may hold values from -0.1875 to 0.1875
- w_down: bfloat16 [32, 512, 1024], P('req'), may hold values from -0.25 to 0.25
Outputs:
- context: bfloat16 [4, 2048, 1024], P('grp', 'req')
- hidden: bfloat16 [4, 2048, 1024], P('grp', 'req')
- expert_mix: bfloat16 [4, 2048, 1024], P('grp', 'req')
Inputs may be any that keep to these rules, and one draw needn't show every extreme that they name: `lengths`: each row sums to 1536, and some request of each row has exactly 256. `assignment`: each row names every request once. `expert_ids`: each token slot names 8 different experts; within the rows of one req index no expert is named more than 96 times, a bound that some block reaches.
All inputs are finite; a program needn't handle non-finite values.
Results may differ from a plain program's by a relative error of at most 0.014.
The roundings to bfloat16 on the way count: a program that leaves them out, or rounds other values in their place, can miss the bound.
Values may be sent and summed in bfloat16 or wider, within the bound.
No kernel may reach another device: no remote copies, remote signals or barrier semaphores. Data moves between devices by JAX's collectives and lax.ppermute only.
A program may use at most 256 MiB of HBM per device.

v0:
```python
import math

import jax
import jax.numpy as jnp
from jax import lax
from jax.sharding import PartitionSpec as P

H = 16
KV = 8
HD = 64
EXPERTS = 32
TOP = 8
CAP = 96


NORM_EPS = 1e-06
ATTN_SCALE = 0.015625
RESIDUAL_SCALE = 0.22
ROPE_BASE = 10000.0


def normalize(head_rows, gain):
    widened = head_rows.astype(jnp.float32)
    mean_square = jnp.mean(widened * widened, axis=-1, keepdims=True)
    return (widened * lax.rsqrt(mean_square + NORM_EPS) * gain).astype(jnp.bfloat16)


def rotate(head_rows, positions):
    half_dim = head_rows.shape[-1] // 2
    frequency = ROPE_BASE ** (
        -(jnp.arange(half_dim, dtype=jnp.float32) * 2.0 / head_rows.shape[-1])
    )
    angles = positions[:, None] * frequency[None, :]
    cosine = jnp.cos(angles)[:, None, :]
    sine_part = jnp.sin(angles)[:, None, :]
    first_half = head_rows[..., :half_dim]
    second_half = head_rows[..., half_dim:]
    return jnp.concatenate(
        [
            first_half * cosine - second_half * sine_part,
            second_half * cosine + first_half * sine_part,
        ],
        axis=-1,
    )


def fresh_state(tok_count):
    return (
        jnp.full((KV, H // KV, tok_count), -jnp.inf, jnp.float32),
        jnp.zeros((KV, H // KV, tok_count), jnp.float32),
        jnp.zeros((KV, H // KV, tok_count, HD), jnp.float32),
    )


def absorb(run_state, grouped, key_rows, value_rows, visible):
    run_max, run_sum, run_acc = run_state
    scores = (
        jnp.einsum("tkgd,skd->kgts", grouped, key_rows, preferred_element_type=jnp.float32)
        * ATTN_SCALE
    )
    scores = jnp.where(visible, scores, -jnp.inf)
    new_max = jnp.maximum(run_max, jnp.max(scores, axis=-1))
    factor = jnp.exp(run_max - new_max)
    weights = jnp.exp(scores - new_max[..., None])
    run_sum = run_sum * factor + jnp.sum(weights, axis=-1)
    gathered_values = jnp.einsum(
        "kgts,skd->kgtd",
        weights.astype(jnp.bfloat16),
        value_rows,
        preferred_element_type=jnp.float32,
    )
    run_acc = run_acc * factor[..., None] + gathered_values
    return (new_max, run_sum, run_acc)


def slot_numbers(ids):
    chosen = ids.reshape(-1)
    hit_table = (chosen[:, None] == jnp.arange(EXPERTS, dtype=jnp.int32)[None, :]).astype(jnp.int32)
    before = jnp.cumsum(hit_table, axis=0) - hit_table
    ranked = jnp.sum(before * hit_table, axis=1)
    return (chosen, ranked)


def local(
    tokens,
    attn_gain,
    w_query,
    w_key,
    w_value,
    w_out,
    prefix_keys,
    prefix_values,
    lengths,
    assignment,
    moe_gain,
    expert_ids,
    route_weights,
    w_gate,
    w_up,
    w_down,
):
    tok_count = tokens.shape[1]
    model_width = tokens.shape[2]
    peer_count = lax.axis_size("req")
    prefix_len = prefix_keys.shape[1] * peer_count
    own_rows = tokens[0]
    normed = normalize(own_rows, attn_gain)
    my_index = lax.axis_index("req")
    request_ids = jnp.arange(lengths.shape[1], dtype=jnp.int32)
    request = jnp.sum(jnp.where(request_ids == my_index, assignment[0], 0))
    suffix_len = jnp.sum(jnp.where(request_ids == request, lengths[0], 0))
    positions = (prefix_len + jnp.arange(tok_count, dtype=jnp.int32)).astype(jnp.float32)
    queries = jnp.dot(normed, w_query, preferred_element_type=jnp.float32).reshape(tok_count, H, HD)
    queries = rotate(queries, positions).astype(jnp.bfloat16)
    suffix_keys = jnp.dot(normed, w_key, preferred_element_type=jnp.float32).reshape(
        tok_count, KV, HD
    )
    suffix_keys = rotate(suffix_keys, positions).astype(jnp.bfloat16)
    suffix_values = (
        jnp.dot(normed, w_value, preferred_element_type=jnp.float32)
        .astype(jnp.bfloat16)
        .reshape(tok_count, KV, HD)
    )
    grouped = queries.reshape(tok_count, KV, H // KV, HD)
    slot_row = jnp.arange(tok_count, dtype=jnp.int32)
    suffix_visible = (slot_row[None, :] <= slot_row[:, None]) & (slot_row[None, :] < suffix_len)
    suffix_state = absorb(
        fresh_state(tok_count), grouped, suffix_keys, suffix_values, suffix_visible[None, None]
    )
    run_state = suffix_state
    key_piece = lax.all_gather(prefix_keys, "req", axis=1, tiled=True)
    value_piece = lax.all_gather(prefix_values, "req", axis=1, tiled=True)
    piece_len = key_piece.shape[1]
    key_block = math.gcd(piece_len, 512)
    key_blocks = key_piece[0].reshape(piece_len // key_block, key_block, KV, HD)
    value_blocks = value_piece[0].reshape(piece_len // key_block, key_block, KV, HD)

    def absorb_step(carry, pair_set):
        return (absorb(carry, grouped, pair_set[0], pair_set[1], True), None)

    run_state, unused = lax.scan(absorb_step, run_state, (key_blocks, value_blocks))
    run_max, run_sum, run_acc = run_state
    context = (
        (run_acc / run_sum[..., None])
        .transpose(2, 0, 1, 3)
        .reshape(tok_count, H * HD)
        .astype(jnp.bfloat16)
    )
    projected = jnp.dot(context, w_out, preferred_element_type=jnp.float32)
    hidden = (own_rows.astype(jnp.float32) + RESIDUAL_SCALE * projected).astype(jnp.bfloat16)
    moe_in = normalize(hidden, moe_gain)
    chosen, ranked = slot_numbers(expert_ids[0])
    slot_index = chosen * CAP + ranked
    sources = jnp.repeat(moe_in, TOP, axis=0)
    outgoing = jnp.zeros((EXPERTS * CAP, model_width), jnp.bfloat16).at[slot_index].set(sources)
    outgoing = outgoing.reshape(peer_count, EXPERTS // peer_count, CAP, model_width)
    arrived = lax.all_to_all(outgoing, "req", split_axis=0, concat_axis=0, tiled=True)
    slot_span = arrived.shape[2]
    results = []
    for expert_local in range(arrived.shape[1]):
        expert_rows = arrived[:, expert_local].reshape(-1, model_width)
        gate_act = jnp.dot(expert_rows, w_gate[expert_local], preferred_element_type=jnp.float32)
        up_act = jnp.dot(expert_rows, w_up[expert_local], preferred_element_type=jnp.float32)
        product = (jax.nn.silu(gate_act) * up_act).astype(jnp.bfloat16)
        expert_out = jnp.dot(
            product, w_down[expert_local], preferred_element_type=jnp.float32
        ).astype(jnp.bfloat16)
        results.append(expert_out.reshape(arrived.shape[0], slot_span, model_width))
    produced = jnp.stack(results, axis=1)
    returned = lax.all_to_all(produced, "req", split_axis=0, concat_axis=0, tiled=True).reshape(
        EXPERTS * CAP, model_width
    )
    picked = returned[slot_index].astype(jnp.float32).reshape(tok_count, TOP, model_width)
    expert_mix = jnp.sum(picked * route_weights[0][..., None], axis=1).astype(jnp.bfloat16)
    return (context[None], hidden[None], expert_mix[None])


def solution(mesh):
    placed = (
        P("grp", "req", None),
        P(),
        P(),
        P(),
        P(),
        P(),
        P("grp", "req", None),
        P("grp", "req", None),
        P("grp", None),
        P("grp", None),
        P(),
        P("grp", "req", None),
        P("grp", "req", None),
        P("req", None, None),
        P("req", None, None),
        P("req", None, None),
    )
    return jax.shard_map(
        local,
        mesh=mesh,
        in_specs=placed,
        out_specs=(P("grp", "req", None), P("grp", "req", None), P("grp", "req", None)),
        check_vma=False,
    )
```

profile of v0, /device:TPU:0, one launch (start us, length us, event | category | flops | bytes accessed | tf_op | source)
XLA Modules:
  0.0 346.9 jit_solution(10591844235018423723)
XLA Ops:
  11.7 4.0 %copy.46 = bf16[1024,1024]{0,1:T(8,128)(2,1)} copy(bf16[1024,1024]{1,0:T(8,128)(2,1)} %param.20) | data formatting | bytes 4194304 | tf_op args[2]
  15.6 2.3 copy.45
  19.9 9.1 %reduce-window.6 = s32[32,16,128]{2,1,0:T(8,128)S(1)} reduce-window(s32[32,16,128]{2,1,0:T(8,128)S(1)} %fusion.98, s32[]{:T(128)} %copy.89), window={size=1x1x128 pad=0_0x0_0x127_0}, to_apply=%region_9.10 | reduce-window | flops 8323072 | bytes 524292 | tf_op jit(solution)/shard_map/reduce-window
  32.6 2.4 fusion.99
  40.6 6.2 %reshape.271 = bf16[4,512,8,64]{3,2,1,0:T(8,128)(2,1)} reshape(bf16[1,2048,512]{2,1,0:T(8,128)(2,1)} %all-gather.3.cloned.1.call-done) | data formatting | bytes 4194304 | tf_op jit(solution)/shard_map/reshape;squeeze | solution.py:135
  46.7 5.5 %copy.51 = bf16[4,512,8,64]{1,3,2,0:T(8,128)(2,1)} copy(bf16[4,512,8,64]{3,2,1,0:T(8,128)(2,1)} %reshape.271) | data formatting | bytes 4194304 | tf_op jit(solution)/shard_map/while | solution.py:141
  52.2 18.2 %all-gather.5.cloned.1.call-done = bf16[1,2048,512]{2,1,0:T(8,128)(2,1)} async-done(((bf16[1,256,512]{2,1,0:T(8,128)(2,1)}), bf16[1,2048,512]{2,1,0:T(8,128)(2,1)}) %all-gather.5.cloned.1.call-update) | async-done | bytes 2097168 | tf_op jit(solution)/shard_map/all_gather | solution.py:132
  70.4 6.2 %reshape.272 = bf16[4,512,8,64]{3,2,1,0:T(8,128)(2,1)} reshape(bf16[1,2048,512]{2,1,0:T(8,128)(2,1)} %all-gather.5.cloned.1.call-done) | data formatting | bytes 4194304 | tf_op jit(solution)/shard_map/reshape;squeeze | solution.py:136
  76.6 5.5 %copy.52 = bf16[4,512,8,64]{1,3,2,0:T(8,128)(2,1)} copy(bf16[4,512,8,64]{3,2,1,0:T(8,128)(2,1)} %reshape.272) | data formatting | bytes 4194304 | tf_op jit(solution)/shard_map/while | solution.py:141
  82.0 27.4 %while.14 = (s32[]{:T(128)}, f32[8,2,256]{2,1,0:T(2,128)S(1)}, f32[8,2,256]{2,1,0:T(2,128)S(1)}, f32[8,2,256,64]{2,3,1,0:T(8,128)S(1)}, bf16[4,512,8,64]{1,3,2,0...) while((s32[]{:T(128)}, f32[8,2,256]{2,1,0:T(2,128)S(1)}, ...), condition=%wide.region_8.9_spmd, body=%wide.region_5.8_spmd.sunk | while | flops 554180608 | bytes 29099092 | solution.py:141
  82.1 2.5 bitcast_reduce_fusion.2
  86.0 2.9 fusion.138
  88.9 2.5 bitcast_reduce_fusion.2
  92.9 2.9 fusion.138
  95.7 2.5 bitcast_reduce_fusion.2
  99.7 2.9 fusion.138
  102.6 2.5 bitcast_reduce_fusion.2
  106.5 2.9 fusion.138
  111.9 13.5 %scatter_custom_fusion = bf16[3072,1024]{1,0:T(8,128)(2,1)} fusion(s32[2048]{0:T(1024)S(1)} %bitcast.258, bf16[]{:T(256)} %constant.60.clone.1, bf16[256,1024]{1,0:T(8,128)(2,1)S(1)} %fusion.46), kind=kCustom, calls=%fused_computation.24 | custom fusion | bytes 6815746 | tf_op jit(solution)/shard_map/scatter | solution.py:155
  125.5 75.2 %all_to_all.10 = bf16[8,4,96,1024]{3,2,1,0:T(8,128)(2,1)S(1)} all-to-all(bf16[8,4,96,1024]{3,2,1,0:T(8,128)(2,1)} %bitcast.224), channel_id=1, replica_groups=mesh['grp'=4,'req'=8] {'req'}, dimensions={0} | all-to-all | bytes 12582912 | tf_op jit(solution)/shard_map/all_to_all | solution.py:157
  203.5 2.2 fusion.65
  207.8 5.5 %convolution_convert_fusion.3 = bf16[768,1024]{1,0:T(8,128)(2,1)} fusion(f32[768,512]{1,0:T(8,128)} %fusion.65, bf16[768,1024]{1,0:T(8,128)(2,1)} %bitcast.243, bf16[4,512,1024]{2,1,0:T(8,128)(2,1)} %param.33, bf16[4,1024,512]{2,1,0:T(8,128)(2,1)} %param.32), kind=kOutput, calls=%fused_computation.41 | convolution fusion | flops 1613758464 | bytes 6815744 | tf_op jit(solution)/shard_map/dot_general | solution.py:165
  213.3 5.6 %convolution_convert_fusion.2 = bf16[768,1024]{1,0:T(8,128)(2,1)} fusion(f32[768,512]{1,0:T(8,128)} %fusion.60, bf16[768,1024]{1,0:T(8,128)(2,1)} %bitcast.240, bf16[4,512,1024]{2,1,0:T(8,128)(2,1)} %param.33, bf16[4,1024,512]{2,1,0:T(8,128)(2,1)} %param.32), kind=kOutput, calls=%fused_computation.40 | convolution fusion | flops 1613758464 | bytes 6815744 | tf_op jit(solution)/shard_map/dot_general | solution.py:165
  218.9 3.8 %fusion.55 = f32[768,512]{1,0:T(8,128)} fusion(bf16[768,1024]{1,0:T(8,128)(2,1)} %bitcast.236, bf16[4,1024,512]{2,1,0:T(8,128)(2,1)} %param.31), kind=kOutput, calls=%fused_computation.71 | convolution fusion | flops 805306368 | bytes 4194304 | tf_op jit(solution)/shard_map/dot_general | solution.py:162
  222.7 5.5 %convolution_convert_fusion.1 = bf16[768,1024]{1,0:T(8,128)(2,1)} fusion(f32[768,512]{1,0:T(8,128)} %fusion.55, bf16[768,1024]{1,0:T(8,128)(2,1)} %bitcast.237, bf16[4,512,1024]{2,1,0:T(8,128)(2,1)} %param.33, bf16[4,1024,512]{2,1,0:T(8,128)(2,1)} %param.32), kind=kOutput, calls=%fused_computation.39 | convolution fusion | flops 1613758464 | bytes 6815744 | tf_op jit(solution)/shard_map/dot_general | solution.py:165
  228.3 3.4 fusion.50
  231.6 5.0 %convolution_convert_fusion = bf16[768,1024]{1,0:T(8,128)(2,1)} fusion(f32[768,512]{1,0:T(8,128)} %fusion.50, bf16[768,1024]{1,0:T(8,128)(2,1)S(1)} %bitcast.234, bf16[4,512,1024]{2,1,0:T(8,128)(2,1)} %param.33, bf16[4,1024,512]{2,1,0:T(8,128)(2,1)} %param.32), kind=kOutput, calls=%fused_computation.38 | convolution fusion | flops 1613758464 | bytes 6815744 | tf_op jit(solution)/shard_map/dot_general | solution.py:165
  236.6 6.5 %pad_maximum_fusion = bf16[8,4,96,1024]{3,2,1,0:T(8,128)(2,1)} fusion(bf16[8,1,96,1024]{3,2,1,0:T(8,128)(2,1)} %bitcast.244, bf16[8,1,96,1024]{3,2,1,0:T(8,128)(2,1)} %bitcast.241, bf16[8,1,96,1024]{3,2,1,0:T(8,128)(2,1)} %bitcast.238, bf16[8,1,96,1024]{3,2,1,0:T(8,128)(2,1)} %bitcast.235), kind=kLoop, calls=%fused_computation.23 | loop fusion | flops 9437184 | bytes 12582912 | tf_op jit(solution)/shard_map/stack | solution.py:169
  243.2 5.2 %all-to-all-start.1 = ((bf16[8,4,96,1024]{3,2,1,0:T(8,128)(2,1)}), bf16[8,4,96,1024]{3,2,1,0:T(8,128)(2,1)}, u32[]{:S(2)}, u32[]{:S(2)}) async-start(bf16[8,4,96,1024]{3,2,1,0:T(8,128)(2,1)} %pad_maximum_fusion), calls=%async_computation.1 | async-start | bytes 12582912 | tf_op jit(solution)/shard_map/all_to_all | solution.py:170
  249.5 70.2 %all-to-all-done.1 = bf16[8,4,96,1024]{3,2,1,0:T(8,128)(2,1)} async-done(((bf16[8,4,96,1024]{3,2,1,0:T(8,128)(2,1)}), bf16[8,4,96,1024]{3,2,1,0:T(8,128)(2,1)}, u32[]{:S(2)}, u32[]{:S(2)}) %all-to-all-start.1) | async-done | bytes 6291488 | tf_op jit(solution)/shard_map/all_to_all | solution.py:170
  319.7 14.7 %gather_fusion = bf16[2048,1024]{1,0:T(8,128)(2,1)} fusion(bf16[3072,1024]{1,0:T(8,128)(2,1)} %bitcast.59, s32[2048]{0:T(1024)S(1)} %broadcast_clamp_fusion), kind=kCustom, calls=%fused_computation | custom fusion | bytes 8396800 | tf_op jit(solution)/shard_map/gather | solution.py:173
  334.4 5.6 %fusion.18 = bf16[256,1024]{1,0:T(8,128)(2,1)} fusion(bf16[2048,1024]{1,0:T(8,128)(2,1)} %gather_fusion, f32[256,8]{1,0:T(8,128)S(1)} %copy.62), kind=kLoop, calls=%fused_computation.22 | loop fusion | flops 6029312 | bytes 4726784 | tf_op jit(solution)/shard_map/reduce_sum | solution.py:174
  (92 shorter events, 29.5 us)
Async XLA Ops:
  7.2 102.4 %copy-start = (bf16[1024,1024]{1,0:T(8,128)(2,1)S(1)}, bf16[1024,1024]{1,0:T(8,128)(2,1)}, u32[]{:S(2)}) copy-start(bf16[1024,1024]{1,0:T(8,128)(2,1)} %param.23) | copy-start | bytes 6291460
  7.2 33.4 %all-gather.3.cloned.1.call-start = ((), (), s32[]{:S(2)}) async-start(), calls=%async_computation.2 | async-start | bytes 2359296 | tf_op jit(solution)/shard_map/all_gather | solution.py:131
  7.9 62.5 %all-gather.5.cloned.1.call-start = ((), (), s32[]{:S(2)}) async-start(), calls=%async_computation.3 | async-start | bytes 2359296 | tf_op jit(solution)/shard_map/all_gather | solution.py:132
  15.6 2.3 copy-start.5
  15.6 2.3 copy-start.12
  18.0 12.1 %copy-start.13 = (s32[1,8]{1,0:T(1,128)S(1)}, s32[1,8]{1,0:T(1,128)}, u32[]{:S(2)}) copy-start(s32[1,8]{1,0:T(1,128)} %param.27) | copy-start | bytes 100
  18.0 12.7 %copy-start.14 = (s32[1,8]{1,0:T(1,128)S(1)}, s32[1,8]{1,0:T(1,128)}, u32[]{:S(2)}) copy-start(s32[1,8]{1,0:T(1,128)} %param.26) | copy-start | bytes 100
  35.1 1.4 copy-start.8
  109.5 2.4 copy-start.2
  109.6 2.1 copy-start.10
  111.7 13.8 %copy-start.4 = (bf16[256,1024]{1,0:T(8,128)(2,1)}, bf16[256,1024]{1,0:T(8,128)(2,1)S(1)}, u32[]{:S(2)}) copy-start(bf16[256,1024]{1,0:T(8,128)(2,1)S(1)} %get-tuple-element.96) | copy-start | bytes 1572868
  200.7 2.8 copy-start.11
  202.7 2.9 copy-start.7
  202.7 2.9 copy-start.6
  243.2 5.2 %copy-start.9 = (f32[1,256,8]{1,2,0:T(8,128)S(1)}, f32[1,256,8]{1,2,0:T(8,128)}, u32[]{:S(2)}) copy-start(f32[1,256,8]{1,2,0:T(8,128)} %param.30) | copy-start | bytes 24580
  243.2 5.3 %copy-start.3 = (bf16[8,2,256,64]{2,3,1,0:T(8,128)(2,1)S(1)}, bf16[8,2,256,64]{2,3,1,0:T(8,128)(2,1)}, u32[]{:S(2)}) copy-start(bf16[8,2,256,64]{2,3,1,0:T(8,128)(2,1)} %copy-done.2) | copy-start | bytes 1572868
  243.2 76.5 %all-to-all-start.1 = ((bf16[8,4,96,1024]{3,2,1,0:T(8,128)(2,1)}), bf16[8,4,96,1024]{3,2,1,0:T(8,128)(2,1)}, u32[]{:S(2)}, u32[]{:S(2)}) async-start(bf16[8,4,96,1024]{3,2,1,0:T(8,128)(2,1)} %pad_maximum_fusion), calls=%async_computation.1 | async-start | bytes 12582912 | tf_op jit(solution)/shard_map/all_to_all | solution.py:170
  319.7 20.4 %copy-start.1 = (bf16[1024,1024]{1,0:T(8,128)(2,1)S(1)}, bf16[1024,1024]{1,0:T(8,128)(2,1)}, u32[]{:S(2)}) copy-start(bf16[1024,1024]{1,0:T(8,128)(2,1)} %param.23) | copy-start | bytes 6291460
Sparse Core Ops, SparseCore 0:
  9.9 30.6 all-gather.2
  42.4 27.9 all-gather.4
where the time goes:
time: 348 us; the launch traced here: 347 us
  waiting for transfers between devices  90.3 us (26%)
  blocking collectives  75.2 us (22%)
  local copies, waits for them, and re-layouts  63.7 us (18%)
  matrix products  63.4 us (18%)
  other arithmetic  34.5 us (10%)
  between operations  14.4 us (4%)
  starting transfers between devices  5.23 us (2%)
    all_to_all x1, blocking collectives, local(): lax.all_to_all(outgoing, 'req', split_axis=0, concat_axis=0, tiled=True)  75.2 us
    all_to_all x1, waiting for transfers between devices, local(): lax.all_to_all(produced, 'req', split_axis=0, concat_axis=0, tiled=True)  70.2 us
    dot_general x4, matrix products, local(): jnp.dot(product, w_down[expert_local], preferred_element_type=jnp.float32)  21.7 us
    all_gather x1, waiting for transfers between devices, local(): value_piece = lax.all_gather(prefix_values, 'req', axis=1, tiled=True)  18.2 us
    gather x1, local copies, waits for them, and re-layouts, local(): returned[slot_index].astype(jnp.float32)  14.7 us
    scatter x1, local copies, waits for them, and re-layouts, local(): jnp.zeros((EXPERTS * CAP, model_width), jnp.bfloat16).at[slot_index]  13.5 us
    dot_general x5, matrix products, absorb(): jnp.einsum('kgts,skd->kgtd', weights.astype(jnp.bfloat16), value_rows, pr...  12.5 us
    dot_general x4, matrix products, local(): jnp.dot(expert_rows, w_gate[expert_local], preferred_element_type=jnp.flo...  11.5 us
  transfers between devices with their start and end apart: 3, of which 3 were waited for; matrix products, arithmetic and copies ran while one was open for 13% of the time, Pallas kernels for 0%

commit v1 on v0

--- a/solution.py
+++ b/solution.py
@@ -1,8 +1,12 @@
+import functools
 import math
 
 import jax
 import jax.numpy as jnp
+import numpy as np
 from jax import lax
+from jax.experimental import pallas as pl
+from jax.experimental.pallas import tpu as pltpu
 from jax.sharding import PartitionSpec as P
 
 H = 16
@@ -81,7 +85,7 @@
     return (chosen, ranked)
 
 
-def local(
+def local_general(
     tokens,
     attn_gain,
     w_query,
@@ -175,6 +179,403 @@
     return (context[None], hidden[None], expert_mix[None])
 
 
+F32 = jnp.float32
+BF16 = jnp.bfloat16
+MIB = 1 << 20
+LANES = 128
+
+
+def dot(lhs, rhs):
+    return jnp.dot(lhs, rhs, preferred_element_type=F32)
+
+
+def dot_nt(lhs, rhs):
+    return lax.dot_general(lhs, rhs, (((1,), (1,)), ((), ())), preferred_element_type=F32)
+
+
+def dot_tn(lhs, rhs):
+    return lax.dot_general(lhs, rhs, (((0,), (0,)), ((), ())), preferred_element_type=F32)
+
+
+def lane_index(shape):
+    return lax.broadcasted_iota(jnp.int32, shape, len(shape) - 1)
+
+
+def rope_tables(prefix_len, tok_count):
+    frequency = ROPE_BASE ** (-(np.arange(HD // 2, dtype=np.float64) * 2.0 / HD))
+    angles = (prefix_len + np.arange(tok_count, dtype=np.float64))[:, None] * frequency[None, :]
+    cosine, sine = np.cos(angles), np.sin(angles)
+    cosine = np.concatenate([cosine, cosine, cosine, cosine], axis=1)
+    sine = np.concatenate([-sine, sine, -sine, sine], axis=1)
+    return jnp.asarray(cosine, F32), jnp.asarray(sine, F32)
+
+
+def rotate_tile(tile, cosine, sine):
+    first = lane_index(tile.shape) % HD < HD // 2
+    other = jnp.where(
+        first, pltpu.roll(tile, LANES - HD // 2, 1), pltpu.roll(tile, HD // 2, 1)
+    )
+    return tile * cosine + other * sine
+
+
+def project_kernel(tok_ref, gain_ref, wq_ref, wk_ref, wv_ref, cos_ref, sin_ref, q_ref, k_ref, v_ref, normed_ref):
+    @pl.when(pl.program_id(0) == 0)
+    def _():
+        rows = tok_ref[...].astype(F32)
+        mean_square = jnp.mean(rows * rows, axis=-1, keepdims=True)
+        normed_ref[...] = (rows * lax.rsqrt(mean_square + NORM_EPS) * gain_ref[...]).astype(BF16)
+
+    normed = normed_ref[...]
+    tok_count = normed.shape[0]
+    cosine, sine = cos_ref[...], sin_ref[...]
+    queries = dot(normed, wq_ref[...])
+    low = lane_index((tok_count, LANES)) < HD
+    for half in range(2):
+        tile = rotate_tile(queries[:, half * LANES : (half + 1) * LANES], cosine, sine) * ATTN_SCALE
+        turned = pltpu.roll(tile, HD, 1)
+        if half == 0:
+            first, second = jnp.where(low, tile, 0.0), jnp.where(low, turned, 0.0)
+        else:
+            first, second = jnp.where(low, 0.0, turned), jnp.where(low, 0.0, tile)
+        q_ref[half, :tok_count, :] = first.astype(BF16)
+        q_ref[half, tok_count:, :] = second.astype(BF16)
+    k_ref[...] = rotate_tile(dot(normed, wk_ref[...]), cosine, sine).astype(BF16)
+    v_ref[...] = dot(normed, wv_ref[...]).astype(BF16)
+
+
+def project(own_rows, attn_gain, w_query, w_key, w_value, prefix_len):
+    tok_count, width = own_rows.shape
+    cosine, sine = rope_tables(prefix_len, tok_count)
+    steps = KV // 2
+    whole = lambda i: (0, 0)
+    column = lambda i: (0, i)
+    return pl.pallas_call(
+        project_kernel,
+        grid=(steps,),
+        in_specs=[
+            pl.BlockSpec((tok_count, width), whole),
+            pl.BlockSpec((1, width), whole),
+            pl.BlockSpec((width, 2 * LANES), column),
+            pl.BlockSpec((width, LANES), column),
+            pl.BlockSpec((width, LANES), column),
+            pl.BlockSpec((tok_count, LANES), whole),
+            pl.BlockSpec((tok_count, LANES), whole),
+        ],
+        out_specs=[
+            pl.BlockSpec((2, 2 * tok_count, LANES), lambda i: (i, 0, 0)),
+            pl.BlockSpec((tok_count, LANES), column),
+            pl.BlockSpec((tok_count, LANES), column),
+        ],
+        out_shape=[
+            jax.ShapeDtypeStruct((KV, 2 * tok_count, LANES), BF16),
+            jax.ShapeDtypeStruct((tok_count, KV * HD), BF16),
+            jax.ShapeDtypeStruct((tok_count, KV * HD), BF16),
+        ],
+        scratch_shapes=[pltpu.VMEM((tok_count, width), BF16)],
+        compiler_params=pltpu.CompilerParams(vmem_limit_bytes=32 * MIB),
+        cost_estimate=pl.CostEstimate(flops=2 * tok_count * width * 2048, bytes_accessed=6 * MIB, transcendentals=0),
+        name="project",
+    )(own_rows, attn_gain.reshape(1, width), w_query, w_key, w_value, cosine, sine)
+
+
+def attend_head(half, queries, key_tiles, value_tiles, suffix_mask, state):
+    scores = [dot_nt(queries, tile) for tile in key_tiles]
+    if suffix_mask is not None:
+        scores[0] = jnp.where(suffix_mask, scores[0], -1e30)
+    top = functools.reduce(jnp.maximum, scores)
+    new_max = jnp.max(top, axis=1, keepdims=True)
+    if state is not None:
+        new_max = jnp.maximum(new_max, state[0])
+    total = None
+    for score, tile in zip(scores, value_tiles):
+        weights = jnp.exp(score - new_max).astype(BF16)
+        low = lane_index(tile.shape) < HD
+        one = jnp.ones_like(tile)
+        values = jnp.where(low, tile, one) if half == 0 else jnp.where(low, one, tile)
+        part = dot(weights, values)
+        total = part if total is None else total + part
+    if state is not None:
+        total = total + state[1] * jnp.exp(state[0] - new_max)
+    return new_max, total
+
+
+def attend_kernel(blocks, first, last, *refs):
+    refs = list(refs)
+    take = lambda n: [refs.pop(0) for _ in range(n)]
+    (q_ref,) = take(1)
+    key_refs, value_refs = take(blocks), take(blocks)
+    if first:
+        (len_ref,) = take(1)
+    else:
+        max_in, acc_in = take(2)
+    if last:
+        tok_ref, w_out_ref, gain_ref = take(3)
+        ctx_ref, hidden_ref, moe_ref, projected_ref = take(4)
+    else:
+        max_out, acc_out = take(2)
+    step = pl.program_id(0)
+    tok_count = q_ref.shape[1] // 2
+    suffix_mask = None
+    if first:
+        shape = (2 * tok_count, tok_count)
+        slot = lane_index(shape)
+        row = lax.broadcasted_iota(jnp.int32, shape, 0) % tok_count
+        suffix_mask = (slot <= row) & (slot < len_ref[0])
+    key_tiles = [ref[...] for ref in key_refs]
+    value_tiles = [ref[...] for ref in value_refs]
+    outs = []
+    for half in range(2):
+        state = None if first else (max_in[half], acc_in[half])
+        new_max, total = attend_head(half, q_ref[half], key_tiles, value_tiles, suffix_mask, state)
+        if not last:
+            max_out[half] = new_max
+            acc_out[half] = total
+            continue
+        mixed = total / pltpu.roll(total, HD, 1)
+        low = lane_index((tok_count, LANES)) < HD
+        one, two = mixed[:tok_count], mixed[tok_count:]
+        if half == 0:
+            outs.append(jnp.where(low, one, pltpu.roll(two, HD, 1)))
+        else:
+            outs.append(jnp.where(low, pltpu.roll(one, HD, 1), two))
+    if last:
+        context = jnp.concatenate(outs, axis=1).astype(BF16)
+        ctx_ref[...] = context
+        part = dot(context, w_out_ref[...])
+
+        @pl.when(step == 0)
+        def _():
+            projected_ref[...] = part
+
+        @pl.when(step > 0)
+        def _():
+            projected_ref[...] += part
+
+        @pl.when(step == pl.num_programs(0) - 1)
+        def _():
+            hidden = (tok_ref[...].astype(F32) + RESIDUAL_SCALE * projected_ref[...]).astype(BF16)
+            hidden_ref[...] = hidden
+            wide = hidden.astype(F32)
+            mean_square = jnp.mean(wide * wide, axis=-1, keepdims=True)
+            moe_ref[...] = (wide * lax.rsqrt(mean_square + NORM_EPS) * gain_ref[...]).astype(BF16)
+
+
+def attend(queries, keys, values, suffix_len=None, state=None, final=None):
+    first, last = state is None, final is not None
+    blocks = len(keys)
+    rows = queries.shape[1]
+    tok_count = rows // 2
+    tile = pl.BlockSpec((keys[0].shape[0], LANES), lambda i: (0, i))
+    pair = lambda lanes: pl.BlockSpec((2, rows, lanes), lambda i: (i, 0, 0))
+    args, in_specs = [queries, *keys, *values], [pair(LANES)] + [tile] * (2 * blocks)
+    if first:
+        args.append(suffix_len)
+        in_specs.append(pl.BlockSpec(memory_space=pltpu.SMEM))
+    else:
+        args.extend(state)
+        in_specs.extend([pair(1), pair(LANES)])
+    scratch = []
+    if last:
+        own_rows, w_out, moe_gain = final
+        width = own_rows.shape[1]
+        args.extend([own_rows, w_out, moe_gain.reshape(1, width)])
+        whole = pl.BlockSpec((tok_count, width), lambda i: (0, 0))
+        in_specs.extend([whole, pl.BlockSpec((2 * LANES, width), lambda i: (i, 0)), pl.BlockSpec((1, width), lambda i: (0, 0))])
+        out_specs = [pl.BlockSpec((tok_count, 2 * LANES), lambda i: (0, i)), whole, whole]
+        out_shape = [jax.ShapeDtypeStruct((tok_count, width), BF16)] * 3
+        scratch = [pltpu.VMEM((tok_count, width), F32)]
+    else:
+        out_specs = [pair(1), pair(LANES)]
+        out_shape = [jax.ShapeDtypeStruct((KV, rows, 1), F32), jax.ShapeDtypeStruct((KV, rows, LANES), F32)]
+    return pl.pallas_call(
+        functools.partial(attend_kernel, blocks, first, last),
+        grid=(KV // 2,),
+        in_specs=in_specs,
+        out_specs=out_specs,
+        out_shape=out_shape,
+        scratch_shapes=scratch,
+        compiler_params=pltpu.CompilerParams(vmem_limit_bytes=48 * MIB),
+        cost_estimate=pl.CostEstimate(flops=blocks * 1200 * MIB, bytes_accessed=4 * MIB, transcendentals=0),
+        name="attend",
+    )(*args)
+
+
+def experts_kernel(sources, *refs):
+    refs = list(refs)
+    take = lambda n: [refs.pop(0) for _ in range(n)]
+    row_refs, route_refs = take(sources), take(sources)
+    gate_own, gate_mate, up_own, up_mate, down_own, down_mate = take(6)
+    own_ref, *away_refs = take(sources)
+    picked_ref, made_ref, combine_ref = refs
+    step = pl.program_id(0)
+    n_experts = pl.num_programs(0)
+    chip_experts = route_refs[0].shape[0]
+    tok_count = row_refs[0].shape[0]
+    slots = chip_experts * CAP
+
+    @pl.when(step == 0)
+    def _():
+        before = lax.broadcasted_iota(jnp.int32, (tok_count, tok_count), 0)
+        after = lax.broadcasted_iota(jnp.int32, (tok_count, tok_count), 1)
+        earlier = jnp.where(before < after, 1.0, 0.0).astype(BF16)
+        slot = lax.broadcasted_iota(jnp.int32, (slots, chip_experts), 0)
+        expert = lane_index((slots, chip_experts))
+        spread = jnp.where(slot // CAP == expert, 1.0, 0.0).astype(BF16)
+        within = (lax.broadcasted_iota(jnp.int32, (slots, tok_count), 0) % CAP).astype(F32)
+        for source in range(sources):
+            route = route_refs[source][...]
+            hit = route > 0.0
+            ranked = dot(jnp.where(hit, 1.0, 0.0).astype(BF16), earlier)
+            ranked = jnp.where(hit, ranked, -1.0).astype(BF16)
+            match = dot(spread, ranked) == within
+            pick = jnp.where(match, 1.0, 0.0).astype(BF16)
+            combine_ref[source] = jnp.where(match, dot(spread, route.astype(BF16)), 0.0).astype(BF16)
+            picked = dot(pick, row_refs[source][...]).astype(BF16)
+            for e in range(chip_experts):
+                picked_ref[e, source] = picked[e * CAP : (e + 1) * CAP]
+
+    def one_expert(gate_ref, up_ref, down_ref):
+        width = picked_ref.shape[-1]
+        rows = picked_ref[step].reshape(sources * CAP, width)
+        gate = dot(rows, gate_ref[0])
+        up = dot(rows, up_ref[0])
+        act = (jax.nn.silu(gate) * up).astype(BF16)
+        made = dot(act, down_ref[0]).astype(BF16)
+        for source in range(sources):
+            made_ref[source, pl.ds(pl.multiple_of(step * CAP, CAP), CAP), :] = made[source * CAP : (source + 1) * CAP]
+
+    @pl.when(step < n_experts // 2)
+    def _():
+        one_expert(gate_own, up_own, down_own)
+
+    @pl.when(step >= n_experts // 2)
+    def _():
+        one_expert(gate_mate, up_mate, down_mate)
+
+    @pl.when(step == n_experts - 1)
+    def _():
+        for source, ref in enumerate([own_ref, *away_refs]):
+            ref[...] = dot_tn(combine_ref[source], made_ref[source]).astype(ref.dtype)
+
+
+def run_experts(rows, routes, gate, up, down):
+    sources = len(rows)
+    tok_count, width = rows[0].shape
+    local_experts, _, hidden = gate[0].shape
+    chip_experts = 2 * local_experts
+    whole = lambda shape: pl.BlockSpec(shape, lambda e: (0,) * len(shape))
+    own = lambda e: (jnp.minimum(e, local_experts - 1), 0, 0)
+    mate = lambda e: (jnp.maximum(e - local_experts, 0), 0, 0)
+    wide = [pl.BlockSpec((1, width, hidden), own), pl.BlockSpec((1, width, hidden), mate)]
+    tall = [pl.BlockSpec((1, hidden, width), own), pl.BlockSpec((1, hidden, width), mate)]
+    return pl.pallas_call(
+        functools.partial(experts_kernel, sources),
+        grid=(chip_experts,),
+        in_specs=[whole((tok_count, width))] * sources
+        + [whole((chip_experts, tok_count))] * sources
+        + wide + wide + tall,
+        out_specs=[whole((tok_count, width))] * sources,
+        out_shape=[jax.ShapeDtypeStruct((tok_count, width), F32 if s == 0 else BF16) for s in range(sources)],
+        scratch_shapes=[
+            pltpu.VMEM((chip_experts, sources, CAP, width), BF16),
+            pltpu.VMEM((sources, chip_experts * CAP, width), BF16),
+            pltpu.VMEM((sources, chip_experts * CAP, tok_count), BF16),
+        ],
+        compiler_params=pltpu.CompilerParams(vmem_limit_bytes=56 * MIB),
+        cost_estimate=pl.CostEstimate(flops=12000 * MIB, bytes_accessed=30 * MIB, transcendentals=0),
+        name="experts",
+    )(*rows, *routes, *gate, *up, *down)
+
+
+CORE, ACROSS_X, ACROSS_Y = 1, 2, 4
+
+
+def swap(array, mask):
+    return lax.ppermute(array, "req", [(i, i ^ mask) for i in range(lax.axis_size("req"))])
+
+
+def gather_pair(one, two):
+    one_x, two_y = swap(one, ACROSS_X), swap(two, ACROSS_Y)
+    two_x, one_y = swap(two, ACROSS_X), swap(one, ACROSS_Y)
+    one_xy, two_xy = swap(one_x, ACROSS_Y), swap(two_y, ACROSS_X)
+    return (one_x, two_x), (one_y, two_y), (one_xy, two_xy)
+
+
+def routes_of(expert_ids, route_weights, peer_count):
+    ids, gains = expert_ids.T, route_weights.T
+    named = ids[None, :, :] == jnp.arange(EXPERTS, dtype=jnp.int32)[:, None, None]
+    dense = jnp.sum(jnp.where(named, gains[None], 0.0), axis=1)
+    tok_count = ids.shape[1]
+    dense = dense.reshape(peer_count // 2, 2, EXPERTS // peer_count, tok_count)
+    core = lax.axis_index("req") % 2
+    dense = jnp.where(core == 0, dense, dense[:, ::-1])
+    return dense.reshape(peer_count // 2, 2 * EXPERTS // peer_count, tok_count)
+
+
+def local_chips(
+    tokens,
+    attn_gain,
+    w_query,
+    w_key,
+    w_value,
+    w_out,
+    prefix_keys,
+    prefix_values,
+    lengths,
+    assignment,
+    moe_gain,
+    expert_ids,
+    route_weights,
+    w_gate,
+    w_up,
+    w_down,
+):
+    peer_count = lax.axis_size("req")
+    own_rows = tokens[0]
+    tok_count = own_rows.shape[0]
+    prefix_len = prefix_keys.shape[1] * peer_count
+    my_index = lax.axis_index("req")
+    request_ids = jnp.arange(lengths.shape[1], dtype=jnp.int32)
+    request = jnp.sum(jnp.where(request_ids == my_index, assignment[0], 0))
+    suffix_len = jnp.sum(jnp.where(request_ids == request, lengths[0], 0)).reshape(1)
+
+    keys, values = prefix_keys[0], prefix_values[0]
+    far = gather_pair(keys, values)
+    pairs = [(keys, values), *far]
+    mates = [(swap(k, CORE), swap(v, CORE)) for k, v in pairs]
+
+    routes = routes_of(expert_ids[0], route_weights[0], peer_count)
+    chip = my_index // 2
+    routes = [
+        routes[chip],
+        swap(routes[chip ^ 1], ACROSS_X),
+        swap(routes[chip ^ 2], ACROSS_Y),
+        swap(routes[chip ^ 3], ACROSS_X | ACROSS_Y),
+    ]
+    gate, up, down = [(w, swap(w, CORE)) for w in (w_gate, w_up, w_down)]
+
+    queries, suffix_keys, suffix_values = project(own_rows, attn_gain, w_query, w_key, w_value, prefix_len)
+    near = [(suffix_keys, suffix_values), pairs[0], mates[0]]
+    state = attend(queries, [k for k, _ in near], [v for _, v in near], suffix_len=suffix_len)
+    rest = pairs[1:] + mates[1:]
+    context, hidden, moe_in = attend(
+        queries, [k for k, _ in rest], [v for _, v in rest], state=state, final=(own_rows, w_out, moe_gain)
+    )
+
+    half = tok_count // 2
+    parts = gather_pair(moe_in[:half], moe_in[half:])
+    rows = [moe_in] + [jnp.concatenate(part, axis=0) for part in parts]
+    own, to_x, to_y, to_xy = run_experts(rows, routes, gate, up, down)
+
+    via_x, via_y = swap(to_xy[:half], ACROSS_X), swap(to_xy[half:], ACROSS_Y)
+    low_y = (to_y[:half].astype(F32) + via_x.astype(F32)).astype(BF16)
+    high_x = (to_x[half:].astype(F32) + via_y.astype(F32)).astype(BF16)
+    low = own[:half] + swap(to_x[:half], ACROSS_X).astype(F32) + swap(low_y, ACROSS_Y).astype(F32)
+    high = own[half:] + swap(to_y[half:], ACROSS_Y).astype(F32) + swap(high_x, ACROSS_X).astype(F32)
+    expert_mix = jnp.concatenate([low, high], axis=0).astype(BF16)
+    return (context[None], hidden[None], expert_mix[None])
+
+
 def solution(mesh):
     placed = (
         P("grp", "req", None),
@@ -195,7 +596,7 @@
         P("req", None, None),
     )
     return jax.shard_map(
-        local,
+        local_chips if mesh.shape["req"] == 8 else local_general,
         mesh=mesh,
         in_specs=placed,
         out_specs=(P("grp", "req", None), P("grp", "req", None), P("grp", "req", None)),

time: 348 us -> 156 us (0.45)
  blocking collectives: 75.2 us -> 0 us
  matrix products: 63.4 us -> 0 us
  Pallas kernels: 0 us -> 51.3 us
  waiting for transfers between devices: 90.3 us -> 44.3 us
  local copies, waits for them, and re-layouts: 63.7 us -> 17.9 us
  starting transfers between devices: 5.23 us -> 31.7 us
  other arithmetic: 34.5 us -> 9.01 us
  between operations: 14.4 us -> 0.88 us
    all_to_all x1 -> x0, blocking collectives: 75.2 us -> none  [local(): lax.all_to_all(outgoing, 'req', split_axis=0, concat_axis=0, tiled=True)]
    all_to_all x1 -> x0, waiting for transfers between devices: 70.2 us -> none  [local(): lax.all_to_all(produced, 'req', split_axis=0, concat_axis=0, tiled=True)]
    dot_general x22 -> x0, matrix products: 63.4 us -> none  [the longest x4 21.7 us: local(): jnp.dot(product, w_down[expert_local], preferred_element_type=jnp.float32)]
    pallas_call x0 -> x4, Pallas kernels: none -> 51.3 us  [the longest x2 24.4 us: attend(): pl.pallas_call(functools.partial(attend_kernel, blocks, first, last), gri...]
    ppermute x0 -> x32, waiting for transfers between devices: none -> 44.3 us  [swap(): lax.ppermute(array, 'req', [(i, i ^ mask) for i in range(lax.axis_size('r...]
    ppermute x0 -> x32, starting transfers between devices: none -> 31.7 us  [swap(): lax.ppermute(array, 'req', [(i, i ^ mask) for i in range(lax.axis_size('r...]
    all_gather x2 -> x0, waiting for transfers between devices: 18.8 us -> none  [the longest x1 18.2 us: local(): value_piece = lax.all_gather(prefix_values, 'req', axis=1, tiled=True)]
    another operation x7 -> x0, other arithmetic: 16.1 us -> none
  transfers between devices with their start and end apart: 3 -> 32, of which waited for: 3 -> 14; matrix products, arithmetic and copies ran while one was open for 13% -> 7% of each run, Pallas kernels for 0% -> 18%
where the time goes in v1:
time: 156 us; the launch traced here: 155 us
  Pallas kernels  51.3 us (33%)
  waiting for transfers between devices  44.3 us (28%)
  starting transfers between devices  31.7 us (20%)
  local copies, waits for them, and re-layouts  17.9 us (11%)
  other arithmetic  9.01 us (6%)
    ppermute x32, waiting for transfers between devices, swap(): lax.ppermute(array, 'req', [(i, i ^ mask) for i in range(lax.axis_size('r...  44.3 us
    ppermute x32, starting transfers between devices, swap(): lax.ppermute(array, 'req', [(i, i ^ mask) for i in range(lax.axis_size('r...  31.7 us
    pallas_call x2, Pallas kernels, attend(): pl.pallas_call(functools.partial(attend_kernel, blocks, first, last), gri...  24.4 us
    pallas_call x1, Pallas kernels, run_experts(): pl.pallas_call(functools.partial(experts_kernel, sources), grid=(chip_exp...  23.1 us
    unnamed x56, local copies, waits for them, and re-layouts  14.1 us
    pallas_call x1, Pallas kernels, project(): pl.pallas_call(project_kernel, grid=(steps,), in_specs=[pl.BlockSpec((tok...  3.84 us
  transfers between devices with their start and end apart: 32, of which 14 were waited for; matrix products, arithmetic and copies ran while one was open for 7% of the time, Pallas kernels for 18%

profile of v1, /device:TPU:0, one launch (start us, length us, event | category | flops | bytes accessed | tf_op | source)
XLA Modules:
  0.0 155.0 jit_solution(13711637393607305010)
XLA Ops:
  1.8 2.9 %collective-permute-start.1 = (bf16[256,512]{1,0:T(8,128)(2,1)}, bf16[256,512]{1,0:T(8,128)(2,1)S(1)}, u32[]{:S(2)}, u32[]{:S(2)}) collective-permute-start(bf16[256,512]{1,0:T(8,128)(2,1)} %bitcast.34), channel_id=1, source_target_pairs={{0,4},{1,5},{2,6},{3,7},{4,0},{5,1},{6,2},{7,3},{8,12},{9,13},{10,... | collective-permute-start | bytes 786440 | tf_op jit(solution)/shard_map/ppermute | solution.py:494
  4.7 4.1 %collective-permute-done.12.refs_3_ = bf16[256,512]{1,0:T(8,128)(2,1)S(1)} collective-permute-done((bf16[256,512]{1,0:T(8,128)(2,1)}, bf16[256,512]{1,0:T(8,128)(2,1)S(1)}, u32[]{:S(2)}, u32[]{:S(2)}) %collective-permute-start.12) | collective-permute-done | bytes 262176 | tf_op jit(solution)/shard_map/ppermute | solution.py:494
  8.8 2.9 %collective-permute-start = (bf16[256,512]{1,0:T(8,128)(2,1)}, bf16[256,512]{1,0:T(8,128)(2,1)S(1)}, u32[]{:S(2)}, u32[]{:S(2)}) collective-permute-start(bf16[256,512]{1,0:T(8,128)(2,1)} %bitcast.35), channel_id=1, source_target_pairs={{0,2},{1,3},{2,0},{3,1},{4,6},{5,7},{6,4},{7,5},{8,10},{9,11},{10,... | collective-permute-start | bytes 786440 | tf_op jit(solution)/shard_map/ppermute | solution.py:494
  11.7 6.8 %collective-permute-done.refs_1_ = bf16[256,512]{1,0:T(8,128)(2,1)S(1)} collective-permute-done((bf16[256,512]{1,0:T(8,128)(2,1)}, bf16[256,512]{1,0:T(8,128)(2,1)S(1)}, u32[]{:S(2)}, u32[]{:S(2)}) %collective-permute-start) | collective-permute-done | bytes 262176 | tf_op jit(solution)/shard_map/ppermute | solution.py:494
  18.5 1.8 %collective-permute-start.7 = (bf16[256,512]{1,0:T(8,128)(2,1)}, bf16[256,512]{1,0:T(8,128)(2,1)S(1)}, u32[]{:S(2)}, u32[]{:S(2)}) collective-permute-start(bf16[256,512]{1,0:T(8,128)(2,1)} %bitcast.38), channel_id=1, source_target_pairs={{0,4},{1,5},{2,6},{3,7},{4,0},{5,1},{6,2},{7,3},{8,12},{9,13},{10,... | collective-permute-start | bytes 786440 | tf_op jit(solution)/shard_map/ppermute | solution.py:494
  20.3 1.5 collective-permute-start.6
  21.8 4.8 %collective-permute-done.7.refs_8_ = bf16[256,512]{1,0:T(8,128)(2,1)S(1)} collective-permute-done((bf16[256,512]{1,0:T(8,128)(2,1)}, bf16[256,512]{1,0:T(8,128)(2,1)S(1)}, u32[]{:S(2)}, u32[]{:S(2)}) %collective-permute-start.7) | collective-permute-done | bytes 262176 | tf_op jit(solution)/shard_map/ppermute | solution.py:494
  30.3 1.3 fusion.2
  31.6 5.7 %collective-permute-done.2.refs_3_ = bf16[256,512]{1,0:T(8,128)(2,1)S(1)} collective-permute-done((bf16[256,512]{1,0:T(8,128)(2,1)S(1)}, bf16[256,512]{1,0:T(8,128)(2,1)S(1)}, u32[]{:S(2)}, u32[]{:S(2)}) %collective-permute-start.2) | collective-permute-done | bytes 262176 | tf_op jit(solution)/shard_map/ppermute | solution.py:494
  37.3 1.5 collective-permute-start.8
  39.5 1.6 %copy-done = bf16[1024,1024]{1,0:T(8,128)(2,1)S(1)} copy-done((bf16[1024,1024]{1,0:T(8,128)(2,1)S(1)}, bf16[1024,1024]{1,0:T(8,128)(2,1)}, u32[]{:S(2)}) %copy-start) | copy-done | bytes 2097176
  47.1 3.8 %project.1 = (bf16[8,512,128]{2,1,0:T(8,128)(2,1)S(1)}, bf16[256,512]{1,0:T(8,128)(2,1)S(1)}, bf16[256,512]{1,0:T(8,128)(2,1)S(1)}) custom-call(bf16[256,1024]{1,0:T(8,128)(2,1)S(1)} %bitcast.30, f32[1,1024]{1,0:T(1,128)S(1)} %bitcast.32, bf16[1024,1024]{1,0:T(8,128)(2,1)S(1)} %copy-done, bf16[1024,512]{1,0:T(8,128)(2,1)S(1)} %copy-done.1, ...), custom_call_target="tpu_custom_call" | custom-call | flops 1073741824 | bytes 6291456 | tf_op jit(solution)/shard_map/project/pallas_call | solution.py:252
  56.8 7.7 %attend.2 = (f32[8,512,1]{2,1,0:T(8,128)S(1)}, f32[8,512,128]{2,1,0:T(8,128)}) custom-call(bf16[8,512,128]{2,1,0:T(8,128)(2,1)S(1)} %get-tuple-element.15.refs_0_, bf16[256,512]{1,0:T(8,128)(2,1)S(1)} %copy-done.18, bf16[256,512]{1,0:T(8,128)(2,1)S(1)} %bitcast.36, bf16[256,512]{1,0:T(8,128)(2,1)S(1)} %collective-permute-done.12.refs_3_, ...), custom_call_target="tpu_custom_call" | custom-call | flops 3774873600 | bytes 4194304 | tf_op jit(solution)/shard_map/attend/pallas_call | solution.py:390
  66.4 16.7 %attend.3 = (bf16[256,1024]{1,0:T(8,128)(2,1)}, bf16[256,1024]{1,0:T(8,128)(2,1)}, bf16[256,1024]{1,0:T(8,128)(2,1)S(1)}) custom-call(bf16[8,512,128]{2,1,0:T(8,128)(2,1)S(1)} %get-tuple-element.15.refs_0_, bf16[256,512]{1,0:T(8,128)(2,1)S(1)} %collective-permute-done.refs_1_, bf16[256,512]{1,0:T(8,128)(2,1)S(1)} %collective-permute-done.1.refs_2_, ...), custom_call_target="tpu_custom_call" | custom-call | flops 7549747200 | bytes 4194304 | tf_op jit(solution)/shard_map/attend/pallas_call | solution.py:390
  83.1 1.5 collective-permute-start.16
  84.6 1.5 collective-permute-start.14
  86.1 5.4 %collective-permute-done.16 = bf16[128,1024]{1,0:T(8,128)(2,1)S(1)} collective-permute-done((bf16[128,1024]{1,0:T(8,128)(2,1)S(1)}, bf16[128,1024]{1,0:T(8,128)(2,1)S(1)}, u32[]{:S(2)}, u32[]{:S(2)}) %collective-permute-start.16) | collective-permute-done | bytes 262176 | tf_op jit(solution)/shard_map/ppermute | solution.py:494
  91.5 1.5 collective-permute-start.17
  93.0 1.5 collective-permute-start.15
  94.5 4.6 %collective-permute-done.17 = bf16[128,1024]{1,0:T(8,128)(2,1)S(1)} collective-permute-done((bf16[128,1024]{1,0:T(8,128)(2,1)S(1)}, bf16[128,1024]{1,0:T(8,128)(2,1)S(1)}, u32[]{:S(2)}, u32[]{:S(2)}) %collective-permute-start.17) | collective-permute-done | bytes 262176 | tf_op jit(solution)/shard_map/ppermute | solution.py:494
  99.0 1.5 collective-permute-start.18
  100.5 1.5 collective-permute-start.19
  103.7 2.0 %collective-permute-done.18 = bf16[128,1024]{1,0:T(8,128)(2,1)S(1)} collective-permute-done((bf16[128,1024]{1,0:T(8,128)(2,1)S(1)}, bf16[128,1024]{1,0:T(8,128)(2,1)S(1)}, u32[]{:S(2)}, u32[]{:S(2)}) %collective-permute-start.18) | collective-permute-done | bytes 262176 | tf_op jit(solution)/shard_map/ppermute | solution.py:494
  105.7 1.5 collective-permute-start.21
  107.1 1.5 collective-permute-start.20
  109.5 1.3 collective-permute-done.20.refs_5_
  111.4 23.1 %experts.1 = (f32[256,1024]{1,0:T(8,128)}, bf16[256,1024]{1,0:T(8,128)(2,1)}, bf16[256,1024]{1,0:T(8,128)(2,1)}, bf16[256,1024]{1,0:T(8,128)(2,1)}) custom-call(bf16[256,1024]{1,0:T(8,128)(2,1)} %copy-done.3, bf16[256,1024]{1,0:T(8,128)(2,1)} %pad_maximum_fusion.refs_1_, bf16[256,1024]{1,0:T(8,128)(2,1)} %pad_maximum_fusion.1.refs_2_, ...), custom_call_target="tpu_custom_call" | custom-call | flops 12582912000 | bytes 31457280 | tf_op jit(solution)/shard_map/experts/pallas_call | solution.py:471
  135.6 1.6 %collective-permute-start.27 = (bf16[128,1024]{1,0:T(8,128)(2,1)S(1)}, bf16[128,1024]{1,0:T(8,128)(2,1)S(1)}, u32[]{:S(2)}, u32[]{:S(2)}) collective-permute-start(bf16[128,1024]{1,0:T(8,128)(2,1)S(1)} %get-tuple-element.29), channel_id=1, source_target_pairs={{0,2},{1,3},{2,0},{3,1},{4,6},{5,7},{6,4},{7,5},{8,10},{9,11},{10,... | collective-permute-start | bytes 786440 | tf_op jit(solution)/shard_map/ppermute | solution.py:494
  139.7 1.5 collective-permute-start.29
  141.7 3.1 %collective-permute-done.27 = bf16[128,1024]{1,0:T(8,128)(2,1)S(1)} collective-permute-done((bf16[128,1024]{1,0:T(8,128)(2,1)S(1)}, bf16[128,1024]{1,0:T(8,128)(2,1)S(1)}, u32[]{:S(2)}, u32[]{:S(2)}) %collective-permute-start.27) | collective-permute-done | bytes 262176 | tf_op jit(solution)/shard_map/ppermute | solution.py:494
  150.4 2.1 %collective-permute-done.28 = bf16[128,1024]{1,0:T(8,128)(2,1)S(1)} collective-permute-done((bf16[128,1024]{1,0:T(8,128)(2,1)S(1)}, bf16[128,1024]{1,0:T(8,128)(2,1)S(1)}, u32[]{:S(2)}, u32[]{:S(2)}) %collective-permute-start.28) | collective-permute-done | bytes 262176 | tf_op jit(solution)/shard_map/ppermute | solution.py:494
  152.6 1.4 collective-permute-done.31
  (110 shorter events, 33.0 us)
Async XLA Ops:
  0.6 110.2 %collective-permute-start.23 = (bf16[4,1024,512]{2,1,0:T(8,128)(2,1)}, bf16[4,1024,512]{2,1,0:T(8,128)(2,1)}, u32[]{:S(2)}, u32[]{:S(2)}) collective-permute-start(bf16[4,1024,512]{2,1,0:T(8,128)(2,1)} %refs_8_.1), channel_id=1, source_target_pairs={{0,1},{1,0},{2,3},{3,2},{4,5},{5,4},{6,7},{7,6},{8,9},{9,8},{10,11... | collective-permute-start | bytes 12582920 | tf_op jit(solution)/shard_map/ppermute | solution.py:494
  1.2 109.6 %collective-permute-start.24 = (bf16[4,1024,512]{2,1,0:T(8,128)(2,1)}, bf16[4,1024,512]{2,1,0:T(8,128)(2,1)}, u32[]{:S(2)}, u32[]{:S(2)}) collective-permute-start(bf16[4,1024,512]{2,1,0:T(8,128)(2,1)} %refs_10_.1), channel_id=1, source_target_pairs={{0,1},{1,0},{2,3},{3,2},{4,5},{5,4},{6,7},{7,6},{8,9},{9,8},{10,11... | collective-permute-start | bytes 12582920 | tf_op jit(solution)/shard_map/ppermute | solution.py:494
  1.2 109.6 %collective-permute-start.25 = (bf16[4,512,1024]{2,1,0:T(8,128)(2,1)}, bf16[4,512,1024]{2,1,0:T(8,128)(2,1)}, u32[]{:S(2)}, u32[]{:S(2)}) collective-permute-start(bf16[4,512,1024]{2,1,0:T(8,128)(2,1)} %refs_12_.1), channel_id=1, source_target_pairs={{0,1},{1,0},{2,3},{3,2},{4,5},{5,4},{6,7},{7,6},{8,9},{9,8},{10,11... | collective-permute-start | bytes 12582920 | tf_op jit(solution)/shard_map/ppermute | solution.py:494
  1.7 7.2 %collective-permute-start.12 = (bf16[256,512]{1,0:T(8,128)(2,1)}, bf16[256,512]{1,0:T(8,128)(2,1)S(1)}, u32[]{:S(2)}, u32[]{:S(2)}) collective-permute-start(bf16[256,512]{1,0:T(8,128)(2,1)} %bitcast.33), channel_id=1, source_target_pairs={{0,1},{1,0},{2,3},{3,2},{4,5},{5,4},{6,7},{7,6},{8,9},{9,8},{10,11... | collective-permute-start | bytes 786440 | tf_op jit(solution)/shard_map/ppermute | solution.py:494
  1.8 9.9 %collective-permute-start.1 = (bf16[256,512]{1,0:T(8,128)(2,1)}, bf16[256,512]{1,0:T(8,128)(2,1)S(1)}, u32[]{:S(2)}, u32[]{:S(2)}) collective-permute-start(bf16[256,512]{1,0:T(8,128)(2,1)} %bitcast.34), channel_id=1, source_target_pairs={{0,4},{1,5},{2,6},{3,7},{4,0},{5,1},{6,2},{7,3},{8,12},{9,13},{10,... | collective-permute-start | bytes 786440 | tf_op jit(solution)/shard_map/ppermute | solution.py:494
  8.8 9.7 %collective-permute-start = (bf16[256,512]{1,0:T(8,128)(2,1)}, bf16[256,512]{1,0:T(8,128)(2,1)S(1)}, u32[]{:S(2)}, u32[]{:S(2)}) collective-permute-start(bf16[256,512]{1,0:T(8,128)(2,1)} %bitcast.35), channel_id=1, source_target_pairs={{0,2},{1,3},{2,0},{3,1},{4,6},{5,7},{6,4},{7,5},{8,10},{9,11},{10,... | collective-permute-start | bytes 786440 | tf_op jit(solution)/shard_map/ppermute | solution.py:494
  11.7 8.6 %collective-permute-start.13 = (bf16[256,512]{1,0:T(8,128)(2,1)}, bf16[256,512]{1,0:T(8,128)(2,1)S(1)}, u32[]{:S(2)}, u32[]{:S(2)}) collective-permute-start(bf16[256,512]{1,0:T(8,128)(2,1)} %bitcast.37), channel_id=1, source_target_pairs={{0,1},{1,0},{2,3},{3,2},{4,5},{5,4},{6,7},{7,6},{8,9},{9,8},{10,11... | collective-permute-start | bytes 786440 | tf_op jit(solution)/shard_map/ppermute | solution.py:494
  18.5 8.0 %collective-permute-start.7 = (bf16[256,512]{1,0:T(8,128)(2,1)}, bf16[256,512]{1,0:T(8,128)(2,1)S(1)}, u32[]{:S(2)}, u32[]{:S(2)}) collective-permute-start(bf16[256,512]{1,0:T(8,128)(2,1)} %bitcast.38), channel_id=1, source_target_pairs={{0,4},{1,5},{2,6},{3,7},{4,0},{5,1},{6,2},{7,3},{8,12},{9,13},{10,... | collective-permute-start | bytes 786440 | tf_op jit(solution)/shard_map/ppermute | solution.py:494
  20.3 7.5 %collective-permute-start.6 = (bf16[256,512]{1,0:T(8,128)(2,1)}, bf16[256,512]{1,0:T(8,128)(2,1)S(1)}, u32[]{:S(2)}, u32[]{:S(2)}) collective-permute-start(bf16[256,512]{1,0:T(8,128)(2,1)} %bitcast.39), channel_id=1, source_target_pairs={{0,2},{1,3},{2,0},{3,1},{4,6},{5,7},{6,4},{7,5},{8,10},{9,11},{10,... | collective-permute-start | bytes 786440 | tf_op jit(solution)/shard_map/ppermute | solution.py:494
  26.6 2.0 %collective-permute-start.4 = (bf16[256,512]{1,0:T(8,128)(2,1)S(1)}, bf16[256,512]{1,0:T(8,128)(2,1)S(1)}, u32[]{:S(2)}, u32[]{:S(2)}) collective-permute-start(bf16[256,512]{1,0:T(8,128)(2,1)S(1)} %collective-permute-done.1.refs_2_), channel_id=1, source_target_pairs={{0,1},{1,0},{2,3},{3,2},{4,5},{5,4},{6,7},{7,6},{8,9},{9,8},{10,11... | collective-permute-start | bytes 786440 | tf_op jit(solution)/shard_map/ppermute | solution.py:494
  27.7 1.8 %collective-permute-start.3 = (bf16[256,512]{1,0:T(8,128)(2,1)S(1)}, bf16[256,512]{1,0:T(8,128)(2,1)S(1)}, u32[]{:S(2)}, u32[]{:S(2)}) collective-permute-start(bf16[256,512]{1,0:T(8,128)(2,1)S(1)} %collective-permute-done.refs_1_), channel_id=1, source_target_pairs={{0,1},{1,0},{2,3},{3,2},{4,5},{5,4},{6,7},{7,6},{8,9},{9,8},{10,11... | collective-permute-start | bytes 786440 | tf_op jit(solution)/shard_map/ppermute | solution.py:494
  28.6 8.8 %collective-permute-start.2 = (bf16[256,512]{1,0:T(8,128)(2,1)S(1)}, bf16[256,512]{1,0:T(8,128)(2,1)S(1)}, u32[]{:S(2)}, u32[]{:S(2)}) collective-permute-start(bf16[256,512]{1,0:T(8,128)(2,1)S(1)} %collective-permute-done.refs_1_), channel_id=1, source_target_pairs={{0,4},{1,5},{2,6},{3,7},{4,0},{5,1},{6,2},{7,3},{8,12},{9,13},{10,... | collective-permute-start | bytes 786440 | tf_op jit(solution)/shard_map/ppermute | solution.py:494
  30.3 8.6 %collective-permute-start.10 = (bf16[256,512]{1,0:T(8,128)(2,1)S(1)}, bf16[256,512]{1,0:T(8,128)(2,1)S(1)}, u32[]{:S(2)}, u32[]{:S(2)}) collective-permute-start(bf16[256,512]{1,0:T(8,128)(2,1)S(1)} %collective-permute-done.7.refs_8_), channel_id=1, source_target_pairs={{0,1},{1,0},{2,3},{3,2},{4,5},{5,4},{6,7},{7,6},{8,9},{9,8},{10,11... | collective-permute-start | bytes 786440 | tf_op jit(solution)/shard_map/ppermute | solution.py:494
  37.3 16.9 %collective-permute-start.8 = (bf16[256,512]{1,0:T(8,128)(2,1)S(1)}, bf16[256,512]{1,0:T(8,128)(2,1)}, u32[]{:S(2)}, u32[]{:S(2)}) collective-permute-start(bf16[256,512]{1,0:T(8,128)(2,1)S(1)} %collective-permute-done.7.refs_8_), channel_id=1, source_target_pairs={{0,2},{1,3},{2,0},{3,1},{4,6},{5,7},{6,4},{7,5},{8,10},{9,11},{10,... | collective-permute-start | bytes 786440 | tf_op jit(solution)/shard_map/ppermute | solution.py:494
  39.5 15.2 %collective-permute-start.9 = (bf16[256,512]{1,0:T(8,128)(2,1)S(1)}, bf16[256,512]{1,0:T(8,128)(2,1)}, u32[]{:S(2)}, u32[]{:S(2)}) collective-permute-start(bf16[256,512]{1,0:T(8,128)(2,1)S(1)} %collective-permute-done.6.refs_7_), channel_id=1, source_target_pairs={{0,1},{1,0},{2,3},{3,2},{4,5},{5,4},{6,7},{7,6},{8,9},{9,8},{10,11... | collective-permute-start | bytes 786440 | tf_op jit(solution)/shard_map/ppermute | solution.py:494
  54.3 11.5 %collective-permute-start.5 = (bf16[256,512]{1,0:T(8,128)(2,1)}, bf16[256,512]{1,0:T(8,128)(2,1)S(1)}, u32[]{:S(2)}, u32[]{:S(2)}) collective-permute-start(bf16[256,512]{1,0:T(8,128)(2,1)} %copy-done.13), channel_id=1, source_target_pairs={{0,1},{1,0},{2,3},{3,2},{4,5},{5,4},{6,7},{7,6},{8,9},{9,8},{10,11... | collective-permute-start | bytes 786440 | tf_op jit(solution)/shard_map/ppermute | solution.py:494
  54.8 11.6 %collective-permute-start.11 = (bf16[256,512]{1,0:T(8,128)(2,1)}, bf16[256,512]{1,0:T(8,128)(2,1)S(1)}, u32[]{:S(2)}, u32[]{:S(2)}) collective-permute-start(bf16[256,512]{1,0:T(8,128)(2,1)} %collective-permute-done.8.refs_9_), channel_id=1, source_target_pairs={{0,1},{1,0},{2,3},{3,2},{4,5},{5,4},{6,7},{7,6},{8,9},{9,8},{10,11... | collective-permute-start | bytes 786440 | tf_op jit(solution)/shard_map/ppermute | solution.py:494
  65.8 18.8 %collective-permute-start.22 = (f32[8,256]{1,0:T(8,128)S(1)}, f32[8,256]{1,0:T(8,128)S(1)}, u32[]{:S(2)}, u32[]{:S(2)}) collective-permute-start(f32[8,256]{1,0:T(8,128)S(1)} %get-tuple-element.33), channel_id=1, source_target_pairs={{0,6},{1,7},{2,4},{3,5},{4,2},{5,3},{6,0},{7,1},{8,14},{9,15},{10,... | collective-permute-start | bytes 24584 | tf_op jit(solution)/shard_map/ppermute | solution.py:494
  83.1 8.4 %collective-permute-start.16 = (bf16[128,1024]{1,0:T(8,128)(2,1)S(1)}, bf16[128,1024]{1,0:T(8,128)(2,1)S(1)}, u32[]{:S(2)}, u32[]{:S(2)}) collective-permute-start(bf16[128,1024]{1,0:T(8,128)(2,1)S(1)} %get-tuple-element.31), channel_id=1, source_target_pairs={{0,4},{1,5},{2,6},{3,7},{4,0},{5,1},{6,2},{7,3},{8,12},{9,13},{10,... | collective-permute-start | bytes 786440 | tf_op jit(solution)/shard_map/ppermute | solution.py:494
  84.6 8.4 %collective-permute-start.14 = (bf16[128,1024]{1,0:T(8,128)(2,1)S(1)}, bf16[128,1024]{1,0:T(8,128)(2,1)S(1)}, u32[]{:S(2)}, u32[]{:S(2)}) collective-permute-start(bf16[128,1024]{1,0:T(8,128)(2,1)S(1)} %get-tuple-element.31), channel_id=1, source_target_pairs={{0,2},{1,3},{2,0},{3,1},{4,6},{5,7},{6,4},{7,5},{8,10},{9,11},{10,... | collective-permute-start | bytes 786440 | tf_op jit(solution)/shard_map/ppermute | solution.py:494
  91.5 7.5 %collective-permute-start.17 = (bf16[128,1024]{1,0:T(8,128)(2,1)S(1)}, bf16[128,1024]{1,0:T(8,128)(2,1)S(1)}, u32[]{:S(2)}, u32[]{:S(2)}) collective-permute-start(bf16[128,1024]{1,0:T(8,128)(2,1)S(1)} %get-tuple-element.32), channel_id=1, source_target_pairs={{0,4},{1,5},{2,6},{3,7},{4,0},{5,1},{6,2},{7,3},{8,12},{9,13},{10,... | collective-permute-start | bytes 786440 | tf_op jit(solution)/shard_map/ppermute | solution.py:494
  93.0 7.5 %collective-permute-start.15 = (bf16[128,1024]{1,0:T(8,128)(2,1)S(1)}, bf16[128,1024]{1,0:T(8,128)(2,1)S(1)}, u32[]{:S(2)}, u32[]{:S(2)}) collective-permute-start(bf16[128,1024]{1,0:T(8,128)(2,1)S(1)} %get-tuple-element.32), channel_id=1, source_target_pairs={{0,2},{1,3},{2,0},{3,1},{4,6},{5,7},{6,4},{7,5},{8,10},{9,11},{10,... | collective-permute-start | bytes 786440 | tf_op jit(solution)/shard_map/ppermute | solution.py:494
  99.0 6.6 %collective-permute-start.18 = (bf16[128,1024]{1,0:T(8,128)(2,1)S(1)}, bf16[128,1024]{1,0:T(8,128)(2,1)S(1)}, u32[]{:S(2)}, u32[]{:S(2)}) collective-permute-start(bf16[128,1024]{1,0:T(8,128)(2,1)S(1)} %collective-permute-done.14), channel_id=1, source_target_pairs={{0,4},{1,5},{2,6},{3,7},{4,0},{5,1},{6,2},{7,3},{8,12},{9,13},{10,... | collective-permute-start | bytes 786440 | tf_op jit(solution)/shard_map/ppermute | solution.py:494
  100.5 6.6 %collective-permute-start.19 = (bf16[128,1024]{1,0:T(8,128)(2,1)S(1)}, bf16[128,1024]{1,0:T(8,128)(2,1)S(1)}, u32[]{:S(2)}, u32[]{:S(2)}) collective-permute-start(bf16[128,1024]{1,0:T(8,128)(2,1)S(1)} %collective-permute-done.17), channel_id=1, source_target_pairs={{0,2},{1,3},{2,0},{3,1},{4,6},{5,7},{6,4},{7,5},{8,10},{9,11},{10,... | collective-permute-start | bytes 786440 | tf_op jit(solution)/shard_map/ppermute | solution.py:494
  105.7 3.8 %collective-permute-start.21 = (f32[8,256]{1,0:T(8,128)S(1)}, f32[8,256]{1,0:T(8,128)S(1)}, u32[]{:S(2)}, u32[]{:S(2)}) collective-permute-start(f32[8,256]{1,0:T(8,128)S(1)} %get-tuple-element.34), channel_id=1, source_target_pairs={{0,4},{1,5},{2,6},{3,7},{4,0},{5,1},{6,2},{7,3},{8,12},{9,13},{10,... | collective-permute-start | bytes 24584 | tf_op jit(solution)/shard_map/ppermute | solution.py:494
  107.1 3.7 %collective-permute-start.20 = (f32[8,256]{1,0:T(8,128)S(1)}, f32[8,256]{1,0:T(8,128)S(1)}, u32[]{:S(2)}, u32[]{:S(2)}) collective-permute-start(f32[8,256]{1,0:T(8,128)S(1)} %get-tuple-element.35), channel_id=1, source_target_pairs={{0,2},{1,3},{2,0},{3,1},{4,6},{5,7},{6,4},{7,5},{8,10},{9,11},{10,... | collective-permute-start | bytes 24584 | tf_op jit(solution)/shard_map/ppermute | solution.py:494
  135.6 9.2 %collective-permute-start.27 = (bf16[128,1024]{1,0:T(8,128)(2,1)S(1)}, bf16[128,1024]{1,0:T(8,128)(2,1)S(1)}, u32[]{:S(2)}, u32[]{:S(2)}) collective-permute-start(bf16[128,1024]{1,0:T(8,128)(2,1)S(1)} %get-tuple-element.29), channel_id=1, source_target_pairs={{0,2},{1,3},{2,0},{3,1},{4,6},{5,7},{6,4},{7,5},{8,10},{9,11},{10,... | collective-permute-start | bytes 786440 | tf_op jit(solution)/shard_map/ppermute | solution.py:494
  137.2 9.3 %collective-permute-start.30 = (bf16[128,1024]{1,0:T(8,128)(2,1)S(1)}, bf16[128,1024]{1,0:T(8,128)(2,1)S(1)}, u32[]{:S(2)}, u32[]{:S(2)}) collective-permute-start(bf16[128,1024]{1,0:T(8,128)(2,1)S(1)} %get-tuple-element.30), channel_id=1, source_target_pairs={{0,4},{1,5},{2,6},{3,7},{4,0},{5,1},{6,2},{7,3},{8,12},{9,13},{10,... | collective-permute-start | bytes 786440 | tf_op jit(solution)/shard_map/ppermute | solution.py:494
  139.7 10.1 %collective-permute-start.29 = (bf16[128,1024]{1,0:T(8,128)(2,1)S(1)}, bf16[128,1024]{1,0:T(8,128)(2,1)S(1)}, u32[]{:S(2)}, u32[]{:S(2)}) collective-permute-start(bf16[128,1024]{1,0:T(8,128)(2,1)S(1)} %slice.37), channel_id=1, source_target_pairs={{0,4},{1,5},{2,6},{3,7},{4,0},{5,1},{6,2},{7,3},{8,12},{9,13},{10,... | collective-permute-start | bytes 786440 | tf_op jit(solution)/shard_map/ppermute | solution.py:494
  141.2 9.2 %collective-permute-start.26 = (bf16[128,1024]{1,0:T(8,128)(2,1)S(1)}, bf16[128,1024]{1,0:T(8,128)(2,1)S(1)}, u32[]{:S(2)}, u32[]{:S(2)}) collective-permute-start(bf16[128,1024]{1,0:T(8,128)(2,1)S(1)} %slice.33), channel_id=1, source_target_pairs={{0,2},{1,3},{2,0},{3,1},{4,6},{5,7},{6,4},{7,5},{8,10},{9,11},{10,... | collective-permute-start | bytes 786440 | tf_op jit(solution)/shard_map/ppermute | solution.py:494
  145.9 6.7 %collective-permute-start.28 = (bf16[128,1024]{1,0:T(8,128)(2,1)S(1)}, bf16[128,1024]{1,0:T(8,128)(2,1)S(1)}, u32[]{:S(2)}, u32[]{:S(2)}) collective-permute-start(bf16[128,1024]{1,0:T(8,128)(2,1)S(1)} %add_convert_fusion.3), channel_id=1, source_target_pairs={{0,4},{1,5},{2,6},{3,7},{4,0},{5,1},{6,2},{7,3},{8,12},{9,13},{10,... | collective-permute-start | bytes 786440 | tf_op jit(solution)/shard_map/ppermute | solution.py:494
  147.5 6.4 %collective-permute-start.31 = (bf16[128,1024]{1,0:T(8,128)(2,1)S(1)}, bf16[128,1024]{1,0:T(8,128)(2,1)S(1)}, u32[]{:S(2)}, u32[]{:S(2)}) collective-permute-start(bf16[128,1024]{1,0:T(8,128)(2,1)S(1)} %add_convert_fusion.1), channel_id=1, source_target_pairs={{0,2},{1,3},{2,0},{3,1},{4,6},{5,7},{6,4},{7,5},{8,10},{9,11},{10,... | collective-permute-start | bytes 786440 | tf_op jit(solution)/shard_map/ppermute | solution.py:494
  (28 other events, 206.4 us)

commit v2 on v0

--- a/solution.py
+++ b/solution.py
@@ -1,8 +1,12 @@
+import functools
 import math
 
 import jax
 import jax.numpy as jnp
+import numpy as np
 from jax import lax
+from jax.experimental import pallas as pl
+from jax.experimental.pallas import tpu as pltpu
 from jax.sharding import PartitionSpec as P
 
 H = 16
@@ -81,7 +85,7 @@
     return (chosen, ranked)
 
 
-def local(
+def local_general(
     tokens,
     attn_gain,
     w_query,
@@ -175,6 +179,436 @@
     return (context[None], hidden[None], expert_mix[None])
 
 
+F32 = jnp.float32
+BF16 = jnp.bfloat16
+MIB = 1 << 20
+LANES = 128
+VMEM_ATTEND = 48
+VMEM_EXPERTS = 60
+
+
+def dot(lhs, rhs):
+    return jnp.dot(lhs, rhs, preferred_element_type=F32)
+
+
+def dot_nt(lhs, rhs):
+    return lax.dot_general(lhs, rhs, (((1,), (1,)), ((), ())), preferred_element_type=F32)
+
+
+def dot_tn(lhs, rhs):
+    return lax.dot_general(lhs, rhs, (((0,), (0,)), ((), ())), preferred_element_type=F32)
+
+
+def held_in_hbm(arrays):
+    return [pltpu.with_memory_space_constraint(array, pltpu.HBM) for array in arrays]
+
+
+def lane_index(shape):
+    return lax.broadcasted_iota(jnp.int32, shape, len(shape) - 1)
+
+
+def rope_tables(prefix_len, tok_count):
+    frequency = ROPE_BASE ** (-(np.arange(HD // 2, dtype=np.float64) * 2.0 / HD))
+    angles = (prefix_len + np.arange(tok_count, dtype=np.float64))[:, None] * frequency[None, :]
+    cosine, sine = np.cos(angles), np.sin(angles)
+    cosine = np.concatenate([cosine, cosine, cosine, cosine], axis=1)
+    sine = np.concatenate([-sine, sine, -sine, sine], axis=1)
+    return jnp.asarray(cosine, F32), jnp.asarray(sine, F32)
+
+
+def rotate_tile(tile, cosine, sine):
+    first = lane_index(tile.shape) % HD < HD // 2
+    other = jnp.where(
+        first, pltpu.roll(tile, LANES - HD // 2, 1), pltpu.roll(tile, HD // 2, 1)
+    )
+    return tile * cosine + other * sine
+
+
+SUM_ROWS = 16
+
+
+def attend_pair(queries, key_tiles, value_tiles, suffix_len, states):
+    tok_count = queries[0].shape[0] // 2
+    turned = [tile.astype(F32).T.astype(BF16) for tile in value_tiles]
+    ones = jnp.ones((SUM_ROWS, turned[0].shape[1]), BF16)
+    scores = []
+    for half in range(2):
+        scores.append([dot_nt(tile, queries[half]) for tile in key_tiles])
+        if suffix_len is not None:
+            shape = scores[half][0].shape
+            slot = lax.broadcasted_iota(jnp.int32, shape, 0)
+            row = lane_index(shape) % tok_count
+            visible = (slot <= row) & (slot < suffix_len)
+            scores[half][0] = jnp.where(visible, scores[half][0], -1e30)
+    results = []
+    for half in range(2):
+        new_max = jnp.max(functools.reduce(jnp.maximum, scores[half]), axis=0, keepdims=True)
+        total = None
+        if states is not None:
+            old_max, old_total = states[half]
+            new_max = jnp.maximum(new_max, old_max)
+            total = old_total * jnp.exp(old_max - new_max)
+        for score, tile in zip(scores[half], turned):
+            weights = jnp.exp(score - new_max).astype(BF16)
+            part = dot(jnp.concatenate([tile[half * HD : (half + 1) * HD], ones], axis=0), weights)
+            total = part if total is None else total + part
+        results.append((new_max, total))
+    return results
+
+
+def near_kernel(blocks, *refs):
+    tok_ref, gain_ref, wq_ref, wk_ref, wv_ref, cos_ref, sin_ref, len_ref = refs[:8]
+    key_refs, value_refs = refs[8 : 8 + blocks], refs[8 + blocks : 8 + 2 * blocks]
+    q_ref, max_ref, acc_ref, normed_ref = refs[8 + 2 * blocks :]
+
+    @pl.when(pl.program_id(0) == 0)
+    def _():
+        rows = tok_ref[...].astype(F32)
+        mean_square = jnp.mean(rows * rows, axis=-1, keepdims=True)
+        normed_ref[...] = (rows * lax.rsqrt(mean_square + NORM_EPS) * gain_ref[...]).astype(BF16)
+
+    normed = normed_ref[...]
+    tok_count = normed.shape[0]
+    cosine, sine = cos_ref[...], sin_ref[...]
+    low = lane_index((tok_count, LANES)) < HD
+    projected = dot(normed, wq_ref[...])
+    suffix_keys = rotate_tile(dot(normed, wk_ref[...]), cosine, sine).astype(BF16)
+    suffix_values = dot(normed, wv_ref[...]).astype(BF16)
+    queries = []
+    for half in range(2):
+        tile = rotate_tile(projected[:, half * LANES : (half + 1) * LANES], cosine, sine) * ATTN_SCALE
+        turned = pltpu.roll(tile, HD, 1)
+        if half == 0:
+            first, second = jnp.where(low, tile, 0.0), jnp.where(low, turned, 0.0)
+        else:
+            first, second = jnp.where(low, 0.0, turned), jnp.where(low, 0.0, tile)
+        queries.append(jnp.concatenate([first, second], axis=0).astype(BF16))
+        q_ref[half] = queries[half]
+    key_tiles = [suffix_keys] + [ref[...] for ref in key_refs]
+    value_tiles = [suffix_values] + [ref[...] for ref in value_refs]
+    results = attend_pair(queries, key_tiles, value_tiles, len_ref[0], None)
+    for half, (new_max, total) in enumerate(results):
+        max_ref[half] = new_max
+        acc_ref[half] = total
+
+
+def pair_spec(*shape):
+    return pl.BlockSpec((2, *shape), lambda i: (i, 0, 0))
+
+
+def whole_spec(*shape):
+    return pl.BlockSpec(shape, lambda i: (0,) * len(shape))
+
+
+def cached_specs(cached):
+    specs = []
+    for kind in range(2):
+        for array in cached:
+            stacked = not isinstance(array, tuple)
+            length = array.shape[0] // 2 if stacked else array[kind].shape[0]
+            place = kind if stacked else 0
+            specs.append(pl.BlockSpec((length, LANES), lambda i, place=place: (place, i)))
+    return specs
+
+
+def cached_args(cached):
+    return [array[kind] if isinstance(array, tuple) else array for kind in range(2) for array in cached]
+
+
+def attend_near(own_rows, attn_gain, w_query, w_key, w_value, prefix_len, suffix_len, cached):
+    tok_count, width = own_rows.shape
+    rows, blocks = 2 * tok_count, len(cached)
+    cosine, sine = rope_tables(prefix_len, tok_count)
+    column = lambda i: (0, i)
+    queries, *state = pl.pallas_call(
+        functools.partial(near_kernel, blocks),
+        grid=(KV // 2,),
+        in_specs=[
+            whole_spec(tok_count, width),
+            whole_spec(1, width),
+            pl.BlockSpec((width, 2 * LANES), column),
+            pl.BlockSpec((width, LANES), column),
+            pl.BlockSpec((width, LANES), column),
+            whole_spec(tok_count, LANES),
+            whole_spec(tok_count, LANES),
+            pl.BlockSpec(memory_space=pltpu.SMEM),
+        ]
+        + cached_specs(cached),
+        out_specs=[pair_spec(rows, LANES), pair_spec(1, rows), pair_spec(HD + SUM_ROWS, rows)],
+        out_shape=[
+            pltpu.HBM((KV, rows, LANES), BF16),
+            pltpu.HBM((KV, 1, rows), F32),
+            pltpu.HBM((KV, HD + SUM_ROWS, rows), F32),
+        ],
+        scratch_shapes=[pltpu.VMEM((tok_count, width), BF16)],
+        compiler_params=pltpu.CompilerParams(vmem_limit_bytes=VMEM_ATTEND * MIB),
+        cost_estimate=pl.CostEstimate(flops=4000 * MIB, bytes_accessed=6 * MIB, transcendentals=0),
+        name="attend_near",
+    )(
+        *held_in_hbm([own_rows, attn_gain.reshape(1, width), w_query, w_key, w_value, cosine, sine]),
+        suffix_len,
+        *held_in_hbm(cached_args(cached)),
+    )
+    return queries, state
+
+
+def far_kernel(blocks, last, *refs):
+    q_ref, max_in, acc_in = refs[:3]
+    key_refs, value_refs = refs[3 : 3 + blocks], refs[3 + blocks : 3 + 2 * blocks]
+    refs = refs[3 + 2 * blocks :]
+    states = [(max_in[half], acc_in[half]) for half in range(2)]
+    key_tiles = [ref[...] for ref in key_refs]
+    value_tiles = [ref[...] for ref in value_refs]
+    results = attend_pair([q_ref[0], q_ref[1]], key_tiles, value_tiles, None, states)
+    if not last:
+        max_ref, acc_ref = refs
+        for half, (new_max, total) in enumerate(results):
+            max_ref[half] = new_max
+            acc_ref[half] = total
+        return
+    tok_ref, w_out_ref, gain_ref, ctx_ref, hidden_ref, moe_ref, projected_ref = refs
+    tok_count = tok_ref.shape[0]
+    step = pl.program_id(0)
+    tiles = []
+    for _, total in results:
+        mixed = total[:HD] / total[HD : HD + 1]
+        tiles.append(jnp.concatenate([mixed[:, :tok_count], mixed[:, tok_count:]], axis=0).T)
+    context = jnp.concatenate(tiles, axis=1).astype(BF16)
+    ctx_ref[...] = context
+    part = dot(context, w_out_ref[...])
+
+    @pl.when(step == 0)
+    def _():
+        projected_ref[...] = part
+
+    @pl.when(step > 0)
+    def _():
+        projected_ref[...] += part
+
+    @pl.when(step == pl.num_programs(0) - 1)
+    def _():
+        hidden = (tok_ref[...].astype(F32) + RESIDUAL_SCALE * projected_ref[...]).astype(BF16)
+        hidden_ref[...] = hidden
+        wide = hidden.astype(F32)
+        mean_square = jnp.mean(wide * wide, axis=-1, keepdims=True)
+        moe_ref[...] = (wide * lax.rsqrt(mean_square + NORM_EPS) * gain_ref[...]).astype(BF16)
+
+
+def attend_far(queries, state, cached, final=None):
+    last, blocks, rows = final is not None, len(cached), queries.shape[1]
+    tok_count = rows // 2
+    args = [queries, *state, *cached_args(cached)]
+    in_specs = [pair_spec(rows, LANES), pair_spec(1, rows), pair_spec(HD + SUM_ROWS, rows)]
+    in_specs += cached_specs(cached)
+    if last:
+        own_rows, w_out, moe_gain = final
+        width = own_rows.shape[1]
+        args += [own_rows, w_out, moe_gain.reshape(1, width)]
+        whole = whole_spec(tok_count, width)
+        in_specs += [whole, pl.BlockSpec((2 * LANES, width), lambda i: (i, 0)), whole_spec(1, width)]
+        out_specs = [pl.BlockSpec((tok_count, 2 * LANES), lambda i: (0, i)), whole, whole]
+        out_shape = [pltpu.HBM((tok_count, width), BF16)] * 3
+        scratch = [pltpu.VMEM((tok_count, width), F32)]
+    else:
+        out_specs = in_specs[1:3]
+        out_shape = [pltpu.HBM(array.shape, F32) for array in state]
+        scratch = []
+    return pl.pallas_call(
+        functools.partial(far_kernel, blocks, last),
+        grid=(KV // 2,),
+        in_specs=in_specs,
+        out_specs=out_specs,
+        out_shape=out_shape,
+        scratch_shapes=scratch,
+        compiler_params=pltpu.CompilerParams(vmem_limit_bytes=VMEM_ATTEND * MIB),
+        cost_estimate=pl.CostEstimate(flops=blocks * 1200 * MIB, bytes_accessed=4 * MIB, transcendentals=0),
+        name="attend_far",
+    )(*held_in_hbm(args))
+
+
+def experts_kernel(sources, pieces, *refs):
+    refs = list(refs)
+    take = lambda n: [refs.pop(0) for _ in range(n)]
+    row_refs, route_refs = [take(pieces) for _ in range(sources)], take(sources)
+    weight_refs = [take(2) for _ in range(3)]
+    out_refs = take(sources)
+    picked_ref, made_ref, combine_ref, *held, sem = refs
+    local_experts = weight_refs[0][0].shape[0]
+    chip_experts = route_refs[0].shape[0]
+    tok_count, width = out_refs[0].shape
+    slots = chip_experts * CAP
+
+    def copy(kind, owner, e, expert):
+        return pltpu.make_async_copy(
+            weight_refs[kind][owner].at[e], held[kind].at[expert], sem.at[kind, expert]
+        )
+
+    for expert in range(chip_experts):
+        for kind in range(3):
+            copy(kind, expert // local_experts, expert % local_experts, expert).start()
+
+    before = lax.broadcasted_iota(jnp.int32, (tok_count, tok_count), 0)
+    after = lane_index((tok_count, tok_count))
+    earlier = jnp.where(before < after, 1.0, 0.0).astype(BF16)
+    slot = lax.broadcasted_iota(jnp.int32, (slots, chip_experts), 0)
+    spread = jnp.where(slot // CAP == lane_index((slots, chip_experts)), 1.0, 0.0).astype(BF16)
+    within = (lax.broadcasted_iota(jnp.int32, (slots, tok_count), 0) % CAP).astype(F32)
+    for source in range(sources):
+        route = route_refs[source][...]
+        hit = route > 0.0
+        ranked = dot(jnp.where(hit, 1.0, 0.0).astype(BF16), earlier)
+        ranked = jnp.where(hit, ranked, -1.0).astype(BF16)
+        match = dot(spread, ranked) == within
+        pick = jnp.where(match, 1.0, 0.0).astype(BF16)
+        combine_ref[source] = jnp.where(match, dot(spread, route.astype(BF16)), 0.0).astype(BF16)
+        rows = jnp.concatenate([ref[...] for ref in row_refs[source]], axis=0)
+        picked = dot(pick, rows).astype(BF16)
+        for e in range(chip_experts):
+            picked_ref[e, source] = picked[e * CAP : (e + 1) * CAP]
+
+    def one_expert(expert, carry):
+        for kind in range(3):
+            copy(kind, 0, 0, expert).wait()
+        rows = picked_ref[expert].reshape(sources * CAP, width)
+        gate = dot(rows, held[0][expert])
+        up = dot(rows, held[1][expert])
+        act = (jax.nn.silu(gate) * up).astype(BF16)
+        made = dot(act, held[2][expert]).astype(BF16)
+        for source in range(sources):
+            made_ref[source, pl.ds(pl.multiple_of(expert * CAP, CAP), CAP), :] = made[
+                source * CAP : (source + 1) * CAP
+            ]
+        return carry
+
+    lax.fori_loop(0, chip_experts, one_expert, 0)
+    for source, ref in enumerate(out_refs):
+        ref[...] = dot_tn(combine_ref[source], made_ref[source]).astype(ref.dtype)
+
+
+def run_experts(rows, routes, weights, out_type=BF16):
+    sources, pieces = len(rows), len(rows[0])
+    tok_count, width = routes[0].shape[1], rows[0][0].shape[1]
+    chip_experts = routes[0].shape[0]
+    hidden = weights[0][0].shape[2]
+    vmem = pl.BlockSpec(memory_space=pltpu.VMEM)
+    return pl.pallas_call(
+        functools.partial(experts_kernel, sources, pieces),
+        in_specs=[vmem] * ((pieces + 1) * sources) + [pl.BlockSpec(memory_space=pl.ANY)] * 6,
+        out_specs=[vmem] * sources,
+        out_shape=[pltpu.HBM((tok_count, width), out_type)] * sources,
+        scratch_shapes=[
+            pltpu.VMEM((chip_experts, sources, CAP, width), BF16),
+            pltpu.VMEM((sources, chip_experts * CAP, width), BF16),
+            pltpu.VMEM((sources, chip_experts * CAP, tok_count), BF16),
+            pltpu.VMEM((chip_experts, width, hidden), BF16),
+            pltpu.VMEM((chip_experts, width, hidden), BF16),
+            pltpu.VMEM((chip_experts, hidden, width), BF16),
+            pltpu.SemaphoreType.DMA((3, chip_experts)),
+        ],
+        compiler_params=pltpu.CompilerParams(vmem_limit_bytes=VMEM_EXPERTS * MIB),
+        cost_estimate=pl.CostEstimate(flops=12000 * MIB, bytes_accessed=30 * MIB, transcendentals=0),
+        name="experts",
+    )(*held_in_hbm([*[piece for source in rows for piece in source], *routes, *[array for pair in weights for array in pair]]))
+
+
+CORE, ACROSS_X, ACROSS_Y = 1, 2, 4
+
+
+def swap(array, mask):
+    return lax.ppermute(array, "req", [(i, i ^ mask) for i in range(lax.axis_size("req"))])
+
+
+def ordered(*arrays):
+    return lax.optimization_barrier(arrays)
+
+
+def routes_of(expert_ids, route_weights, peer_count):
+    ids, gains = expert_ids.T, route_weights.T
+    named = ids[None, :, :] == jnp.arange(EXPERTS, dtype=jnp.int32)[:, None, None]
+    dense = jnp.sum(jnp.where(named, gains[None], 0.0), axis=1)
+    tok_count = ids.shape[1]
+    dense = dense.reshape(peer_count // 2, 2, EXPERTS // peer_count, tok_count)
+    core = lax.axis_index("req") % 2
+    dense = jnp.where(core == 0, dense, dense[:, ::-1])
+    return dense.reshape(peer_count // 2, 2 * EXPERTS // peer_count, tok_count)
+
+
+def local_chips(
+    tokens,
+    attn_gain,
+    w_query,
+    w_key,
+    w_value,
+    w_out,
+    prefix_keys,
+    prefix_values,
+    lengths,
+    assignment,
+    moe_gain,
+    expert_ids,
+    route_weights,
+    w_gate,
+    w_up,
+    w_down,
+):
+    peer_count = lax.axis_size("req")
+    own_rows = tokens[0]
+    tok_count = own_rows.shape[0]
+    prefix_len = prefix_keys.shape[1] * peer_count
+    my_index = lax.axis_index("req")
+    request_ids = jnp.arange(lengths.shape[1], dtype=jnp.int32)
+    request = jnp.sum(jnp.where(request_ids == my_index, assignment[0], 0))
+    suffix_len = jnp.sum(jnp.where(request_ids == request, lengths[0], 0)).reshape(1)
+
+    keys, values = prefix_keys[0], prefix_values[0]
+    block = keys.shape[0]
+    cached = jnp.concatenate([keys, values], axis=0)
+    cached_x, cached_y = swap(cached, ACROSS_X), swap(cached, ACROSS_Y)
+    cached_mate = swap(cached, CORE)
+    gate, up = (w_gate, swap(w_gate, CORE)), (w_up, swap(w_up, CORE))
+    routes = routes_of(expert_ids[0], route_weights[0], peer_count)
+    chip = my_index // 2
+    own_route = routes[chip]
+
+    queries, state = attend_near(
+        own_rows, attn_gain, w_query, w_key, w_value, prefix_len, suffix_len, [(keys, values), cached_mate]
+    )
+    cached_x, cached_y, w_down, routes, *state = ordered(cached_x, cached_y, w_down, routes, *state)
+    far = [swap(cached_x[:block], ACROSS_Y), swap(cached_y[block:], ACROSS_X)]
+    mates = [swap(cached_x, CORE), swap(cached_y, CORE)]
+    routes = [
+        own_route,
+        swap(routes[chip ^ 1], ACROSS_X),
+        swap(routes[chip ^ 2], ACROSS_Y),
+        swap(routes[chip ^ 3], ACROSS_X | ACROSS_Y),
+    ]
+    cached_x, cached_y, w_down, *mates = ordered(cached_x, cached_y, w_down, *mates)
+    down = (w_down, swap(w_down, CORE))
+    state = attend_far(queries, state, [cached_x, cached_y, *mates])
+    *far, routes_x, routes_y, routes_xy, s0, s1 = ordered(*far, *routes[1:], *state)
+    context, hidden, moe_in = attend_far(
+        queries,
+        [s0, s1],
+        [tuple(far), tuple(swap(array, CORE) for array in far)],
+        final=(own_rows, w_out, moe_gain),
+    )
+
+    weights = (gate, up, down)
+    half = tok_count // 2
+    rows_x, rows_y = swap(moe_in, ACROSS_X), swap(moe_in, ACROSS_Y)
+    (own,) = run_experts([[moe_in]], [own_route], weights, F32)
+    rows_x, rows_y, own = ordered(rows_x, rows_y, own)
+    low_xy, high_xy = swap(rows_x[:half], ACROSS_Y), swap(rows_y[half:], ACROSS_X)
+    to_x, to_y = run_experts([[rows_x], [rows_y]], [routes_x, routes_y], weights)
+    low_xy, high_xy, to_x, to_y = ordered(low_xy, high_xy, to_x, to_y)
+    from_x, from_y = swap(to_x, ACROSS_X), swap(to_y, ACROSS_Y)
+    (to_xy,) = run_experts([[low_xy, high_xy]], [routes_xy], weights)
+    from_xy = swap(to_xy, ACROSS_X | ACROSS_Y)
+    partial, from_xy = ordered(own + from_x.astype(F32) + from_y.astype(F32), from_xy)
+    expert_mix = (partial + from_xy.astype(F32)).astype(BF16)
+    return (context[None], hidden[None], expert_mix[None])
+
+
 def solution(mesh):
     placed = (
         P("grp", "req", None),
@@ -195,7 +629,7 @@
         P("req", None, None),
     )
     return jax.shard_map(
-        local,
+        local_chips if mesh.shape["req"] == 8 else local_general,
         mesh=mesh,
         in_specs=placed,
         out_specs=(P("grp", "req", None), P("grp", "req", None), P("grp", "req", None)),

time: 348 us -> 113 us (0.32)
  blocking collectives: 75.2 us -> 0 us
  waiting for transfers between devices: 90.3 us -> 23.1 us
  Pallas kernels: 0 us -> 63.9 us
  matrix products: 63.4 us -> 0 us
  local copies, waits for them, and re-layouts: 63.7 us -> 2.24 us
  other arithmetic: 34.5 us -> 6.25 us
  between operations: 14.4 us -> 0.88 us
  starting transfers between devices: 5.23 us -> 15.8 us
    all_to_all x1 -> x0, blocking collectives: 75.2 us -> none  [local(): lax.all_to_all(outgoing, 'req', split_axis=0, concat_axis=0, tiled=True)]
    all_to_all x1 -> x0, waiting for transfers between devices: 70.2 us -> none  [local(): lax.all_to_all(produced, 'req', split_axis=0, concat_axis=0, tiled=True)]
    pallas_call x0 -> x6, Pallas kernels: none -> 63.9 us  [the longest x3 35.8 us: run_experts(): pl.pallas_call(functools.partial(experts_kernel, sources, pieces), in_spe...]
    dot_general x22 -> x0, matrix products: 63.4 us -> none  [the longest x4 21.7 us: local(): jnp.dot(product, w_down[expert_local], preferred_element_type=jnp.float32)]
    ppermute x0 -> x22, waiting for transfers between devices: none -> 23.1 us  [swap(): lax.ppermute(array, 'req', [(i, i ^ mask) for i in range(lax.axis_size('r...]
    all_gather x2 -> x0, waiting for transfers between devices: 18.8 us -> none  [the longest x1 18.2 us: local(): value_piece = lax.all_gather(prefix_values, 'req', axis=1, tiled=True)]
    another operation x7 -> x0, other arithmetic: 16.1 us -> none
    ppermute x0 -> x22, starting transfers between devices: none -> 15.8 us  [swap(): lax.ppermute(array, 'req', [(i, i ^ mask) for i in range(lax.axis_size('r...]
  transfers between devices with their start and end apart: 3 -> 22, of which waited for: 3 -> 10; matrix products, arithmetic and copies ran while one was open for 13% -> 4% of each run, Pallas kernels for 0% -> 57%
where the time goes in v2:
time: 113 us; the launch traced here: 112 us
  Pallas kernels  63.9 us (57%)
  waiting for transfers between devices  23.1 us (20%)
  starting transfers between devices  15.8 us (14%)
  other arithmetic  6.25 us (6%)
  local copies, waits for them, and re-layouts  2.24 us (2%)
    pallas_call x3, Pallas kernels, run_experts(): pl.pallas_call(functools.partial(experts_kernel, sources, pieces), in_spe...  35.8 us
    ppermute x22, waiting for transfers between devices, swap(): lax.ppermute(array, 'req', [(i, i ^ mask) for i in range(lax.axis_size('r...  23.1 us
    pallas_call x2, Pallas kernels, attend_far(): pl.pallas_call(functools.partial(far_kernel, blocks, last), grid=(KV // 2...  17.3 us
    ppermute x22, starting transfers between devices, swap(): lax.ppermute(array, 'req', [(i, i ^ mask) for i in range(lax.axis_size('r...  15.8 us
    pallas_call x1, Pallas kernels, attend_near(): pl.pallas_call(functools.partial(near_kernel, blocks), grid=(KV // 2,), i...  10.7 us
  transfers between devices with their start and end apart: 22, of which 10 were waited for; matrix products, arithmetic and copies ran while one was open for 4% of the time, Pallas kernels for 57%

profile of v2, /device:TPU:0, one launch (start us, length us, event | category | flops | bytes accessed | tf_op | source)
XLA Modules:
  0.0 112.2 jit_solution(11785864916085508137)
XLA Ops:
  0.6 1.1 pad_maximum_fusion
  1.7 0.5 collective-permute-start
  2.2 2.6 %collective-permute-start.1 = (bf16[512,512]{1,0:T(8,128)(2,1)S(1)}, bf16[512,512]{1,0:T(8,128)(2,1)S(1)}, u32[]{:S(2)}, u32[]{:S(2)}) collective-permute-start(bf16[512,512]{1,0:T(8,128)(2,1)S(1)} %pad_maximum_fusion), channel_id=1, source_target_pairs={{0,2},{1,3},{2,0},{3,1},{4,6},{5,7},{6,4},{7,5},{8,10},{9,11},{10,... | collective-permute-start | bytes 1572872 | tf_op jit(solution)/shard_map/ppermute | solution.py:518
  4.8 1.5 %collective-permute-start.2 = (bf16[512,512]{1,0:T(8,128)(2,1)S(1)}, bf16[512,512]{1,0:T(8,128)(2,1)S(1)}, u32[]{:S(2)}, u32[]{:S(2)}) collective-permute-start(bf16[512,512]{1,0:T(8,128)(2,1)S(1)} %pad_maximum_fusion), channel_id=1, source_target_pairs={{0,4},{1,5},{2,6},{3,7},{4,0},{5,1},{6,2},{7,3},{8,12},{9,13},{10,... | collective-permute-start | bytes 1572872 | tf_op jit(solution)/shard_map/ppermute | solution.py:518
  6.3 0.8 select_reduce_fusion
  7.1 1.3 %fusion.1 = s32[]{:T(128)} fusion(s32[1,8]{1,0:T(1,128)} %param.27, s32[]{:T(128)S(6)} %axis_index.16), kind=kLoop, calls=%fused_computation.13 | loop fusion | flops 23 | bytes 40 | tf_op jit(solution)/shard_map/reduce_sum | solution.py:560
  8.4 1.9 %fusion.2 = s32[]{:T(128)} fusion(s32[1,8]{1,0:T(1,128)} %param.26, s32[]{:T(128)} %fusion.1), kind=kLoop, calls=%fused_computation.14 | loop fusion | flops 23 | bytes 40 | tf_op jit(solution)/shard_map/reduce_sum | solution.py:561
  10.4 0.8 copy-done.7
  11.2 10.7 %attend_near.1 = (bf16[8,512,128]{2,1,0:T(8,128)(2,1)}, f32[8,1,512]{2,1,0:T(1,128)}, f32[8,80,512]{2,1,0:T(8,128)}) custom-call(bf16[256,1024]{1,0:T(8,128)(2,1)} %bitcast.34, f32[1,1024]{1,0:T(1,128)} %bitcast.36, bf16[1024,1024]{1,0:T(8,128)(2,1)} %refs_2_.2, bf16[1024,512]{1,0:T(8,128)(2,1)} %refs_3_.2, bf16[1024,512]{1,0:T(8,128)(2,1)} %refs_4_.3, ...), custom_call_target="tpu_custom_call" | custom-call | flops 4194304000 | bytes 6291456 | tf_op jit(solution)/shard_map/attend_near/pallas_call | solution.py:323
  22.0 0.5 collective-permute-start.9
  23.1 0.9 collective-permute-done.8.refs_5_.refs_9_
  23.9 1.5 %collective-permute-done.9.refs_6_.refs_10_ = bf16[512,512]{1,0:T(8,128)(2,1)S(1)} collective-permute-done((bf16[512,512]{1,0:T(8,128)(2,1)S(1)}, bf16[512,512]{1,0:T(8,128)(2,1)S(1)}, u32[]{:S(2)}, u32[]{:S(2)}) %collective-permute-start.9) | collective-permute-done | bytes 524320 | tf_op jit(solution)/shard_map/ppermute | solution.py:518
  25.6 0.5 collective-permute-start.5
  26.2 3.1 %collective-permute-done.5.refs_2_ = f32[8,256]{1,0:T(8,128)S(1)} collective-permute-done((f32[8,256]{1,0:T(8,128)S(1)}, f32[8,256]{1,0:T(8,128)S(1)}, u32[]{:S(2)}, u32[]{:S(2)}) %collective-permute-start.5) | collective-permute-done | bytes 8224 | tf_op jit(solution)/shard_map/ppermute | solution.py:518
  29.8 1.6 %collective-permute-start.3 = (bf16[256,512]{1,0:T(8,128)(2,1)S(1)}, bf16[256,512]{1,0:T(8,128)(2,1)S(1)}, u32[]{:S(2)}, u32[]{:S(2)}) collective-permute-start(bf16[256,512]{1,0:T(8,128)(2,1)S(1)} %slice.12), channel_id=1, source_target_pairs={{0,4},{1,5},{2,6},{3,7},{4,0},{5,1},{6,2},{7,3},{8,12},{9,13},{10,... | collective-permute-start | bytes 786440 | tf_op jit(solution)/shard_map/ppermute | solution.py:518
  31.4 2.5 %collective-permute-done.7.refs_2_ = f32[8,256]{1,0:T(8,128)S(1)} collective-permute-done((f32[8,256]{1,0:T(8,128)S(1)}, f32[8,256]{1,0:T(8,128)S(1)}, u32[]{:S(2)}, u32[]{:S(2)}) %collective-permute-start.7) | collective-permute-done | bytes 8224 | tf_op jit(solution)/shard_map/ppermute | solution.py:518
  33.9 0.5 collective-permute-start.4
  34.5 8.8 %attend_far.2 = (f32[8,1,512]{2,1,0:T(1,128)}, f32[8,80,512]{2,1,0:T(8,128)}) custom-call(bf16[8,512,128]{2,1,0:T(8,128)(2,1)} %get-tuple-element.40.refs_0_, f32[8,1,512]{2,1,0:T(1,128)} %get-tuple-element.46.refs_1_, f32[8,80,512]{2,1,0:T(8,128)} %get-tuple-element.47.refs_2_, bf16[512,512]{1,0:T(8,128)(2,1)} %copy-done.1, bf16[512,512]{1,0:T(8,128)(2,1)} %copy-done.2, ...), custom_call_target="tpu_custom_call" | custom-call | flops 5033164800 | bytes 4194304 | tf_op jit(solution)/shard_map/attend_far/pallas_call | solution.py:416
  43.4 0.5 collective-permute-start.11
  43.9 0.6 dynamic-slice_bitcast_fusion.refs_1_
  46.0 8.6 %attend_far.3 = (bf16[256,1024]{1,0:T(8,128)(2,1)}, bf16[256,1024]{1,0:T(8,128)(2,1)}, bf16[256,1024]{1,0:T(8,128)(2,1)}) custom-call(bf16[8,512,128]{2,1,0:T(8,128)(2,1)} %get-tuple-element.40.refs_0_, f32[8,1,512]{2,1,0:T(1,128)} %get-tuple-element.55.refs_1_, f32[8,80,512]{2,1,0:T(8,128)} %get-tuple-element.56.refs_2_, bf16[256,512]{1,0:T(8,128)(2,1)} %copy-done.8, ...), custom_call_target="tpu_custom_call" | custom-call | flops 2516582400 | bytes 4194304 | tf_op jit(solution)/shard_map/attend_far/pallas_call | solution.py:416
  54.5 1.6 %collective-permute-start.12 = (bf16[256,1024]{1,0:T(8,128)(2,1)}, bf16[256,1024]{1,0:T(8,128)(2,1)S(1)}, u32[]{:S(2)}, u32[]{:S(2)}) collective-permute-start(bf16[256,1024]{1,0:T(8,128)(2,1)} %get-tuple-element.61.refs_0_), channel_id=1, source_target_pairs={{0,2},{1,3},{2,0},{3,1},{4,6},{5,7},{6,4},{7,5},{8,10},{9,11},{10,... | collective-permute-start | bytes 1572872 | tf_op jit(solution)/shard_map/ppermute | solution.py:518
  56.1 0.5 collective-permute-start.13
  56.6 11.8 %experts.3 = f32[256,1024]{1,0:T(8,128)} custom-call(bf16[256,1024]{1,0:T(8,128)(2,1)} %get-tuple-element.61.refs_0_, f32[8,256]{1,0:T(8,128)} %dynamic-slice_bitcast_fusion.refs_1_, bf16[4,1024,512]{2,1,0:T(8,128)(2,1)} %refs_3_.3, bf16[4,1024,512]{2,1,0:T(8,128)(2,1)} %collective-permute-done.14.refs_3_.refs_5_.refs_4_, bf16[4,1024,512]{2,1,0:T(8,128)(2,1)} %refs_5_.2, ...), custom_call_target="tpu_custom_call" | custom-call | flops 12582912000 | bytes 31457280 | tf_op jit(solution)/shard_map/experts/pallas_call | solution.py:494
  68.8 1.2 %collective-permute-done.13.refs_1_ = bf16[256,1024]{1,0:T(8,128)(2,1)S(1)} collective-permute-done((bf16[256,1024]{1,0:T(8,128)(2,1)}, bf16[256,1024]{1,0:T(8,128)(2,1)S(1)}, u32[]{:S(2)}, u32[]{:S(2)}) %collective-permute-start.13) | collective-permute-done | bytes 524320 | tf_op jit(solution)/shard_map/ppermute | solution.py:518
  70.0 0.6 collective-permute-start.17
  71.1 12.5 %experts.4 = (bf16[256,1024]{1,0:T(8,128)(2,1)}, bf16[256,1024]{1,0:T(8,128)(2,1)}) custom-call(bf16[256,1024]{1,0:T(8,128)(2,1)} %copy-done.3, bf16[256,1024]{1,0:T(8,128)(2,1)} %copy-done.4, f32[8,256]{1,0:T(8,128)} %copy-done.15, f32[8,256]{1,0:T(8,128)} %copy-done.16, bf16[4,1024,512]{2,1,0:T(8,128)(2,1)} %refs_3_.3, ...), custom_call_target="tpu_custom_call" | custom-call | flops 12582912000 | bytes 31457280 | tf_op jit(solution)/shard_map/experts/pallas_call | solution.py:494
  83.6 1.7 %collective-permute-start.19 = (bf16[256,1024]{1,0:T(8,128)(2,1)}, bf16[256,1024]{1,0:T(8,128)(2,1)S(1)}, u32[]{:S(2)}, u32[]{:S(2)}) collective-permute-start(bf16[256,1024]{1,0:T(8,128)(2,1)} %get-tuple-element.70), channel_id=1, source_target_pairs={{0,2},{1,3},{2,0},{3,1},{4,6},{5,7},{6,4},{7,5},{8,10},{9,11},{10,... | collective-permute-start | bytes 1572872 | tf_op jit(solution)/shard_map/ppermute | solution.py:518
  85.3 1.5 %collective-permute-start.20 = (bf16[256,1024]{1,0:T(8,128)(2,1)}, bf16[256,1024]{1,0:T(8,128)(2,1)S(1)}, u32[]{:S(2)}, u32[]{:S(2)}) collective-permute-start(bf16[256,1024]{1,0:T(8,128)(2,1)} %get-tuple-element.71), channel_id=1, source_target_pairs={{0,4},{1,5},{2,6},{3,7},{4,0},{5,1},{6,2},{7,3},{8,12},{9,13},{10,... | collective-permute-start | bytes 1572872 | tf_op jit(solution)/shard_map/ppermute | solution.py:518
  86.8 11.5 %experts.5 = bf16[256,1024]{1,0:T(8,128)(2,1)} custom-call(bf16[128,1024]{1,0:T(8,128)(2,1)} %copy-done.10, bf16[128,1024]{1,0:T(8,128)(2,1)} %copy-done.12, f32[8,256]{1,0:T(8,128)} %copy-done.14, bf16[4,1024,512]{2,1,0:T(8,128)(2,1)} %refs_3_.3, bf16[4,1024,512]{2,1,0:T(8,128)(2,1)} %collective-permute-done.14.refs_3_.refs_5_.refs_4_, ...), custom_call_target="tpu_custom_call" | custom-call | flops 12582912000 | bytes 31457280 | tf_op jit(solution)/shard_map/experts/pallas_call | solution.py:494
  99.0 12.2 %collective-permute-done.21 = bf16[256,1024]{1,0:T(8,128)(2,1)S(1)} collective-permute-done((bf16[256,1024]{1,0:T(8,128)(2,1)}, bf16[256,1024]{1,0:T(8,128)(2,1)S(1)}, u32[]{:S(2)}, u32[]{:S(2)}) %collective-permute-start.21) | collective-permute-done | bytes 524320 | tf_op jit(solution)/shard_map/ppermute | solution.py:518
  111.2 0.9 fusion
  (67 shorter events, 4.5 us)
Async XLA Ops:
  1.7 8.7 %collective-permute-start = (bf16[512,512]{1,0:T(8,128)(2,1)S(1)}, bf16[512,512]{1,0:T(8,128)(2,1)S(1)}, u32[]{:S(2)}, u32[]{:S(2)}) collective-permute-start(bf16[512,512]{1,0:T(8,128)(2,1)S(1)} %pad_maximum_fusion), channel_id=1, source_target_pairs={{0,1},{1,0},{2,3},{3,2},{4,5},{5,4},{6,7},{7,6},{8,9},{9,8},{10,11... | collective-permute-start | bytes 1572872 | tf_op jit(solution)/shard_map/ppermute | solution.py:518
  2.2 19.7 %collective-permute-start.1 = (bf16[512,512]{1,0:T(8,128)(2,1)S(1)}, bf16[512,512]{1,0:T(8,128)(2,1)S(1)}, u32[]{:S(2)}, u32[]{:S(2)}) collective-permute-start(bf16[512,512]{1,0:T(8,128)(2,1)S(1)} %pad_maximum_fusion), channel_id=1, source_target_pairs={{0,2},{1,3},{2,0},{3,1},{4,6},{5,7},{6,4},{7,5},{8,10},{9,11},{10,... | collective-permute-start | bytes 1572872 | tf_op jit(solution)/shard_map/ppermute | solution.py:518
  4.8 17.2 %collective-permute-start.2 = (bf16[512,512]{1,0:T(8,128)(2,1)S(1)}, bf16[512,512]{1,0:T(8,128)(2,1)S(1)}, u32[]{:S(2)}, u32[]{:S(2)}) collective-permute-start(bf16[512,512]{1,0:T(8,128)(2,1)S(1)} %pad_maximum_fusion), channel_id=1, source_target_pairs={{0,4},{1,5},{2,6},{3,7},{4,0},{5,1},{6,2},{7,3},{8,12},{9,13},{10,... | collective-permute-start | bytes 1572872 | tf_op jit(solution)/shard_map/ppermute | solution.py:518
  21.9 12.5 %copy-start.1 = (bf16[512,512]{1,0:T(8,128)(2,1)}, bf16[512,512]{1,0:T(8,128)(2,1)S(1)}, u32[]{:S(2)}) copy-start(bf16[512,512]{1,0:T(8,128)(2,1)S(1)} %collective-permute-done.1.refs_3_.refs_7_) | copy-start | bytes 1572868
  22.0 12.5 %copy-start.2 = (bf16[512,512]{1,0:T(8,128)(2,1)}, bf16[512,512]{1,0:T(8,128)(2,1)S(1)}, u32[]{:S(2)}) copy-start(bf16[512,512]{1,0:T(8,128)(2,1)S(1)} %collective-permute-done.2.refs_4_.refs_8_) | copy-start | bytes 1572868
  22.0 2.0 %collective-permute-start.8 = (bf16[512,512]{1,0:T(8,128)(2,1)S(1)}, bf16[512,512]{1,0:T(8,128)(2,1)S(1)}, u32[]{:S(2)}, u32[]{:S(2)}) collective-permute-start(bf16[512,512]{1,0:T(8,128)(2,1)S(1)} %collective-permute-done.1.refs_3_.refs_7_), channel_id=1, source_target_pairs={{0,1},{1,0},{2,3},{3,2},{4,5},{5,4},{6,7},{7,6},{8,9},{9,8},{10,11... | collective-permute-start | bytes 1572872 | tf_op jit(solution)/shard_map/ppermute | solution.py:518
  22.0 3.4 %collective-permute-start.9 = (bf16[512,512]{1,0:T(8,128)(2,1)S(1)}, bf16[512,512]{1,0:T(8,128)(2,1)S(1)}, u32[]{:S(2)}, u32[]{:S(2)}) collective-permute-start(bf16[512,512]{1,0:T(8,128)(2,1)S(1)} %collective-permute-done.2.refs_4_.refs_8_), channel_id=1, source_target_pairs={{0,1},{1,0},{2,3},{3,2},{4,5},{5,4},{6,7},{7,6},{8,9},{9,8},{10,11... | collective-permute-start | bytes 1572872 | tf_op jit(solution)/shard_map/ppermute | solution.py:518
  22.5 34.1 %collective-permute-start.14 = (bf16[4,1024,512]{2,1,0:T(8,128)(2,1)}, bf16[4,1024,512]{2,1,0:T(8,128)(2,1)}, u32[]{:S(2)}, u32[]{:S(2)}) collective-permute-start(bf16[4,1024,512]{2,1,0:T(8,128)(2,1)} %refs_3_.3), channel_id=1, source_target_pairs={{0,1},{1,0},{2,3},{3,2},{4,5},{5,4},{6,7},{7,6},{8,9},{9,8},{10,11... | collective-permute-start | bytes 12582920 | tf_op jit(solution)/shard_map/ppermute | solution.py:518
  22.6 34.0 %collective-permute-start.15 = (bf16[4,1024,512]{2,1,0:T(8,128)(2,1)}, bf16[4,1024,512]{2,1,0:T(8,128)(2,1)}, u32[]{:S(2)}, u32[]{:S(2)}) collective-permute-start(bf16[4,1024,512]{2,1,0:T(8,128)(2,1)} %refs_5_.2), channel_id=1, source_target_pairs={{0,1},{1,0},{2,3},{3,2},{4,5},{5,4},{6,7},{7,6},{8,9},{9,8},{10,11... | collective-permute-start | bytes 12582920 | tf_op jit(solution)/shard_map/ppermute | solution.py:518
  23.9 10.5 %copy-start.5 = (bf16[512,512]{1,0:T(8,128)(2,1)}, bf16[512,512]{1,0:T(8,128)(2,1)S(1)}, u32[]{:S(2)}) copy-start(bf16[512,512]{1,0:T(8,128)(2,1)S(1)} %collective-permute-done.8.refs_5_.refs_9_) | copy-start | bytes 1572868
  25.4 9.0 %copy-start.6 = (bf16[512,512]{1,0:T(8,128)(2,1)}, bf16[512,512]{1,0:T(8,128)(2,1)S(1)}, u32[]{:S(2)}) copy-start(bf16[512,512]{1,0:T(8,128)(2,1)S(1)} %collective-permute-done.9.refs_6_.refs_10_) | copy-start | bytes 1572868
  25.4 31.2 %collective-permute-start.16 = (bf16[4,512,1024]{2,1,0:T(8,128)(2,1)}, bf16[4,512,1024]{2,1,0:T(8,128)(2,1)}, u32[]{:S(2)}, u32[]{:S(2)}) collective-permute-start(bf16[4,512,1024]{2,1,0:T(8,128)(2,1)} %refs_7_), channel_id=1, source_target_pairs={{0,1},{1,0},{2,3},{3,2},{4,5},{5,4},{6,7},{7,6},{8,9},{9,8},{10,11... | collective-permute-start | bytes 12582920 | tf_op jit(solution)/shard_map/ppermute | solution.py:518
  25.6 3.7 %collective-permute-start.5 = (f32[8,256]{1,0:T(8,128)S(1)}, f32[8,256]{1,0:T(8,128)S(1)}, u32[]{:S(2)}, u32[]{:S(2)}) collective-permute-start(f32[8,256]{1,0:T(8,128)S(1)} %get-tuple-element.79), channel_id=1, source_target_pairs={{0,2},{1,3},{2,0},{3,1},{4,6},{5,7},{6,4},{7,5},{8,10},{9,11},{10,... | collective-permute-start | bytes 24584 | tf_op jit(solution)/shard_map/ppermute | solution.py:518
  26.1 3.7 %collective-permute-start.6 = (f32[8,256]{1,0:T(8,128)S(1)}, f32[8,256]{1,0:T(8,128)S(1)}, u32[]{:S(2)}, u32[]{:S(2)}) collective-permute-start(f32[8,256]{1,0:T(8,128)S(1)} %get-tuple-element.78), channel_id=1, source_target_pairs={{0,4},{1,5},{2,6},{3,7},{4,0},{5,1},{6,2},{7,3},{8,12},{9,13},{10,... | collective-permute-start | bytes 24584 | tf_op jit(solution)/shard_map/ppermute | solution.py:518
  29.3 14.0 %copy-start.15 = (f32[8,256]{1,0:T(8,128)}, f32[8,256]{1,0:T(8,128)S(1)}, u32[]{:S(2)}) copy-start(f32[8,256]{1,0:T(8,128)S(1)} %collective-permute-done.5.refs_2_) | copy-start | bytes 24580
  29.3 4.7 %collective-permute-start.7 = (f32[8,256]{1,0:T(8,128)S(1)}, f32[8,256]{1,0:T(8,128)S(1)}, u32[]{:S(2)}, u32[]{:S(2)}) collective-permute-start(f32[8,256]{1,0:T(8,128)S(1)} %get-tuple-element.77), channel_id=1, source_target_pairs={{0,6},{1,7},{2,4},{3,5},{4,2},{5,3},{6,0},{7,1},{8,14},{9,15},{10,... | collective-permute-start | bytes 24584 | tf_op jit(solution)/shard_map/ppermute | solution.py:518
  29.8 13.4 %copy-start.16 = (f32[8,256]{1,0:T(8,128)}, f32[8,256]{1,0:T(8,128)S(1)}, u32[]{:S(2)}) copy-start(f32[8,256]{1,0:T(8,128)S(1)} %collective-permute-done.6.refs_3_) | copy-start | bytes 24580
  29.8 13.5 %collective-permute-start.3 = (bf16[256,512]{1,0:T(8,128)(2,1)S(1)}, bf16[256,512]{1,0:T(8,128)(2,1)S(1)}, u32[]{:S(2)}, u32[]{:S(2)}) collective-permute-start(bf16[256,512]{1,0:T(8,128)(2,1)S(1)} %slice.12), channel_id=1, source_target_pairs={{0,4},{1,5},{2,6},{3,7},{4,0},{5,1},{6,2},{7,3},{8,12},{9,13},{10,... | collective-permute-start | bytes 786440 | tf_op jit(solution)/shard_map/ppermute | solution.py:518
  33.9 9.3 %copy-start.14 = (f32[8,256]{1,0:T(8,128)}, f32[8,256]{1,0:T(8,128)S(1)}, u32[]{:S(2)}) copy-start(f32[8,256]{1,0:T(8,128)S(1)} %collective-permute-done.7.refs_2_) | copy-start | bytes 24580
  33.9 9.4 %collective-permute-start.4 = (bf16[256,512]{1,0:T(8,128)(2,1)S(1)}, bf16[256,512]{1,0:T(8,128)(2,1)S(1)}, u32[]{:S(2)}, u32[]{:S(2)}) collective-permute-start(bf16[256,512]{1,0:T(8,128)(2,1)S(1)} %slice.13), channel_id=1, source_target_pairs={{0,2},{1,3},{2,0},{3,1},{4,6},{5,7},{6,4},{7,5},{8,10},{9,11},{10,... | collective-permute-start | bytes 786440 | tf_op jit(solution)/shard_map/ppermute | solution.py:518
  43.3 1.6 %collective-permute-start.10 = (bf16[256,512]{1,0:T(8,128)(2,1)S(1)}, bf16[256,512]{1,0:T(8,128)(2,1)S(1)}, u32[]{:S(2)}, u32[]{:S(2)}) collective-permute-start(bf16[256,512]{1,0:T(8,128)(2,1)S(1)} %collective-permute-done.3.refs_3_), channel_id=1, source_target_pairs={{0,1},{1,0},{2,3},{3,2},{4,5},{5,4},{6,7},{7,6},{8,9},{9,8},{10,11... | collective-permute-start | bytes 786440 | tf_op jit(solution)/shard_map/ppermute | solution.py:518
  43.4 1.9 %collective-permute-start.11 = (bf16[256,512]{1,0:T(8,128)(2,1)S(1)}, bf16[256,512]{1,0:T(8,128)(2,1)S(1)}, u32[]{:S(2)}, u32[]{:S(2)}) collective-permute-start(bf16[256,512]{1,0:T(8,128)(2,1)S(1)} %collective-permute-done.4.refs_5_), channel_id=1, source_target_pairs={{0,1},{1,0},{2,3},{3,2},{4,5},{5,4},{6,7},{7,6},{8,9},{9,8},{10,11... | collective-permute-start | bytes 786440 | tf_op jit(solution)/shard_map/ppermute | solution.py:518
  54.5 14.2 %collective-permute-start.12 = (bf16[256,1024]{1,0:T(8,128)(2,1)}, bf16[256,1024]{1,0:T(8,128)(2,1)S(1)}, u32[]{:S(2)}, u32[]{:S(2)}) collective-permute-start(bf16[256,1024]{1,0:T(8,128)(2,1)} %get-tuple-element.61.refs_0_), channel_id=1, source_target_pairs={{0,2},{1,3},{2,0},{3,1},{4,6},{5,7},{6,4},{7,5},{8,10},{9,11},{10,... | collective-permute-start | bytes 1572872 | tf_op jit(solution)/shard_map/ppermute | solution.py:518
  56.1 13.9 %collective-permute-start.13 = (bf16[256,1024]{1,0:T(8,128)(2,1)}, bf16[256,1024]{1,0:T(8,128)(2,1)S(1)}, u32[]{:S(2)}, u32[]{:S(2)}) collective-permute-start(bf16[256,1024]{1,0:T(8,128)(2,1)} %get-tuple-element.61.refs_0_), channel_id=1, source_target_pairs={{0,4},{1,5},{2,6},{3,7},{4,0},{5,1},{6,2},{7,3},{8,12},{9,13},{10,... | collective-permute-start | bytes 1572872 | tf_op jit(solution)/shard_map/ppermute | solution.py:518
  70.0 13.6 %collective-permute-start.17 = (bf16[128,1024]{1,0:T(8,128)(2,1)S(1)}, bf16[128,1024]{1,0:T(8,128)(2,1)S(1)}, u32[]{:S(2)}, u32[]{:S(2)}) collective-permute-start(bf16[128,1024]{1,0:T(8,128)(2,1)S(1)} %slice.14), channel_id=1, source_target_pairs={{0,4},{1,5},{2,6},{3,7},{4,0},{5,1},{6,2},{7,3},{8,12},{9,13},{10,... | collective-permute-start | bytes 786440 | tf_op jit(solution)/shard_map/ppermute | solution.py:518
  70.6 13.0 %collective-permute-start.18 = (bf16[128,1024]{1,0:T(8,128)(2,1)S(1)}, bf16[128,1024]{1,0:T(8,128)(2,1)S(1)}, u32[]{:S(2)}, u32[]{:S(2)}) collective-permute-start(bf16[128,1024]{1,0:T(8,128)(2,1)S(1)} %slice.15), channel_id=1, source_target_pairs={{0,2},{1,3},{2,0},{3,1},{4,6},{5,7},{6,4},{7,5},{8,10},{9,11},{10,... | collective-permute-start | bytes 786440 | tf_op jit(solution)/shard_map/ppermute | solution.py:518
  83.6 3.3 %copy-start.10 = (bf16[128,1024]{1,0:T(8,128)(2,1)}, bf16[128,1024]{1,0:T(8,128)(2,1)S(1)}, u32[]{:S(2)}) copy-start(bf16[128,1024]{1,0:T(8,128)(2,1)S(1)} %collective-permute-done.17.refs_0_) | copy-start | bytes 786436
  83.6 3.2 %copy-start.12 = (bf16[128,1024]{1,0:T(8,128)(2,1)}, bf16[128,1024]{1,0:T(8,128)(2,1)S(1)}, u32[]{:S(2)}) copy-start(bf16[128,1024]{1,0:T(8,128)(2,1)S(1)} %collective-permute-done.18.refs_1_) | copy-start | bytes 786436
  83.6 15.2 %copy-start = (f32[256,1024]{1,0:T(8,128)S(1)}, f32[256,1024]{1,0:T(8,128)}, u32[]{:S(2)}) copy-start(f32[256,1024]{1,0:T(8,128)} %experts.3) | copy-start | bytes 3145732
  83.6 15.2 %collective-permute-start.19 = (bf16[256,1024]{1,0:T(8,128)(2,1)}, bf16[256,1024]{1,0:T(8,128)(2,1)S(1)}, u32[]{:S(2)}, u32[]{:S(2)}) collective-permute-start(bf16[256,1024]{1,0:T(8,128)(2,1)} %get-tuple-element.70), channel_id=1, source_target_pairs={{0,2},{1,3},{2,0},{3,1},{4,6},{5,7},{6,4},{7,5},{8,10},{9,11},{10,... | collective-permute-start | bytes 1572872 | tf_op jit(solution)/shard_map/ppermute | solution.py:518
  85.3 13.4 %collective-permute-start.20 = (bf16[256,1024]{1,0:T(8,128)(2,1)}, bf16[256,1024]{1,0:T(8,128)(2,1)S(1)}, u32[]{:S(2)}, u32[]{:S(2)}) collective-permute-start(bf16[256,1024]{1,0:T(8,128)(2,1)} %get-tuple-element.71), channel_id=1, source_target_pairs={{0,4},{1,5},{2,6},{3,7},{4,0},{5,1},{6,2},{7,3},{8,12},{9,13},{10,... | collective-permute-start | bytes 1572872 | tf_op jit(solution)/shard_map/ppermute | solution.py:518
  98.4 12.9 %collective-permute-start.21 = (bf16[256,1024]{1,0:T(8,128)(2,1)}, bf16[256,1024]{1,0:T(8,128)(2,1)S(1)}, u32[]{:S(2)}, u32[]{:S(2)}) collective-permute-start(bf16[256,1024]{1,0:T(8,128)(2,1)} %experts.5), channel_id=1, source_target_pairs={{0,6},{1,7},{2,4},{3,5},{4,2},{5,3},{6,0},{7,1},{8,14},{9,15},{10,... | collective-permute-start | bytes 1572872 | tf_op jit(solution)/shard_map/ppermute | solution.py:518
  (7 other events, 9.5 us)

commit v3 on v2

--- a/solution.py
+++ b/solution.py
@@ -184,7 +184,8 @@
 MIB = 1 << 20
 LANES = 128
 VMEM_ATTEND = 48
-VMEM_EXPERTS = 60
+NOTE_ROWS = 16
+VMEM_EXPERTS = 50
 
 
 def dot(lhs, rhs):
@@ -201,6 +202,10 @@
 
 def held_in_hbm(arrays):
     return [pltpu.with_memory_space_constraint(array, pltpu.HBM) for array in arrays]
+
+
+def held_in_vmem(arrays):
+    return [pltpu.with_memory_space_constraint(array, pltpu.VMEM) for array in arrays]
 
 
 def lane_index(shape):
@@ -257,9 +262,10 @@
 
 
 def near_kernel(blocks, *refs):
-    tok_ref, gain_ref, wq_ref, wk_ref, wv_ref, cos_ref, sin_ref, len_ref = refs[:8]
-    key_refs, value_refs = refs[8 : 8 + blocks], refs[8 + blocks : 8 + 2 * blocks]
-    q_ref, max_ref, acc_ref, normed_ref = refs[8 + 2 * blocks :]
+    tok_ref, gain_ref, wq_ref, wk_ref, wv_ref, cos_ref, sin_ref, lengths_ref, order_ref = refs[:9]
+    key_refs, value_refs = refs[9 : 9 + blocks], refs[9 + blocks : 9 + 2 * blocks]
+    q_ref, max_ref, acc_ref, normed_ref = refs[9 + 2 * blocks :]
+    suffix_len = lengths_ref[0, order_ref[0, lax.axis_index("req")]]
 
     @pl.when(pl.program_id(0) == 0)
     def _():
@@ -286,7 +292,7 @@
         q_ref[half] = queries[half]
     key_tiles = [suffix_keys] + [ref[...] for ref in key_refs]
     value_tiles = [suffix_values] + [ref[...] for ref in value_refs]
-    results = attend_pair(queries, key_tiles, value_tiles, len_ref[0], None)
+    results = attend_pair(queries, key_tiles, value_tiles, suffix_len, None)
     for half, (new_max, total) in enumerate(results):
         max_ref[half] = new_max
         acc_ref[half] = total
@@ -305,7 +311,7 @@
     for kind in range(2):
         for array in cached:
             stacked = not isinstance(array, tuple)
-            length = array.shape[0] // 2 if stacked else array[kind].shape[0]
+            length = array.shape[0] // 2 if stacked else array[0].shape[0]
             place = kind if stacked else 0
             specs.append(pl.BlockSpec((length, LANES), lambda i, place=place: (place, i)))
     return specs
@@ -315,8 +321,9 @@
     return [array[kind] if isinstance(array, tuple) else array for kind in range(2) for array in cached]
 
 
-def attend_near(own_rows, attn_gain, w_query, w_key, w_value, prefix_len, suffix_len, cached):
+def attend_near(own_rows, attn_gain, w_query, w_key, w_value, prefix_len, lengths, assignment, keys, values, mate):
     tok_count, width = own_rows.shape
+    cached = [(keys, values), mate]
     rows, blocks = 2 * tok_count, len(cached)
     cosine, sine = rope_tables(prefix_len, tok_count)
     column = lambda i: (0, i)
@@ -332,13 +339,14 @@
             whole_spec(tok_count, LANES),
             whole_spec(tok_count, LANES),
             pl.BlockSpec(memory_space=pltpu.SMEM),
+            pl.BlockSpec(memory_space=pltpu.SMEM),
         ]
         + cached_specs(cached),
         out_specs=[pair_spec(rows, LANES), pair_spec(1, rows), pair_spec(HD + SUM_ROWS, rows)],
         out_shape=[
-            pltpu.HBM((KV, rows, LANES), BF16),
-            pltpu.HBM((KV, 1, rows), F32),
-            pltpu.HBM((KV, HD + SUM_ROWS, rows), F32),
+            pltpu.VMEM((KV, rows, LANES), BF16),
+            pltpu.VMEM((KV, 1, rows), F32),
+            pltpu.VMEM((KV, HD + SUM_ROWS, rows), F32),
         ],
         scratch_shapes=[pltpu.VMEM((tok_count, width), BF16)],
         compiler_params=pltpu.CompilerParams(vmem_limit_bytes=VMEM_ATTEND * MIB),
@@ -346,8 +354,10 @@
         name="attend_near",
     )(
         *held_in_hbm([own_rows, attn_gain.reshape(1, width), w_query, w_key, w_value, cosine, sine]),
-        suffix_len,
-        *held_in_hbm(cached_args(cached)),
+        *held_in_hbm([lengths, assignment, keys]),
+        held_in_vmem([mate])[0],
+        *held_in_hbm([values]),
+        held_in_vmem([mate])[0],
     )
     return queries, state
 
@@ -366,7 +376,7 @@
             max_ref[half] = new_max
             acc_ref[half] = total
         return
-    tok_ref, w_out_ref, gain_ref, ctx_ref, hidden_ref, moe_ref, projected_ref = refs
+    tok_ref, w_out_ref, gain_ref, ids_ref, route_ref, ctx_ref, hidden_ref, moe_ref, projected_ref = refs
     tok_count = tok_ref.shape[0]
     step = pl.program_id(0)
     tiles = []
@@ -391,27 +401,32 @@
         hidden_ref[...] = hidden
         wide = hidden.astype(F32)
         mean_square = jnp.mean(wide * wide, axis=-1, keepdims=True)
-        moe_ref[...] = (wide * lax.rsqrt(mean_square + NORM_EPS) * gain_ref[...]).astype(BF16)
+        moe_ref[:tok_count] = (wide * lax.rsqrt(mean_square + NORM_EPS) * gain_ref[...]).astype(BF16)
+        moe_ref[tok_count:] = jnp.zeros((NOTE_ROWS, wide.shape[1]), BF16)
+        moe_ref[tok_count : tok_count + TOP, :tok_count] = ids_ref[...].astype(F32).astype(BF16)
+        moe_ref[tok_count : tok_count + TOP, tok_count : 2 * tok_count] = route_ref[...].astype(BF16)
 
 
 def attend_far(queries, state, cached, final=None):
     last, blocks, rows = final is not None, len(cached), queries.shape[1]
     tok_count = rows // 2
-    args = [queries, *state, *cached_args(cached)]
+    args, tiles = [queries, *state], held_in_vmem(cached_args(cached))
     in_specs = [pair_spec(rows, LANES), pair_spec(1, rows), pair_spec(HD + SUM_ROWS, rows)]
     in_specs += cached_specs(cached)
     if last:
-        own_rows, w_out, moe_gain = final
+        own_rows, w_out, moe_gain, expert_ids, route_weights = final
         width = own_rows.shape[1]
-        args += [own_rows, w_out, moe_gain.reshape(1, width)]
+        own_args = [own_rows, w_out, moe_gain.reshape(1, width), expert_ids.T, route_weights.T]
         whole = whole_spec(tok_count, width)
         in_specs += [whole, pl.BlockSpec((2 * LANES, width), lambda i: (i, 0)), whole_spec(1, width)]
-        out_specs = [pl.BlockSpec((tok_count, 2 * LANES), lambda i: (0, i)), whole, whole]
-        out_shape = [pltpu.HBM((tok_count, width), BF16)] * 3
+        in_specs += [whole_spec(TOP, tok_count)] * 2
+        out_specs = [pl.BlockSpec((tok_count, 2 * LANES), lambda i: (0, i)), whole, whole_spec(tok_count + NOTE_ROWS, width)]
+        out_shape = [pltpu.HBM((tok_count, width), BF16)] * 2 + [pltpu.VMEM((tok_count + NOTE_ROWS, width), BF16)]
         scratch = [pltpu.VMEM((tok_count, width), F32)]
     else:
+        own_args = []
         out_specs = in_specs[1:3]
-        out_shape = [pltpu.HBM(array.shape, F32) for array in state]
+        out_shape = [pltpu.VMEM(array.shape, F32) for array in state]
         scratch = []
     return pl.pallas_call(
         functools.partial(far_kernel, blocks, last),
@@ -423,20 +438,22 @@
         compiler_params=pltpu.CompilerParams(vmem_limit_bytes=VMEM_ATTEND * MIB),
         cost_estimate=pl.CostEstimate(flops=blocks * 1200 * MIB, bytes_accessed=4 * MIB, transcendentals=0),
         name="attend_far",
-    )(*held_in_hbm(args))
+    )(*held_in_vmem(args), *tiles, *held_in_hbm(own_args))
 
 
 def experts_kernel(sources, pieces, *refs):
     refs = list(refs)
     take = lambda n: [refs.pop(0) for _ in range(n)]
-    row_refs, route_refs = [take(pieces) for _ in range(sources)], take(sources)
+    row_refs = [take(pieces) for _ in range(sources)]
     weight_refs = [take(2) for _ in range(3)]
     out_refs = take(sources)
     picked_ref, made_ref, combine_ref, *held, sem = refs
     local_experts = weight_refs[0][0].shape[0]
-    chip_experts = route_refs[0].shape[0]
+    chip_experts = 2 * local_experts
     tok_count, width = out_refs[0].shape
     slots = chip_experts * CAP
+    me = lax.axis_index("req")
+    first_own, first_mate = me * local_experts, (me + 1 - 2 * lax.rem(me, 2)) * local_experts
 
     def copy(kind, owner, e, expert):
         return pltpu.make_async_copy(
@@ -450,18 +467,24 @@
     before = lax.broadcasted_iota(jnp.int32, (tok_count, tok_count), 0)
     after = lane_index((tok_count, tok_count))
     earlier = jnp.where(before < after, 1.0, 0.0).astype(BF16)
-    slot = lax.broadcasted_iota(jnp.int32, (slots, chip_experts), 0)
-    spread = jnp.where(slot // CAP == lane_index((slots, chip_experts)), 1.0, 0.0).astype(BF16)
+    slot = lax.broadcasted_iota(jnp.int32, (slots, EXPERTS), 0) // CAP
+    held_here = jnp.where(slot < local_experts, slot + first_own, slot + (first_mate - local_experts))
+    spread = jnp.where(held_here == lane_index((slots, EXPERTS)), 1.0, 0.0).astype(BF16)
     within = (lax.broadcasted_iota(jnp.int32, (slots, tok_count), 0) % CAP).astype(F32)
+    expert_row = lax.broadcasted_iota(jnp.int32, (EXPERTS, tok_count), 0).astype(F32)
     for source in range(sources):
-        route = route_refs[source][...]
+        message = jnp.concatenate([ref[...] for ref in row_refs[source]], axis=0)
+        rows, note = message[:tok_count], message[tok_count:].astype(F32)
+        route = jnp.zeros((EXPERTS, tok_count), F32)
+        for k in range(TOP):
+            chosen, gain = note[k : k + 1, :tok_count], note[k : k + 1, tok_count : 2 * tok_count]
+            route = jnp.where(chosen == expert_row, gain, route)
         hit = route > 0.0
         ranked = dot(jnp.where(hit, 1.0, 0.0).astype(BF16), earlier)
         ranked = jnp.where(hit, ranked, -1.0).astype(BF16)
         match = dot(spread, ranked) == within
         pick = jnp.where(match, 1.0, 0.0).astype(BF16)
         combine_ref[source] = jnp.where(match, dot(spread, route.astype(BF16)), 0.0).astype(BF16)
-        rows = jnp.concatenate([ref[...] for ref in row_refs[source]], axis=0)
         picked = dot(pick, rows).astype(BF16)
         for e in range(chip_experts):
             picked_ref[e, source] = picked[e * CAP : (e + 1) * CAP]
@@ -485,17 +508,17 @@
         ref[...] = dot_tn(combine_ref[source], made_ref[source]).astype(ref.dtype)
 
 
-def run_experts(rows, routes, weights, out_type=BF16):
+def run_experts(rows, weights, out_type=BF16):
     sources, pieces = len(rows), len(rows[0])
-    tok_count, width = routes[0].shape[1], rows[0][0].shape[1]
-    chip_experts = routes[0].shape[0]
+    tok_count, width = sum(piece.shape[0] for piece in rows[0]) - NOTE_ROWS, rows[0][0].shape[1]
+    chip_experts = 2 * weights[0][0].shape[0]
     hidden = weights[0][0].shape[2]
     vmem = pl.BlockSpec(memory_space=pltpu.VMEM)
     return pl.pallas_call(
         functools.partial(experts_kernel, sources, pieces),
-        in_specs=[vmem] * ((pieces + 1) * sources) + [pl.BlockSpec(memory_space=pl.ANY)] * 6,
+        in_specs=[vmem] * (pieces * sources) + [pl.BlockSpec(memory_space=pl.ANY)] * 6,
         out_specs=[vmem] * sources,
-        out_shape=[pltpu.HBM((tok_count, width), out_type)] * sources,
+        out_shape=[pltpu.VMEM((tok_count, width), out_type)] * sources,
         scratch_shapes=[
             pltpu.VMEM((chip_experts, sources, CAP, width), BF16),
             pltpu.VMEM((sources, chip_experts * CAP, width), BF16),
@@ -508,7 +531,10 @@
         compiler_params=pltpu.CompilerParams(vmem_limit_bytes=VMEM_EXPERTS * MIB),
         cost_estimate=pl.CostEstimate(flops=12000 * MIB, bytes_accessed=30 * MIB, transcendentals=0),
         name="experts",
-    )(*held_in_hbm([*[piece for source in rows for piece in source], *routes, *[array for pair in weights for array in pair]]))
+    )(
+        *held_in_vmem([piece for source in rows for piece in source]),
+        *[array for pair in weights for array in pair],
+    )
 
 
 CORE, ACROSS_X, ACROSS_Y = 1, 2, 4
@@ -520,17 +546,6 @@
 
 def ordered(*arrays):
     return lax.optimization_barrier(arrays)
-
-
-def routes_of(expert_ids, route_weights, peer_count):
-    ids, gains = expert_ids.T, route_weights.T
-    named = ids[None, :, :] == jnp.arange(EXPERTS, dtype=jnp.int32)[:, None, None]
-    dense = jnp.sum(jnp.where(named, gains[None], 0.0), axis=1)
-    tok_count = ids.shape[1]
-    dense = dense.reshape(peer_count // 2, 2, EXPERTS // peer_count, tok_count)
-    core = lax.axis_index("req") % 2
-    dense = jnp.where(core == 0, dense, dense[:, ::-1])
-    return dense.reshape(peer_count // 2, 2 * EXPERTS // peer_count, tok_count)
 
 
 def local_chips(
@@ -555,54 +570,42 @@
     own_rows = tokens[0]
     tok_count = own_rows.shape[0]
     prefix_len = prefix_keys.shape[1] * peer_count
-    my_index = lax.axis_index("req")
-    request_ids = jnp.arange(lengths.shape[1], dtype=jnp.int32)
-    request = jnp.sum(jnp.where(request_ids == my_index, assignment[0], 0))
-    suffix_len = jnp.sum(jnp.where(request_ids == request, lengths[0], 0)).reshape(1)
-
     keys, values = prefix_keys[0], prefix_values[0]
     block = keys.shape[0]
     cached = jnp.concatenate([keys, values], axis=0)
     cached_x, cached_y = swap(cached, ACROSS_X), swap(cached, ACROSS_Y)
     cached_mate = swap(cached, CORE)
-    gate, up = (w_gate, swap(w_gate, CORE)), (w_up, swap(w_up, CORE))
-    routes = routes_of(expert_ids[0], route_weights[0], peer_count)
-    chip = my_index // 2
-    own_route = routes[chip]
 
     queries, state = attend_near(
-        own_rows, attn_gain, w_query, w_key, w_value, prefix_len, suffix_len, [(keys, values), cached_mate]
-    )
-    cached_x, cached_y, w_down, routes, *state = ordered(cached_x, cached_y, w_down, routes, *state)
+        own_rows, attn_gain, w_query, w_key, w_value, prefix_len, lengths, assignment, keys, values, cached_mate
+    )
+    cached_x, cached_y, *state = ordered(cached_x, cached_y, *state)
     far = [swap(cached_x[:block], ACROSS_Y), swap(cached_y[block:], ACROSS_X)]
     mates = [swap(cached_x, CORE), swap(cached_y, CORE)]
-    routes = [
-        own_route,
-        swap(routes[chip ^ 1], ACROSS_X),
-        swap(routes[chip ^ 2], ACROSS_Y),
-        swap(routes[chip ^ 3], ACROSS_X | ACROSS_Y),
-    ]
-    cached_x, cached_y, w_down, *mates = ordered(cached_x, cached_y, w_down, *mates)
-    down = (w_down, swap(w_down, CORE))
+    *mates, w_gate = ordered(*mates, w_gate)
+    gate = (w_gate, swap(w_gate, CORE))
     state = attend_far(queries, state, [cached_x, cached_y, *mates])
-    *far, routes_x, routes_y, routes_xy, s0, s1 = ordered(*far, *routes[1:], *state)
+    *far, gate, s0, s1 = ordered(*far, gate, *state)
+    far_mate = [swap(array, CORE) for array in far]
+    *far_mate, w_up, w_down = ordered(*far_mate, w_up, w_down)
+    up, down = (w_up, swap(w_up, CORE)), (w_down, swap(w_down, CORE))
     context, hidden, moe_in = attend_far(
         queries,
         [s0, s1],
-        [tuple(far), tuple(swap(array, CORE) for array in far)],
-        final=(own_rows, w_out, moe_gain),
+        [tuple(far), tuple(far_mate)],
+        final=(own_rows, w_out, moe_gain, expert_ids[0], route_weights[0]),
     )
 
     weights = (gate, up, down)
     half = tok_count // 2
     rows_x, rows_y = swap(moe_in, ACROSS_X), swap(moe_in, ACROSS_Y)
-    (own,) = run_experts([[moe_in]], [own_route], weights, F32)
+    (own,) = run_experts([[moe_in]], weights, F32)
     rows_x, rows_y, own = ordered(rows_x, rows_y, own)
     low_xy, high_xy = swap(rows_x[:half], ACROSS_Y), swap(rows_y[half:], ACROSS_X)
-    to_x, to_y = run_experts([[rows_x], [rows_y]], [routes_x, routes_y], weights)
+    to_x, to_y = run_experts([[rows_x], [rows_y]], weights)
     low_xy, high_xy, to_x, to_y = ordered(low_xy, high_xy, to_x, to_y)
     from_x, from_y = swap(to_x, ACROSS_X), swap(to_y, ACROSS_Y)
-    (to_xy,) = run_experts([[low_xy, high_xy]], [routes_xy], weights)
+    (to_xy,) = run_experts([[low_xy, high_xy]], weights)
     from_xy = swap(to_xy, ACROSS_X | ACROSS_Y)
     partial, from_xy = ordered(own + from_x.astype(F32) + from_y.astype(F32), from_xy)
     expert_mix = (partial + from_xy.astype(F32)).astype(BF16)

time: 113 us -> 98.2 us (0.87)
  Pallas kernels: 63.9 us -> 56.7 us
  other arithmetic: 6.25 us -> 2.24 us
  local copies, waits for them, and re-layouts: 2.24 us -> 0.08 us
    reduce_sum x3 -> x0, other arithmetic: 4.03 us -> none  [the longest x1 1.94 us: local_chips(): jnp.sum(jnp.where(request_ids == request, lengths[0], 0)).reshape(1)]
    pallas_call x3, Pallas kernels: 35.8 us -> 32 us  [run_experts(): pl.pallas_call(functools.partial(experts_kernel, sources, pieces), in_spe...]
    pallas_call x2, Pallas kernels: 17.3 us -> 15.2 us  [attend_far(): pl.pallas_call(functools.partial(far_kernel, blocks, last), grid=(KV // 2...]
    unnamed x34 -> x4, local copies, waits for them, and re-layouts: 1.54 us -> 0.01 us
    pallas_call x1, Pallas kernels: 10.7 us -> 9.45 us  [attend_near(): pl.pallas_call(functools.partial(near_kernel, blocks), grid=(KV // 2,), i...]
    ppermute x22 -> x19, starting transfers between devices: 15.8 us -> 15.2 us  [swap(): lax.ppermute(array, 'req', [(i, i ^ mask) for i in range(lax.axis_size('r...]
    ppermute x22 -> x19, waiting for transfers between devices: 23.1 us -> 23.1 us  [swap(): lax.ppermute(array, 'req', [(i, i ^ mask) for i in range(lax.axis_size('r...]
  transfers between devices with their start and end apart: 22 -> 19, of which waited for: 10 -> 12; matrix products, arithmetic and copies ran while one was open for 4% -> 0% of each run, Pallas kernels for 57% -> 58%
where the time goes in v3:
time: 98.2 us; the launch traced here: 98 us
  Pallas kernels  56.7 us (58%)
  waiting for transfers between devices  23.1 us (24%)
  starting transfers between devices  15.2 us (15%)
  other arithmetic  2.24 us (2%)
    pallas_call x3, Pallas kernels, run_experts(): pl.pallas_call(functools.partial(experts_kernel, sources, pieces), in_spe...  32 us
    ppermute x19, waiting for transfers between devices, swap(): lax.ppermute(array, 'req', [(i, i ^ mask) for i in range(lax.axis_size('r...  23.1 us
    pallas_call x2, Pallas kernels, attend_far(): pl.pallas_call(functools.partial(far_kernel, blocks, last), grid=(KV // 2...  15.2 us
    ppermute x19, starting transfers between devices, swap(): lax.ppermute(array, 'req', [(i, i ^ mask) for i in range(lax.axis_size('r...  15.2 us
    pallas_call x1, Pallas kernels, attend_near(): pl.pallas_call(functools.partial(near_kernel, blocks), grid=(KV // 2,), i...  9.45 us
  transfers between devices with their start and end apart: 19, of which 12 were waited for; matrix products, arithmetic and copies ran while one was open for 0% of the time, Pallas kernels for 58%

profile of v3, /device:TPU:0, one launch (start us, length us, event | category | flops | bytes accessed | tf_op | source)
XLA Modules:
  0.0 98.0 jit_solution(12329153436540548530)
XLA Ops:
  0.6 1.1 %pad_maximum_fusion = bf16[512,512]{1,0:T(8,128)(2,1)S(1)} fusion(bf16[256,512]{1,0:T(8,128)(2,1)} %bitcast.17, bf16[256,512]{1,0:T(8,128)(2,1)} %bitcast.15), kind=kLoop, calls=%fused_computation.3 | loop fusion | flops 1048576 | bytes 1048576 | tf_op jit(solution)/shard_map/concatenate | solution.py:575
  1.7 0.5 collective-permute-start
  2.2 2.6 %collective-permute-start.2 = (bf16[512,512]{1,0:T(8,128)(2,1)S(1)}, bf16[512,512]{1,0:T(8,128)(2,1)S(1)}, u32[]{:S(2)}, u32[]{:S(2)}) collective-permute-start(bf16[512,512]{1,0:T(8,128)(2,1)S(1)} %pad_maximum_fusion), channel_id=1, source_target_pairs={{0,4},{1,5},{2,6},{3,7},{4,0},{5,1},{6,2},{7,3},{8,12},{9,13},{10,... | collective-permute-start | bytes 1572872 | tf_op jit(solution)/shard_map/ppermute | solution.py:544
  4.8 1.5 %collective-permute-start.1 = (bf16[512,512]{1,0:T(8,128)(2,1)S(1)}, bf16[512,512]{1,0:T(8,128)(2,1)S(1)}, u32[]{:S(2)}, u32[]{:S(2)}) collective-permute-start(bf16[512,512]{1,0:T(8,128)(2,1)S(1)} %pad_maximum_fusion), channel_id=1, source_target_pairs={{0,2},{1,3},{2,0},{3,1},{4,6},{5,7},{6,4},{7,5},{8,10},{9,11},{10,... | collective-permute-start | bytes 1572872 | tf_op jit(solution)/shard_map/ppermute | solution.py:544
  6.3 9.4 %attend_near.1 = (bf16[8,512,128]{2,1,0:T(8,128)(2,1)S(1)}, f32[8,1,512]{2,1,0:T(1,128)S(1)}, f32[8,80,512]{2,1,0:T(8,128)S(1)}) custom-call(bf16[256,1024]{1,0:T(8,128)(2,1)} %bitcast.19, f32[1,1024]{1,0:T(1,128)} %bitcast.23, bf16[1024,1024]{1,0:T(8,128)(2,1)} %refs_2_.1, bf16[1024,512]{1,0:T(8,128)(2,1)} %refs_3_.1, bf16[1024,512]{1,0:T(8,128)(2,1)} %refs_4_.1, ...), custom_call_target="tpu_custom_call" | custom-call | flops 4194304000 | bytes 6291456 | tf_op jit(solution)/shard_map/attend_near/pallas_call | solution.py:330
  15.8 1.6 %collective-permute-done.2.refs_4_.refs_8_ = bf16[512,512]{1,0:T(8,128)(2,1)S(1)} collective-permute-done((bf16[512,512]{1,0:T(8,128)(2,1)S(1)}, bf16[512,512]{1,0:T(8,128)(2,1)S(1)}, u32[]{:S(2)}, u32[]{:S(2)}) %collective-permute-start.2) | collective-permute-done | bytes 524320 | tf_op jit(solution)/shard_map/ppermute | solution.py:544
  17.3 1.5 %collective-permute-done.1.refs_3_.refs_7_ = bf16[512,512]{1,0:T(8,128)(2,1)S(1)} collective-permute-done((bf16[512,512]{1,0:T(8,128)(2,1)S(1)}, bf16[512,512]{1,0:T(8,128)(2,1)S(1)}, u32[]{:S(2)}, u32[]{:S(2)}) %collective-permute-start.1) | collective-permute-done | bytes 524320 | tf_op jit(solution)/shard_map/ppermute | solution.py:544
  18.8 0.5 collective-permute-start.6
  19.3 1.4 %collective-permute-done.5.refs_5_.refs_9_ = bf16[512,512]{1,0:T(8,128)(2,1)S(1)} collective-permute-done((bf16[512,512]{1,0:T(8,128)(2,1)S(1)}, bf16[512,512]{1,0:T(8,128)(2,1)S(1)}, u32[]{:S(2)}, u32[]{:S(2)}) %collective-permute-start.5) | collective-permute-done | bytes 524320 | tf_op jit(solution)/shard_map/ppermute | solution.py:544
  20.7 0.7 collective-permute-done.6.refs_6_.refs_10_
  21.7 1.6 %collective-permute-start.4 = (bf16[256,512]{1,0:T(8,128)(2,1)S(1)}, bf16[256,512]{1,0:T(8,128)(2,1)S(1)}, u32[]{:S(2)}, u32[]{:S(2)}) collective-permute-start(bf16[256,512]{1,0:T(8,128)(2,1)S(1)} %slice.13), channel_id=1, source_target_pairs={{0,2},{1,3},{2,0},{3,1},{4,6},{5,7},{6,4},{7,5},{8,10},{9,11},{10,... | collective-permute-start | bytes 786440 | tf_op jit(solution)/shard_map/ppermute | solution.py:544
  23.2 0.5 collective-permute-start.3
  23.7 7.1 %attend_far.2 = (f32[8,1,512]{2,1,0:T(1,128)S(1)}, f32[8,80,512]{2,1,0:T(8,128)S(1)}) custom-call(bf16[8,512,128]{2,1,0:T(8,128)(2,1)S(1)} %get-tuple-element.39.refs_0_, f32[8,1,512]{2,1,0:T(1,128)S(1)} %get-tuple-element.45.refs_1_, f32[8,80,512]{2,1,0:T(8,128)S(1)} %get-tuple-element.46.refs_2_, ...), custom_call_target="tpu_custom_call" | custom-call | flops 5033164800 | bytes 4194304 | tf_op jit(solution)/shard_map/attend_far/pallas_call | solution.py:431
  30.8 0.7 collective-permute-done.3.refs_3_
  31.5 0.5 collective-permute-start.9
  32.0 1.0 %collective-permute-done.8.refs_4_ = bf16[256,512]{1,0:T(8,128)(2,1)S(1)} collective-permute-done((bf16[256,512]{1,0:T(8,128)(2,1)S(1)}, bf16[256,512]{1,0:T(8,128)(2,1)S(1)}, u32[]{:S(2)}, u32[]{:S(2)}) %collective-permute-start.8) | collective-permute-done | bytes 262176 | tf_op jit(solution)/shard_map/ppermute | solution.py:544
  33.1 0.4 collective-permute-done.9.refs_6_
  33.9 8.2 %attend_far.3 = (bf16[256,1024]{1,0:T(8,128)(2,1)}, bf16[256,1024]{1,0:T(8,128)(2,1)}, bf16[272,1024]{1,0:T(8,128)(2,1)S(1)}) custom-call(bf16[8,512,128]{2,1,0:T(8,128)(2,1)S(1)} %get-tuple-element.39.refs_0_, f32[8,1,512]{2,1,0:T(1,128)S(1)} %get-tuple-element.51.refs_1_, f32[8,80,512]{2,1,0:T(8,128)S(1)} %get-tuple-element.52.refs_2_, ...), custom_call_target="tpu_custom_call" | custom-call | flops 2516582400 | bytes 4194304 | tf_op jit(solution)/shard_map/attend_far/pallas_call | solution.py:431
  42.1 0.9 collective-permute-start.11
  43.0 0.5 collective-permute-start.10
  43.6 1.8 %collective-permute-done.12.refs_4_.refs_5_ = bf16[4,1024,512]{2,1,0:T(8,128)(2,1)} collective-permute-done((bf16[4,1024,512]{2,1,0:T(8,128)(2,1)S(1)}, bf16[4,1024,512]{2,1,0:T(8,128)(2,1)}, u32[]{:S(2)}, u32[]{:S(2)}) %collective-permute-start.12) | collective-permute-done | bytes 4194336 | tf_op jit(solution)/shard_map/ppermute | solution.py:544
  45.4 1.6 %collective-permute-done.13.refs_6_.refs_7_ = bf16[4,512,1024]{2,1,0:T(8,128)(2,1)} collective-permute-done((bf16[4,512,1024]{2,1,0:T(8,128)(2,1)}, bf16[4,512,1024]{2,1,0:T(8,128)(2,1)}, u32[]{:S(2)}, u32[]{:S(2)}) %collective-permute-start.13) | collective-permute-done | bytes 4194336 | tf_op jit(solution)/shard_map/ppermute | solution.py:544
  46.9 10.2 %experts.3 = f32[256,1024]{1,0:T(8,128)S(1)} custom-call(bf16[272,1024]{1,0:T(8,128)(2,1)S(1)} %get-tuple-element.59.refs_0_, bf16[4,1024,512]{2,1,0:T(8,128)(2,1)} %refs_2_.3, bf16[4,1024,512]{2,1,0:T(8,128)(2,1)} %collective-permute-done.7.refs_2_.refs_3_, bf16[4,1024,512]{2,1,0:T(8,128)(2,1)} %refs_4_.3, ...), custom_call_target="tpu_custom_call" | custom-call | flops 12582912000 | bytes 31457280 | tf_op jit(solution)/shard_map/experts/pallas_call | solution.py:517
  57.4 1.2 %collective-permute-start.14 = (bf16[128,1024]{1,0:T(8,128)(2,1)S(1)}, bf16[128,1024]{1,0:T(8,128)(2,1)S(1)}, u32[]{:S(2)}, u32[]{:S(2)}) collective-permute-start(bf16[128,1024]{1,0:T(8,128)(2,1)S(1)} %slice.14), channel_id=1, source_target_pairs={{0,4},{1,5},{2,6},{3,7},{4,0},{5,1},{6,2},{7,3},{8,12},{9,13},{10,... | collective-permute-start | bytes 786440 | tf_op jit(solution)/shard_map/ppermute | solution.py:544
  58.6 0.6 collective-permute-start.15
  59.2 11.6 %experts.4 = (bf16[256,1024]{1,0:T(8,128)(2,1)S(1)}, bf16[256,1024]{1,0:T(8,128)(2,1)S(1)}) custom-call(bf16[272,1024]{1,0:T(8,128)(2,1)S(1)} %collective-permute-done.10.refs_0_, bf16[272,1024]{1,0:T(8,128)(2,1)S(1)} %collective-permute-done.11.refs_1_, bf16[4,1024,512]{2,1,0:T(8,128)(2,1)} %refs_2_.3, ...), custom_call_target="tpu_custom_call" | custom-call | flops 12582912000 | bytes 31457280 | tf_op jit(solution)/shard_map/experts/pallas_call | solution.py:517
  70.8 1.5 %collective-permute-start.16 = (bf16[256,1024]{1,0:T(8,128)(2,1)S(1)}, bf16[256,1024]{1,0:T(8,128)(2,1)S(1)}, u32[]{:S(2)}, u32[]{:S(2)}) collective-permute-start(bf16[256,1024]{1,0:T(8,128)(2,1)S(1)} %get-tuple-element.69), channel_id=1, source_target_pairs={{0,2},{1,3},{2,0},{3,1},{4,6},{5,7},{6,4},{7,5},{8,10},{9,11},{10,... | collective-permute-start | bytes 1572872 | tf_op jit(solution)/shard_map/ppermute | solution.py:544
  72.4 1.0 collective-permute-start.17
  73.3 10.2 %experts.5 = bf16[256,1024]{1,0:T(8,128)(2,1)S(1)} custom-call(bf16[128,1024]{1,0:T(8,128)(2,1)S(1)} %collective-permute-done.14.refs_0_, bf16[144,1024]{1,0:T(8,128)(2,1)S(1)} %collective-permute-done.15.refs_1_, bf16[4,1024,512]{2,1,0:T(8,128)(2,1)} %refs_2_.3, bf16[4,1024,512]{2,1,0:T(8,128)(2,1)} %collective-permute-done.7.refs_2_.refs_3_, ...), custom_call_target="tpu_custom_call" | custom-call | flops 12582912000 | bytes 31457280 | tf_op jit(solution)/shard_map/experts/pallas_call | solution.py:517
  83.5 1.1 %collective-permute-start.18 = (bf16[256,1024]{1,0:T(8,128)(2,1)S(1)}, bf16[256,1024]{1,0:T(8,128)(2,1)S(1)}, u32[]{:S(2)}, u32[]{:S(2)}) collective-permute-start(bf16[256,1024]{1,0:T(8,128)(2,1)S(1)} %experts.5), channel_id=1, source_target_pairs={{0,6},{1,7},{2,4},{3,5},{4,2},{5,3},{6,0},{7,1},{8,14},{9,15},{10,... | collective-permute-start | bytes 1572872 | tf_op jit(solution)/shard_map/ppermute | solution.py:544
  85.3 11.8 %collective-permute-done.18 = bf16[256,1024]{1,0:T(8,128)(2,1)S(1)} collective-permute-done((bf16[256,1024]{1,0:T(8,128)(2,1)S(1)}, bf16[256,1024]{1,0:T(8,128)(2,1)S(1)}, u32[]{:S(2)}, u32[]{:S(2)}) %collective-permute-start.18) | collective-permute-done | bytes 524320 | tf_op jit(solution)/shard_map/ppermute | solution.py:544
  97.1 0.9 fusion
  (23 shorter events, 1.6 us)
Async XLA Ops:
  1.7 4.6 %collective-permute-start = (bf16[512,512]{1,0:T(8,128)(2,1)S(1)}, bf16[512,512]{1,0:T(8,128)(2,1)S(1)}, u32[]{:S(2)}, u32[]{:S(2)}) collective-permute-start(bf16[512,512]{1,0:T(8,128)(2,1)S(1)} %pad_maximum_fusion), channel_id=1, source_target_pairs={{0,1},{1,0},{2,3},{3,2},{4,5},{5,4},{6,7},{7,6},{8,9},{9,8},{10,11... | collective-permute-start | bytes 1572872 | tf_op jit(solution)/shard_map/ppermute | solution.py:544
  2.2 15.1 %collective-permute-start.2 = (bf16[512,512]{1,0:T(8,128)(2,1)S(1)}, bf16[512,512]{1,0:T(8,128)(2,1)S(1)}, u32[]{:S(2)}, u32[]{:S(2)}) collective-permute-start(bf16[512,512]{1,0:T(8,128)(2,1)S(1)} %pad_maximum_fusion), channel_id=1, source_target_pairs={{0,4},{1,5},{2,6},{3,7},{4,0},{5,1},{6,2},{7,3},{8,12},{9,13},{10,... | collective-permute-start | bytes 1572872 | tf_op jit(solution)/shard_map/ppermute | solution.py:544
  4.8 14.0 %collective-permute-start.1 = (bf16[512,512]{1,0:T(8,128)(2,1)S(1)}, bf16[512,512]{1,0:T(8,128)(2,1)S(1)}, u32[]{:S(2)}, u32[]{:S(2)}) collective-permute-start(bf16[512,512]{1,0:T(8,128)(2,1)S(1)} %pad_maximum_fusion), channel_id=1, source_target_pairs={{0,2},{1,3},{2,0},{3,1},{4,6},{5,7},{6,4},{7,5},{8,10},{9,11},{10,... | collective-permute-start | bytes 1572872 | tf_op jit(solution)/shard_map/ppermute | solution.py:544
  6.3 15.2 %copy-start = (bf16[4,1024,512]{2,1,0:T(8,128)(2,1)S(1)}, bf16[4,1024,512]{2,1,0:T(8,128)(2,1)}, u32[]{:S(2)}) copy-start(bf16[4,1024,512]{2,1,0:T(8,128)(2,1)} %refs_2_.3) | copy-start | bytes 12582916
  18.8 1.9 %collective-permute-start.5 = (bf16[512,512]{1,0:T(8,128)(2,1)S(1)}, bf16[512,512]{1,0:T(8,128)(2,1)S(1)}, u32[]{:S(2)}, u32[]{:S(2)}) collective-permute-start(bf16[512,512]{1,0:T(8,128)(2,1)S(1)} %collective-permute-done.1.refs_3_.refs_7_), channel_id=1, source_target_pairs={{0,1},{1,0},{2,3},{3,2},{4,5},{5,4},{6,7},{7,6},{8,9},{9,8},{10,11... | collective-permute-start | bytes 1572872 | tf_op jit(solution)/shard_map/ppermute | solution.py:544
  18.8 2.7 %collective-permute-start.6 = (bf16[512,512]{1,0:T(8,128)(2,1)S(1)}, bf16[512,512]{1,0:T(8,128)(2,1)S(1)}, u32[]{:S(2)}, u32[]{:S(2)}) collective-permute-start(bf16[512,512]{1,0:T(8,128)(2,1)S(1)} %collective-permute-done.2.refs_4_.refs_8_), channel_id=1, source_target_pairs={{0,1},{1,0},{2,3},{3,2},{4,5},{5,4},{6,7},{7,6},{8,9},{9,8},{10,11... | collective-permute-start | bytes 1572872 | tf_op jit(solution)/shard_map/ppermute | solution.py:544
  21.5 10.1 %collective-permute-start.7 = (bf16[4,1024,512]{2,1,0:T(8,128)(2,1)S(1)}, bf16[4,1024,512]{2,1,0:T(8,128)(2,1)}, u32[]{:S(2)}, u32[]{:S(2)}) collective-permute-start(bf16[4,1024,512]{2,1,0:T(8,128)(2,1)S(1)} %copy-done), channel_id=1, source_target_pairs={{0,1},{1,0},{2,3},{3,2},{4,5},{5,4},{6,7},{7,6},{8,9},{9,8},{10,11... | collective-permute-start | bytes 12582920 | tf_op jit(solution)/shard_map/ppermute | solution.py:544
  21.7 9.2 %collective-permute-start.4 = (bf16[256,512]{1,0:T(8,128)(2,1)S(1)}, bf16[256,512]{1,0:T(8,128)(2,1)S(1)}, u32[]{:S(2)}, u32[]{:S(2)}) collective-permute-start(bf16[256,512]{1,0:T(8,128)(2,1)S(1)} %slice.13), channel_id=1, source_target_pairs={{0,2},{1,3},{2,0},{3,1},{4,6},{5,7},{6,4},{7,5},{8,10},{9,11},{10,... | collective-permute-start | bytes 786440 | tf_op jit(solution)/shard_map/ppermute | solution.py:544
  23.2 8.3 %collective-permute-start.3 = (bf16[256,512]{1,0:T(8,128)(2,1)S(1)}, bf16[256,512]{1,0:T(8,128)(2,1)S(1)}, u32[]{:S(2)}, u32[]{:S(2)}) collective-permute-start(bf16[256,512]{1,0:T(8,128)(2,1)S(1)} %slice.12), channel_id=1, source_target_pairs={{0,4},{1,5},{2,6},{3,7},{4,0},{5,1},{6,2},{7,3},{8,12},{9,13},{10,... | collective-permute-start | bytes 786440 | tf_op jit(solution)/shard_map/ppermute | solution.py:544
  23.7 9.7 %copy-start.1 = (bf16[4,1024,512]{2,1,0:T(8,128)(2,1)S(1)}, bf16[4,1024,512]{2,1,0:T(8,128)(2,1)}, u32[]{:S(2)}) copy-start(bf16[4,1024,512]{2,1,0:T(8,128)(2,1)} %refs_4_.3) | copy-start | bytes 12582916
  31.5 1.5 %collective-permute-start.8 = (bf16[256,512]{1,0:T(8,128)(2,1)S(1)}, bf16[256,512]{1,0:T(8,128)(2,1)S(1)}, u32[]{:S(2)}, u32[]{:S(2)}) collective-permute-start(bf16[256,512]{1,0:T(8,128)(2,1)S(1)} %collective-permute-done.3.refs_3_), channel_id=1, source_target_pairs={{0,1},{1,0},{2,3},{3,2},{4,5},{5,4},{6,7},{7,6},{8,9},{9,8},{10,11... | collective-permute-start | bytes 786440 | tf_op jit(solution)/shard_map/ppermute | solution.py:544
  31.5 1.9 %collective-permute-start.9 = (bf16[256,512]{1,0:T(8,128)(2,1)S(1)}, bf16[256,512]{1,0:T(8,128)(2,1)S(1)}, u32[]{:S(2)}, u32[]{:S(2)}) collective-permute-start(bf16[256,512]{1,0:T(8,128)(2,1)S(1)} %collective-permute-done.4.refs_5_), channel_id=1, source_target_pairs={{0,1},{1,0},{2,3},{3,2},{4,5},{5,4},{6,7},{7,6},{8,9},{9,8},{10,11... | collective-permute-start | bytes 786440 | tf_op jit(solution)/shard_map/ppermute | solution.py:544
  33.4 11.9 %collective-permute-start.12 = (bf16[4,1024,512]{2,1,0:T(8,128)(2,1)S(1)}, bf16[4,1024,512]{2,1,0:T(8,128)(2,1)}, u32[]{:S(2)}, u32[]{:S(2)}) collective-permute-start(bf16[4,1024,512]{2,1,0:T(8,128)(2,1)S(1)} %copy-done.1), channel_id=1, source_target_pairs={{0,1},{1,0},{2,3},{3,2},{4,5},{5,4},{6,7},{7,6},{8,9},{9,8},{10,11... | collective-permute-start | bytes 12582920 | tf_op jit(solution)/shard_map/ppermute | solution.py:544
  33.6 13.4 %collective-permute-start.13 = (bf16[4,512,1024]{2,1,0:T(8,128)(2,1)}, bf16[4,512,1024]{2,1,0:T(8,128)(2,1)}, u32[]{:S(2)}, u32[]{:S(2)}) collective-permute-start(bf16[4,512,1024]{2,1,0:T(8,128)(2,1)} %refs_6_.2), channel_id=1, source_target_pairs={{0,1},{1,0},{2,3},{3,2},{4,5},{5,4},{6,7},{7,6},{8,9},{9,8},{10,11... | collective-permute-start | bytes 12582920 | tf_op jit(solution)/shard_map/ppermute | solution.py:544
  42.1 15.0 %collective-permute-start.11 = (bf16[272,1024]{1,0:T(8,128)(2,1)S(1)}, bf16[272,1024]{1,0:T(8,128)(2,1)S(1)}, u32[]{:S(2)}, u32[]{:S(2)}) collective-permute-start(bf16[272,1024]{1,0:T(8,128)(2,1)S(1)} %get-tuple-element.59.refs_0_), channel_id=1, source_target_pairs={{0,4},{1,5},{2,6},{3,7},{4,0},{5,1},{6,2},{7,3},{8,12},{9,13},{10,... | collective-permute-start | bytes 1671176 | tf_op jit(solution)/shard_map/ppermute | solution.py:544
  43.0 14.4 %collective-permute-start.10 = (bf16[272,1024]{1,0:T(8,128)(2,1)S(1)}, bf16[272,1024]{1,0:T(8,128)(2,1)S(1)}, u32[]{:S(2)}, u32[]{:S(2)}) collective-permute-start(bf16[272,1024]{1,0:T(8,128)(2,1)S(1)} %get-tuple-element.59.refs_0_), channel_id=1, source_target_pairs={{0,2},{1,3},{2,0},{3,1},{4,6},{5,7},{6,4},{7,5},{8,10},{9,11},{10,... | collective-permute-start | bytes 1671176 | tf_op jit(solution)/shard_map/ppermute | solution.py:544
  57.4 13.4 %collective-permute-start.14 = (bf16[128,1024]{1,0:T(8,128)(2,1)S(1)}, bf16[128,1024]{1,0:T(8,128)(2,1)S(1)}, u32[]{:S(2)}, u32[]{:S(2)}) collective-permute-start(bf16[128,1024]{1,0:T(8,128)(2,1)S(1)} %slice.14), channel_id=1, source_target_pairs={{0,4},{1,5},{2,6},{3,7},{4,0},{5,1},{6,2},{7,3},{8,12},{9,13},{10,... | collective-permute-start | bytes 786440 | tf_op jit(solution)/shard_map/ppermute | solution.py:544
  58.6 12.2 %collective-permute-start.15 = (bf16[144,1024]{1,0:T(8,128)(2,1)S(1)}, bf16[144,1024]{1,0:T(8,128)(2,1)S(1)}, u32[]{:S(2)}, u32[]{:S(2)}) collective-permute-start(bf16[144,1024]{1,0:T(8,128)(2,1)S(1)} %slice.15), channel_id=1, source_target_pairs={{0,2},{1,3},{2,0},{3,1},{4,6},{5,7},{6,4},{7,5},{8,10},{9,11},{10,... | collective-permute-start | bytes 884744 | tf_op jit(solution)/shard_map/ppermute | solution.py:544
  70.8 13.8 %collective-permute-start.16 = (bf16[256,1024]{1,0:T(8,128)(2,1)S(1)}, bf16[256,1024]{1,0:T(8,128)(2,1)S(1)}, u32[]{:S(2)}, u32[]{:S(2)}) collective-permute-start(bf16[256,1024]{1,0:T(8,128)(2,1)S(1)} %get-tuple-element.69), channel_id=1, source_target_pairs={{0,2},{1,3},{2,0},{3,1},{4,6},{5,7},{6,4},{7,5},{8,10},{9,11},{10,... | collective-permute-start | bytes 1572872 | tf_op jit(solution)/shard_map/ppermute | solution.py:544
  72.4 12.7 %collective-permute-start.17 = (bf16[256,1024]{1,0:T(8,128)(2,1)S(1)}, bf16[256,1024]{1,0:T(8,128)(2,1)S(1)}, u32[]{:S(2)}, u32[]{:S(2)}) collective-permute-start(bf16[256,1024]{1,0:T(8,128)(2,1)S(1)} %get-tuple-element.70), channel_id=1, source_target_pairs={{0,4},{1,5},{2,6},{3,7},{4,0},{5,1},{6,2},{7,3},{8,12},{9,13},{10,... | collective-permute-start | bytes 1572872 | tf_op jit(solution)/shard_map/ppermute | solution.py:544
  83.5 13.5 %collective-permute-start.18 = (bf16[256,1024]{1,0:T(8,128)(2,1)S(1)}, bf16[256,1024]{1,0:T(8,128)(2,1)S(1)}, u32[]{:S(2)}, u32[]{:S(2)}) collective-permute-start(bf16[256,1024]{1,0:T(8,128)(2,1)S(1)} %experts.5), channel_id=1, source_target_pairs={{0,6},{1,7},{2,4},{3,5},{4,2},{5,3},{6,0},{7,1},{8,14},{9,15},{10,... | collective-permute-start | bytes 1572872 | tf_op jit(solution)/shard_map/ppermute | solution.py:544

commit v4 on v3

--- a/solution.py
+++ b/solution.py
@@ -185,7 +185,7 @@
 LANES = 128
 VMEM_ATTEND = 48
 NOTE_ROWS = 16
-VMEM_EXPERTS = 50
+VMEM_EXPERTS = 30
 
 
 def dot(lhs, rhs):
@@ -232,74 +232,77 @@
 SUM_ROWS = 16
 
 
-def attend_pair(queries, key_tiles, value_tiles, suffix_len, states):
+def attend_heads(queries, key_tiles, value_tiles, suffix_len, states):
+    heads = len(queries)
     tok_count = queries[0].shape[0] // 2
-    turned = [tile.astype(F32).T.astype(BF16) for tile in value_tiles]
-    ones = jnp.ones((SUM_ROWS, turned[0].shape[1]), BF16)
-    scores = []
-    for half in range(2):
-        scores.append([dot_nt(tile, queries[half]) for tile in key_tiles])
+    turned = [[tile.astype(F32).T.astype(BF16) for tile in tiles] for tiles in value_tiles]
+    ones = jnp.ones((SUM_ROWS, turned[0][0].shape[1]), BF16)
+
+    def scores_of(head):
+        scores = [dot_nt(tile, queries[head]) for tile in key_tiles[head // 2]]
         if suffix_len is not None:
-            shape = scores[half][0].shape
+            shape = scores[0].shape
             slot = lax.broadcasted_iota(jnp.int32, shape, 0)
             row = lane_index(shape) % tok_count
             visible = (slot <= row) & (slot < suffix_len)
-            scores[half][0] = jnp.where(visible, scores[half][0], -1e30)
+            scores[0] = jnp.where(visible, scores[0], -1e30)
+        return scores
+
     results = []
-    for half in range(2):
-        new_max = jnp.max(functools.reduce(jnp.maximum, scores[half]), axis=0, keepdims=True)
+    ahead = scores_of(0)
+    for head in range(heads):
+        scores, ahead = ahead, scores_of(head + 1) if head + 1 < heads else None
+        new_max = jnp.max(functools.reduce(jnp.maximum, scores), axis=0, keepdims=True)
         total = None
         if states is not None:
-            old_max, old_total = states[half]
+            old_max, old_total = states[head]
             new_max = jnp.maximum(new_max, old_max)
             total = old_total * jnp.exp(old_max - new_max)
-        for score, tile in zip(scores[half], turned):
+        first_row = head % 2 * HD
+        for score, tile in zip(scores, turned[head // 2]):
             weights = jnp.exp(score - new_max).astype(BF16)
-            part = dot(jnp.concatenate([tile[half * HD : (half + 1) * HD], ones], axis=0), weights)
+            part = dot(jnp.concatenate([tile[first_row : first_row + HD], ones], axis=0), weights)
             total = part if total is None else total + part
         results.append((new_max, total))
     return results
 
 
-def near_kernel(blocks, *refs):
-    tok_ref, gain_ref, wq_ref, wk_ref, wv_ref, cos_ref, sin_ref, lengths_ref, order_ref = refs[:9]
-    key_refs, value_refs = refs[9 : 9 + blocks], refs[9 + blocks : 9 + 2 * blocks]
-    q_ref, max_ref, acc_ref, normed_ref = refs[9 + 2 * blocks :]
+def pair_tiles(refs):
+    pairs = refs[0].shape[1] // LANES
+    return [[ref[:, pair * LANES : (pair + 1) * LANES] for ref in refs] for pair in range(pairs)]
+
+
+def near_kernel(*refs):
+    tok_ref, gain_ref, *held = refs[:5]
+    cos_ref, sin_ref, lengths_ref, order_ref, keys_ref, values_ref, mate_keys_ref, mate_values_ref = refs[5:13]
+    q_ref, max_ref, acc_ref = refs[13:]
     suffix_len = lengths_ref[0, order_ref[0, lax.axis_index("req")]]
-
-    @pl.when(pl.program_id(0) == 0)
-    def _():
-        rows = tok_ref[...].astype(F32)
-        mean_square = jnp.mean(rows * rows, axis=-1, keepdims=True)
-        normed_ref[...] = (rows * lax.rsqrt(mean_square + NORM_EPS) * gain_ref[...]).astype(BF16)
-
-    normed = normed_ref[...]
-    tok_count = normed.shape[0]
+    rows = tok_ref[...].astype(F32)
+    mean_square = jnp.mean(rows * rows, axis=-1, keepdims=True)
+    normed = (rows * lax.rsqrt(mean_square + NORM_EPS) * gain_ref[...]).astype(BF16)
     cosine, sine = cos_ref[...], sin_ref[...]
-    low = lane_index((tok_count, LANES)) < HD
-    projected = dot(normed, wq_ref[...])
-    suffix_keys = rotate_tile(dot(normed, wk_ref[...]), cosine, sine).astype(BF16)
-    suffix_values = dot(normed, wv_ref[...]).astype(BF16)
-    queries = []
-    for half in range(2):
-        tile = rotate_tile(projected[:, half * LANES : (half + 1) * LANES], cosine, sine) * ATTN_SCALE
-        turned = pltpu.roll(tile, HD, 1)
-        if half == 0:
-            first, second = jnp.where(low, tile, 0.0), jnp.where(low, turned, 0.0)
-        else:
-            first, second = jnp.where(low, 0.0, turned), jnp.where(low, 0.0, tile)
-        queries.append(jnp.concatenate([first, second], axis=0).astype(BF16))
-        q_ref[half] = queries[half]
-    key_tiles = [suffix_keys] + [ref[...] for ref in key_refs]
-    value_tiles = [suffix_values] + [ref[...] for ref in value_refs]
-    results = attend_pair(queries, key_tiles, value_tiles, suffix_len, None)
-    for half, (new_max, total) in enumerate(results):
-        max_ref[half] = new_max
-        acc_ref[half] = total
-
-
-def pair_spec(*shape):
-    return pl.BlockSpec((2, *shape), lambda i: (i, 0, 0))
+    low = lane_index(cosine.shape) < HD
+    queries, key_tiles, value_tiles = [], [], []
+    for pair in range(KV // 2):
+        lanes = slice(pair * LANES, (pair + 1) * LANES)
+        suffix_keys = rotate_tile(dot(normed, held[1][:, lanes]), cosine, sine).astype(BF16)
+        suffix_values = dot(normed, held[2][:, lanes]).astype(BF16)
+        key_tiles.append([suffix_keys, keys_ref[:, lanes], mate_keys_ref[:, lanes]])
+        value_tiles.append([suffix_values, values_ref[:, lanes], mate_values_ref[:, lanes]])
+        projected = dot(normed, held[0][:, 2 * pair * LANES : 2 * (pair + 1) * LANES])
+        for half in range(2):
+            tile = rotate_tile(projected[:, half * LANES : (half + 1) * LANES], cosine, sine) * ATTN_SCALE
+            turned = pltpu.roll(tile, HD, 1)
+            if half == 0:
+                first, second = jnp.where(low, tile, 0.0), jnp.where(low, turned, 0.0)
+            else:
+                first, second = jnp.where(low, 0.0, turned), jnp.where(low, 0.0, tile)
+            queries.append(jnp.concatenate([first, second], axis=0).astype(BF16))
+            q_ref[2 * pair + half] = queries[-1]
+    results = attend_heads(queries, key_tiles, value_tiles, suffix_len, None)
+    for head, (new_max, total) in enumerate(results):
+        max_ref[head] = new_max
+        acc_ref[head] = total
 
 
 def whole_spec(*shape):
@@ -313,7 +316,7 @@
             stacked = not isinstance(array, tuple)
             length = array.shape[0] // 2 if stacked else array[0].shape[0]
             place = kind if stacked else 0
-            specs.append(pl.BlockSpec((length, LANES), lambda i, place=place: (place, i)))
+            specs.append(pl.BlockSpec((length, KV * HD), lambda i, place=place: (place, 0)))
     return specs
 
 
@@ -323,41 +326,32 @@
 
 def attend_near(own_rows, attn_gain, w_query, w_key, w_value, prefix_len, lengths, assignment, keys, values, mate):
     tok_count, width = own_rows.shape
-    cached = [(keys, values), mate]
-    rows, blocks = 2 * tok_count, len(cached)
+    rows, block = 2 * tok_count, keys.shape[0]
     cosine, sine = rope_tables(prefix_len, tok_count)
-    column = lambda i: (0, i)
+    smem = pl.BlockSpec(memory_space=pltpu.SMEM)
+    mate_specs = [pl.BlockSpec((block, KV * HD), lambda i, kind=kind: (kind, 0)) for kind in range(2)]
     queries, *state = pl.pallas_call(
-        functools.partial(near_kernel, blocks),
-        grid=(KV // 2,),
-        in_specs=[
-            whole_spec(tok_count, width),
-            whole_spec(1, width),
-            pl.BlockSpec((width, 2 * LANES), column),
-            pl.BlockSpec((width, LANES), column),
-            pl.BlockSpec((width, LANES), column),
-            whole_spec(tok_count, LANES),
-            whole_spec(tok_count, LANES),
-            pl.BlockSpec(memory_space=pltpu.SMEM),
-            pl.BlockSpec(memory_space=pltpu.SMEM),
-        ]
-        + cached_specs(cached),
-        out_specs=[pair_spec(rows, LANES), pair_spec(1, rows), pair_spec(HD + SUM_ROWS, rows)],
+        near_kernel,
+        grid=(1,),
+        in_specs=[whole_spec(tok_count, width), whole_spec(1, width)]
+        + [whole_spec(*array.shape) for array in (w_query, w_key, w_value)]
+        + [whole_spec(tok_count, LANES)] * 2
+        + [smem, smem]
+        + [whole_spec(block, KV * HD)] * 2
+        + mate_specs,
+        out_specs=[whole_spec(KV, rows, LANES), whole_spec(KV, 1, rows), whole_spec(KV, HD + SUM_ROWS, rows)],
         out_shape=[
             pltpu.VMEM((KV, rows, LANES), BF16),
             pltpu.VMEM((KV, 1, rows), F32),
             pltpu.VMEM((KV, HD + SUM_ROWS, rows), F32),
         ],
-        scratch_shapes=[pltpu.VMEM((tok_count, width), BF16)],
         compiler_params=pltpu.CompilerParams(vmem_limit_bytes=VMEM_ATTEND * MIB),
         cost_estimate=pl.CostEstimate(flops=4000 * MIB, bytes_accessed=6 * MIB, transcendentals=0),
         name="attend_near",
     )(
         *held_in_hbm([own_rows, attn_gain.reshape(1, width), w_query, w_key, w_value, cosine, sine]),
-        *held_in_hbm([lengths, assignment, keys]),
-        held_in_vmem([mate])[0],
-        *held_in_hbm([values]),
-        held_in_vmem([mate])[0],
+        *held_in_hbm([lengths, assignment, keys, values]),
+        *held_in_vmem([mate, mate]),
     )
     return queries, state
 
@@ -366,90 +360,77 @@
     q_ref, max_in, acc_in = refs[:3]
     key_refs, value_refs = refs[3 : 3 + blocks], refs[3 + blocks : 3 + 2 * blocks]
     refs = refs[3 + 2 * blocks :]
-    states = [(max_in[half], acc_in[half]) for half in range(2)]
-    key_tiles = [ref[...] for ref in key_refs]
-    value_tiles = [ref[...] for ref in value_refs]
-    results = attend_pair([q_ref[0], q_ref[1]], key_tiles, value_tiles, None, states)
+    heads = q_ref.shape[0]
+    states = [(max_in[head], acc_in[head]) for head in range(heads)]
+    queries = [q_ref[head] for head in range(heads)]
+    results = attend_heads(queries, pair_tiles(key_refs), pair_tiles(value_refs), None, states)
     if not last:
         max_ref, acc_ref = refs
         for half, (new_max, total) in enumerate(results):
             max_ref[half] = new_max
             acc_ref[half] = total
         return
-    tok_ref, w_out_ref, gain_ref, ids_ref, route_ref, ctx_ref, hidden_ref, moe_ref, projected_ref = refs
+    tok_ref, w_out_ref, gain_ref, ids_ref, route_ref, ctx_ref, hidden_ref, moe_ref = refs
     tok_count = tok_ref.shape[0]
-    step = pl.program_id(0)
     tiles = []
     for _, total in results:
         mixed = total[:HD] / total[HD : HD + 1]
         tiles.append(jnp.concatenate([mixed[:, :tok_count], mixed[:, tok_count:]], axis=0).T)
     context = jnp.concatenate(tiles, axis=1).astype(BF16)
     ctx_ref[...] = context
-    part = dot(context, w_out_ref[...])
-
-    @pl.when(step == 0)
-    def _():
-        projected_ref[...] = part
-
-    @pl.when(step > 0)
-    def _():
-        projected_ref[...] += part
-
-    @pl.when(step == pl.num_programs(0) - 1)
-    def _():
-        hidden = (tok_ref[...].astype(F32) + RESIDUAL_SCALE * projected_ref[...]).astype(BF16)
-        hidden_ref[...] = hidden
-        wide = hidden.astype(F32)
-        mean_square = jnp.mean(wide * wide, axis=-1, keepdims=True)
-        moe_ref[:tok_count] = (wide * lax.rsqrt(mean_square + NORM_EPS) * gain_ref[...]).astype(BF16)
-        moe_ref[tok_count:] = jnp.zeros((NOTE_ROWS, wide.shape[1]), BF16)
-        moe_ref[tok_count : tok_count + TOP, :tok_count] = ids_ref[...].astype(F32).astype(BF16)
-        moe_ref[tok_count : tok_count + TOP, tok_count : 2 * tok_count] = route_ref[...].astype(BF16)
+    projected = dot(context, w_out_ref[...])
+    hidden = (tok_ref[...].astype(F32) + RESIDUAL_SCALE * projected).astype(BF16)
+    hidden_ref[...] = hidden
+    wide = hidden.astype(F32)
+    mean_square = jnp.mean(wide * wide, axis=-1, keepdims=True)
+    moe_ref[:tok_count] = (wide * lax.rsqrt(mean_square + NORM_EPS) * gain_ref[...]).astype(BF16)
+    moe_ref[tok_count:] = jnp.zeros((NOTE_ROWS, wide.shape[1]), BF16)
+    moe_ref[tok_count : tok_count + TOP, :tok_count] = ids_ref[...].astype(F32).astype(BF16)
+    moe_ref[tok_count : tok_count + TOP, tok_count : 2 * tok_count] = route_ref[...].astype(BF16)
 
 
 def attend_far(queries, state, cached, final=None):
     last, blocks, rows = final is not None, len(cached), queries.shape[1]
     tok_count = rows // 2
     args, tiles = [queries, *state], held_in_vmem(cached_args(cached))
-    in_specs = [pair_spec(rows, LANES), pair_spec(1, rows), pair_spec(HD + SUM_ROWS, rows)]
+    in_specs = [whole_spec(KV, rows, LANES), whole_spec(KV, 1, rows), whole_spec(KV, HD + SUM_ROWS, rows)]
     in_specs += cached_specs(cached)
     if last:
         own_rows, w_out, moe_gain, expert_ids, route_weights = final
         width = own_rows.shape[1]
         own_args = [own_rows, w_out, moe_gain.reshape(1, width), expert_ids.T, route_weights.T]
         whole = whole_spec(tok_count, width)
-        in_specs += [whole, pl.BlockSpec((2 * LANES, width), lambda i: (i, 0)), whole_spec(1, width)]
+        in_specs += [whole, whole_spec(*w_out.shape), whole_spec(1, width)]
         in_specs += [whole_spec(TOP, tok_count)] * 2
-        out_specs = [pl.BlockSpec((tok_count, 2 * LANES), lambda i: (0, i)), whole, whole_spec(tok_count + NOTE_ROWS, width)]
+        out_specs = [whole, whole, whole_spec(tok_count + NOTE_ROWS, width)]
         out_shape = [pltpu.HBM((tok_count, width), BF16)] * 2 + [pltpu.VMEM((tok_count + NOTE_ROWS, width), BF16)]
-        scratch = [pltpu.VMEM((tok_count, width), F32)]
     else:
         own_args = []
         out_specs = in_specs[1:3]
         out_shape = [pltpu.VMEM(array.shape, F32) for array in state]
-        scratch = []
     return pl.pallas_call(
         functools.partial(far_kernel, blocks, last),
-        grid=(KV // 2,),
+        grid=(1,),
         in_specs=in_specs,
         out_specs=out_specs,
         out_shape=out_shape,
-        scratch_shapes=scratch,
         compiler_params=pltpu.CompilerParams(vmem_limit_bytes=VMEM_ATTEND * MIB),
         cost_estimate=pl.CostEstimate(flops=blocks * 1200 * MIB, bytes_accessed=4 * MIB, transcendentals=0),
         name="attend_far",
     )(*held_in_vmem(args), *tiles, *held_in_hbm(own_args))
 
 
-def experts_kernel(sources, pieces, *refs):
+def experts_kernel(sources, pieces, load, *refs):
     refs = list(refs)
     take = lambda n: [refs.pop(0) for _ in range(n)]
     row_refs = [take(pieces) for _ in range(sources)]
-    weight_refs = [take(2) for _ in range(3)]
+    weight_refs = [take(2) for _ in range(3)] if load else None
+    held = None if load else take(3)
     out_refs = take(sources)
-    picked_ref, made_ref, combine_ref, *held, sem = refs
-    local_experts = weight_refs[0][0].shape[0]
-    chip_experts = 2 * local_experts
+    held = take(3) if load else held
+    picked_ref, made_ref, combine_ref, *sems = refs
+    chip_experts = held[0].shape[0]
+    local_experts = chip_experts // 2
     tok_count, width = out_refs[0].shape
     slots = chip_experts * CAP
     me = lax.axis_index("req")
@@ -457,10 +438,10 @@
 
     def copy(kind, owner, e, expert):
         return pltpu.make_async_copy(
-            weight_refs[kind][owner].at[e], held[kind].at[expert], sem.at[kind, expert]
+            weight_refs[kind][owner].at[e], held[kind].at[expert], sems[0].at[kind, expert]
         )
 
-    for expert in range(chip_experts):
+    for expert in range(chip_experts if load else 0):
         for kind in range(3):
             copy(kind, expert // local_experts, expert % local_experts, expert).start()
 
@@ -490,7 +471,7 @@
             picked_ref[e, source] = picked[e * CAP : (e + 1) * CAP]
 
     def one_expert(expert, carry):
-        for kind in range(3):
+        for kind in range(3 if load else 0):
             copy(kind, 0, 0, expert).wait()
         rows = picked_ref[expert].reshape(sources * CAP, width)
         gate = dot(rows, held[0][expert])
@@ -508,33 +489,35 @@
         ref[...] = dot_tn(combine_ref[source], made_ref[source]).astype(ref.dtype)
 
 
-def run_experts(rows, weights, out_type=BF16):
+def run_experts(rows, weights, load=False, out_type=BF16):
     sources, pieces = len(rows), len(rows[0])
     tok_count, width = sum(piece.shape[0] for piece in rows[0]) - NOTE_ROWS, rows[0][0].shape[1]
-    chip_experts = 2 * weights[0][0].shape[0]
-    hidden = weights[0][0].shape[2]
     vmem = pl.BlockSpec(memory_space=pltpu.VMEM)
+    out_shape = [pltpu.VMEM((tok_count, width), out_type)] * sources
+    if load:
+        chip_experts = 2 * weights[0][0].shape[0]
+        out_shape = out_shape + [pltpu.VMEM((chip_experts, *own.shape[1:]), BF16) for own, _ in weights]
+        weight_args = [array for pair in weights for array in pair]
+        weight_specs = [pl.BlockSpec(memory_space=pl.ANY)] * 6
+        semaphores = [pltpu.SemaphoreType.DMA((3, chip_experts))]
+    else:
+        chip_experts = weights[0].shape[0]
+        weight_args, weight_specs, semaphores = held_in_vmem(weights), [vmem] * 3, []
     return pl.pallas_call(
-        functools.partial(experts_kernel, sources, pieces),
-        in_specs=[vmem] * (pieces * sources) + [pl.BlockSpec(memory_space=pl.ANY)] * 6,
-        out_specs=[vmem] * sources,
-        out_shape=[pltpu.VMEM((tok_count, width), out_type)] * sources,
+        functools.partial(experts_kernel, sources, pieces, load),
+        in_specs=[vmem] * (pieces * sources) + weight_specs,
+        out_specs=[vmem] * len(out_shape),
+        out_shape=out_shape,
         scratch_shapes=[
             pltpu.VMEM((chip_experts, sources, CAP, width), BF16),
             pltpu.VMEM((sources, chip_experts * CAP, width), BF16),
             pltpu.VMEM((sources, chip_experts * CAP, tok_count), BF16),
-            pltpu.VMEM((chip_experts, width, hidden), BF16),
-            pltpu.VMEM((chip_experts, width, hidden), BF16),
-            pltpu.VMEM((chip_experts, hidden, width), BF16),
-            pltpu.SemaphoreType.DMA((3, chip_experts)),
+            *semaphores,
         ],
         compiler_params=pltpu.CompilerParams(vmem_limit_bytes=VMEM_EXPERTS * MIB),
         cost_estimate=pl.CostEstimate(flops=12000 * MIB, bytes_accessed=30 * MIB, transcendentals=0),
         name="experts",
-    )(
-        *held_in_vmem([piece for source in rows for piece in source]),
-        *[array for pair in weights for array in pair],
-    )
+    )(*held_in_vmem([piece for source in rows for piece in source]), *weight_args)
 
 
 CORE, ACROSS_X, ACROSS_Y = 1, 2, 4
@@ -599,7 +582,7 @@
     weights = (gate, up, down)
     half = tok_count // 2
     rows_x, rows_y = swap(moe_in, ACROSS_X), swap(moe_in, ACROSS_Y)
-    (own,) = run_experts([[moe_in]], weights, F32)
+    own, *weights = run_experts([[moe_in]], weights, load=True, out_type=F32)
     rows_x, rows_y, own = ordered(rows_x, rows_y, own)
     low_xy, high_xy = swap(rows_x[:half], ACROSS_Y), swap(rows_y[half:], ACROSS_X)
     to_x, to_y = run_experts([[rows_x], [rows_y]], weights)

time: 98.2 us -> 95.1 us (0.968)
  Pallas kernels: 56.7 us -> 47.7 us
  waiting for transfers between devices: 23.1 us -> 30.2 us
  starting transfers between devices: 15.2 us -> 13.9 us
    pallas_call x6, Pallas kernels: 56.7 us -> 47.7 us  [the longest x3 26.9 us: run_experts(): pl.pallas_call(functools.partial(experts_kernel, sources, pieces, load),...]
    ppermute x19, waiting for transfers between devices: 23.1 us -> 30.2 us  [swap(): lax.ppermute(array, 'req', [(i, i ^ mask) for i in range(lax.axis_size('r...]
    ppermute x19, starting transfers between devices: 15.2 us -> 13.9 us  [swap(): lax.ppermute(array, 'req', [(i, i ^ mask) for i in range(lax.axis_size('r...]
  transfers between devices with their start and end apart: 19 -> 19, of which waited for: 12 -> 12; matrix products, arithmetic and copies ran while one was open for 0% -> 0% of each run, Pallas kernels for 58% -> 50%
where the time goes in v4:
time: 95.1 us; the launch traced here: 94.9 us
  Pallas kernels  47.7 us (50%)
  waiting for transfers between devices  30.2 us (32%)
  starting transfers between devices  13.9 us (15%)
  other arithmetic  2.24 us (2%)
    ppermute x19, waiting for transfers between devices, swap(): lax.ppermute(array, 'req', [(i, i ^ mask) for i in range(lax.axis_size('r...  30.2 us
    pallas_call x3, Pallas kernels, run_experts(): pl.pallas_call(functools.partial(experts_kernel, sources, pieces, load),...  26.9 us
    ppermute x19, starting transfers between devices, swap(): lax.ppermute(array, 'req', [(i, i ^ mask) for i in range(lax.axis_size('r...  13.9 us
    pallas_call x2, Pallas kernels, attend_far(): pl.pallas_call(functools.partial(far_kernel, blocks, last), grid=(1,), in...  12.2 us
    pallas_call x1, Pallas kernels, attend_near(): pl.pallas_call(near_kernel, grid=(1,), in_specs=[whole_spec(tok_count, wi...  8.63 us
  transfers between devices with their start and end apart: 19, of which 12 were waited for; matrix products, arithmetic and copies ran while one was open for 0% of the time, Pallas kernels for 50%

profile of v4, /device:TPU:0, one launch (start us, length us, event | category | flops | bytes accessed | tf_op | source)
XLA Modules:
  0.0 94.9 jit_solution(7669676321051203024)
XLA Ops:
  0.6 1.1 %pad_maximum_fusion = bf16[512,512]{1,0:T(8,128)(2,1)S(1)} fusion(bf16[256,512]{1,0:T(8,128)(2,1)} %bitcast.17, bf16[256,512]{1,0:T(8,128)(2,1)} %bitcast.15), kind=kLoop, calls=%fused_computation.3 | loop fusion | flops 1048576 | bytes 1048576 | tf_op jit(solution)/shard_map/concatenate | solution.py:558
  1.7 0.5 collective-permute-start
  2.2 2.6 %collective-permute-start.1 = (bf16[512,512]{1,0:T(8,128)(2,1)S(1)}, bf16[512,512]{1,0:T(8,128)(2,1)S(1)}, u32[]{:S(2)}, u32[]{:S(2)}) collective-permute-start(bf16[512,512]{1,0:T(8,128)(2,1)S(1)} %pad_maximum_fusion), channel_id=1, source_target_pairs={{0,2},{1,3},{2,0},{3,1},{4,6},{5,7},{6,4},{7,5},{8,10},{9,11},{10,... | collective-permute-start | bytes 1572872 | tf_op jit(solution)/shard_map/ppermute | solution.py:527
  4.8 1.5 %collective-permute-start.2 = (bf16[512,512]{1,0:T(8,128)(2,1)S(1)}, bf16[512,512]{1,0:T(8,128)(2,1)S(1)}, u32[]{:S(2)}, u32[]{:S(2)}) collective-permute-start(bf16[512,512]{1,0:T(8,128)(2,1)S(1)} %pad_maximum_fusion), channel_id=1, source_target_pairs={{0,4},{1,5},{2,6},{3,7},{4,0},{5,1},{6,2},{7,3},{8,12},{9,13},{10,... | collective-permute-start | bytes 1572872 | tf_op jit(solution)/shard_map/ppermute | solution.py:527
  6.3 8.6 %attend_near.1 = (bf16[8,512,128]{2,1,0:T(8,128)(2,1)S(1)}, f32[8,1,512]{2,1,0:T(1,128)S(1)}, f32[8,80,512]{2,1,0:T(8,128)S(1)}) custom-call(bf16[256,1024]{1,0:T(8,128)(2,1)} %bitcast.19, f32[1,1024]{1,0:T(1,128)} %bitcast.23, bf16[1024,1024]{1,0:T(8,128)(2,1)} %refs_2_.1, bf16[1024,512]{1,0:T(8,128)(2,1)} %refs_3_.1, bf16[1024,512]{1,0:T(8,128)(2,1)} %refs_4_.1, ...), custom_call_target="tpu_custom_call" | custom-call | flops 4194304000 | bytes 6291456 | tf_op jit(solution)/shard_map/attend_near/pallas_call | solution.py:333
  14.9 2.4 %collective-permute-done.1.refs_3_.refs_7_ = bf16[512,512]{1,0:T(8,128)(2,1)S(1)} collective-permute-done((bf16[512,512]{1,0:T(8,128)(2,1)S(1)}, bf16[512,512]{1,0:T(8,128)(2,1)S(1)}, u32[]{:S(2)}, u32[]{:S(2)}) %collective-permute-start.1) | collective-permute-done | bytes 524320 | tf_op jit(solution)/shard_map/ppermute | solution.py:527
  17.3 1.5 %collective-permute-done.2.refs_4_.refs_8_ = bf16[512,512]{1,0:T(8,128)(2,1)S(1)} collective-permute-done((bf16[512,512]{1,0:T(8,128)(2,1)S(1)}, bf16[512,512]{1,0:T(8,128)(2,1)S(1)}, u32[]{:S(2)}, u32[]{:S(2)}) %collective-permute-start.2) | collective-permute-done | bytes 524320 | tf_op jit(solution)/shard_map/ppermute | solution.py:527
  18.8 0.5 collective-permute-start.6
  19.3 1.4 %collective-permute-done.5.refs_5_.refs_9_ = bf16[512,512]{1,0:T(8,128)(2,1)S(1)} collective-permute-done((bf16[512,512]{1,0:T(8,128)(2,1)S(1)}, bf16[512,512]{1,0:T(8,128)(2,1)S(1)}, u32[]{:S(2)}, u32[]{:S(2)}) %collective-permute-start.5) | collective-permute-done | bytes 524320 | tf_op jit(solution)/shard_map/ppermute | solution.py:527
  20.7 0.7 collective-permute-done.6.refs_6_.refs_10_
  21.6 1.6 %collective-permute-start.3 = (bf16[256,512]{1,0:T(8,128)(2,1)S(1)}, bf16[256,512]{1,0:T(8,128)(2,1)S(1)}, u32[]{:S(2)}, u32[]{:S(2)}) collective-permute-start(bf16[256,512]{1,0:T(8,128)(2,1)S(1)} %slice.12), channel_id=1, source_target_pairs={{0,4},{1,5},{2,6},{3,7},{4,0},{5,1},{6,2},{7,3},{8,12},{9,13},{10,... | collective-permute-start | bytes 786440 | tf_op jit(solution)/shard_map/ppermute | solution.py:527
  23.2 0.5 collective-permute-start.4
  23.8 5.9 %attend_far.2 = (f32[8,1,512]{2,1,0:T(1,128)S(1)}, f32[8,80,512]{2,1,0:T(8,128)S(1)}) custom-call(bf16[8,512,128]{2,1,0:T(8,128)(2,1)S(1)} %get-tuple-element.43.refs_0_, f32[8,1,512]{2,1,0:T(1,128)S(1)} %get-tuple-element.49.refs_1_, f32[8,80,512]{2,1,0:T(8,128)S(1)} %get-tuple-element.50.refs_2_, ...), custom_call_target="tpu_custom_call" | custom-call | flops 5033164800 | bytes 4194304 | tf_op jit(solution)/shard_map/attend_far/pallas_call | solution.py:411
  29.7 0.6 collective-permute-done.3.refs_3_
  30.3 1.2 %collective-permute-done.4.refs_5_ = bf16[256,512]{1,0:T(8,128)(2,1)S(1)} collective-permute-done((bf16[256,512]{1,0:T(8,128)(2,1)S(1)}, bf16[256,512]{1,0:T(8,128)(2,1)S(1)}, u32[]{:S(2)}, u32[]{:S(2)}) %collective-permute-start.4) | collective-permute-done | bytes 262176 | tf_op jit(solution)/shard_map/ppermute | solution.py:527
  31.5 0.5 collective-permute-start.9
  32.0 1.0 %collective-permute-done.8.refs_4_ = bf16[256,512]{1,0:T(8,128)(2,1)S(1)} collective-permute-done((bf16[256,512]{1,0:T(8,128)(2,1)S(1)}, bf16[256,512]{1,0:T(8,128)(2,1)S(1)}, u32[]{:S(2)}, u32[]{:S(2)}) %collective-permute-start.8) | collective-permute-done | bytes 262176 | tf_op jit(solution)/shard_map/ppermute | solution.py:527
  33.9 6.3 %attend_far.3 = (bf16[256,1024]{1,0:T(8,128)(2,1)}, bf16[256,1024]{1,0:T(8,128)(2,1)}, bf16[272,1024]{1,0:T(8,128)(2,1)S(1)}) custom-call(bf16[8,512,128]{2,1,0:T(8,128)(2,1)S(1)} %get-tuple-element.43.refs_0_, f32[8,1,512]{2,1,0:T(1,128)S(1)} %get-tuple-element.55.refs_1_, f32[8,80,512]{2,1,0:T(8,128)S(1)} %get-tuple-element.56.refs_2_, ...), custom_call_target="tpu_custom_call" | custom-call | flops 2516582400 | bytes 4194304 | tf_op jit(solution)/shard_map/attend_far/pallas_call | solution.py:411
  40.2 0.5 collective-permute-start.10
  41.1 4.2 %collective-permute-done.12.refs_4_ = bf16[4,1024,512]{2,1,0:T(8,128)(2,1)} collective-permute-done((bf16[4,1024,512]{2,1,0:T(8,128)(2,1)S(1)}, bf16[4,1024,512]{2,1,0:T(8,128)(2,1)}, u32[]{:S(2)}, u32[]{:S(2)}) %collective-permute-start.12) | collective-permute-done | bytes 4194336 | tf_op jit(solution)/shard_map/ppermute | solution.py:527
  45.4 1.6 %collective-permute-done.13.refs_6_ = bf16[4,512,1024]{2,1,0:T(8,128)(2,1)} collective-permute-done((bf16[4,512,1024]{2,1,0:T(8,128)(2,1)}, bf16[4,512,1024]{2,1,0:T(8,128)(2,1)}, u32[]{:S(2)}, u32[]{:S(2)}) %collective-permute-start.13) | collective-permute-done | bytes 4194336 | tf_op jit(solution)/shard_map/ppermute | solution.py:527
  46.9 9.8 %experts.3 = (f32[256,1024]{1,0:T(8,128)S(1)}, bf16[8,1024,512]{2,1,0:T(8,128)(2,1)S(1)}, bf16[8,1024,512]{2,1,0:T(8,128)(2,1)S(1)}, bf16[8,512,1024]{2,1,0:T(8,128)(2,1)S(1)}) custom-call(bf16[272,1024]{1,0:T(8,128)(2,1)S(1)} %get-tuple-element.63.refs_0_, bf16[4,1024,512]{2,1,0:T(8,128)(2,1)} %refs_1_, ...), custom_call_target="tpu_custom_call" | custom-call | flops 12582912000 | bytes 31457280 | tf_op jit(solution)/shard_map/experts/pallas_call | solution.py:506
  56.8 0.6 collective-permute-start.15
  57.4 0.4 collective-permute-start.14
  57.9 9.7 %experts.4 = (bf16[256,1024]{1,0:T(8,128)(2,1)S(1)}, bf16[256,1024]{1,0:T(8,128)(2,1)S(1)}) custom-call(bf16[272,1024]{1,0:T(8,128)(2,1)S(1)} %collective-permute-done.10.refs_0_, bf16[272,1024]{1,0:T(8,128)(2,1)S(1)} %collective-permute-done.11.refs_1_, bf16[8,1024,512]{2,1,0:T(8,128)(2,1)S(1)} %get-tuple-element.72.refs_2_, ...), custom_call_target="tpu_custom_call" | custom-call | flops 12582912000 | bytes 31457280 | tf_op jit(solution)/shard_map/experts/pallas_call | solution.py:506
  67.7 1.7 %collective-permute-start.16 = (bf16[256,1024]{1,0:T(8,128)(2,1)S(1)}, bf16[256,1024]{1,0:T(8,128)(2,1)S(1)}, u32[]{:S(2)}, u32[]{:S(2)}) collective-permute-start(bf16[256,1024]{1,0:T(8,128)(2,1)S(1)} %get-tuple-element.77), channel_id=1, source_target_pairs={{0,2},{1,3},{2,0},{3,1},{4,6},{5,7},{6,4},{7,5},{8,10},{9,11},{10,... | collective-permute-start | bytes 1572872 | tf_op jit(solution)/shard_map/ppermute | solution.py:527
  69.4 1.5 %collective-permute-start.17 = (bf16[256,1024]{1,0:T(8,128)(2,1)S(1)}, bf16[256,1024]{1,0:T(8,128)(2,1)S(1)}, u32[]{:S(2)}, u32[]{:S(2)}) collective-permute-start(bf16[256,1024]{1,0:T(8,128)(2,1)S(1)} %get-tuple-element.78), channel_id=1, source_target_pairs={{0,4},{1,5},{2,6},{3,7},{4,0},{5,1},{6,2},{7,3},{8,12},{9,13},{10,... | collective-permute-start | bytes 1572872 | tf_op jit(solution)/shard_map/ppermute | solution.py:527
  70.9 7.3 %experts.5 = bf16[256,1024]{1,0:T(8,128)(2,1)S(1)} custom-call(bf16[128,1024]{1,0:T(8,128)(2,1)S(1)} %collective-permute-done.14.refs_0_, bf16[144,1024]{1,0:T(8,128)(2,1)S(1)} %collective-permute-done.15.refs_1_, bf16[8,1024,512]{2,1,0:T(8,128)(2,1)S(1)} %get-tuple-element.72.refs_2_, bf16[8,1024,512]{2,1,0:T(8,128)(2,1)S(1)} %get-tuple-element.73.refs_3_, ...), custom_call_target="tpu_custom_call" | custom-call | flops 12582912000 | bytes 31457280 | tf_op jit(solution)/shard_map/experts/pallas_call | solution.py:506
  78.2 0.4 collective-permute-start.18
  78.6 3.8 %collective-permute-done.16 = bf16[256,1024]{1,0:T(8,128)(2,1)S(1)} collective-permute-done((bf16[256,1024]{1,0:T(8,128)(2,1)S(1)}, bf16[256,1024]{1,0:T(8,128)(2,1)S(1)}, u32[]{:S(2)}, u32[]{:S(2)}) %collective-permute-start.16) | collective-permute-done | bytes 524320 | tf_op jit(solution)/shard_map/ppermute | solution.py:527
  82.4 11.4 %collective-permute-done.17 = bf16[256,1024]{1,0:T(8,128)(2,1)S(1)} collective-permute-done((bf16[256,1024]{1,0:T(8,128)(2,1)S(1)}, bf16[256,1024]{1,0:T(8,128)(2,1)S(1)}, u32[]{:S(2)}, u32[]{:S(2)}) %collective-permute-start.17) | collective-permute-done | bytes 524320 | tf_op jit(solution)/shard_map/ppermute | solution.py:527
  94.0 0.9 fusion
  (23 shorter events, 1.7 us)
Async XLA Ops:
  1.7 4.6 %collective-permute-start = (bf16[512,512]{1,0:T(8,128)(2,1)S(1)}, bf16[512,512]{1,0:T(8,128)(2,1)S(1)}, u32[]{:S(2)}, u32[]{:S(2)}) collective-permute-start(bf16[512,512]{1,0:T(8,128)(2,1)S(1)} %pad_maximum_fusion), channel_id=1, source_target_pairs={{0,1},{1,0},{2,3},{3,2},{4,5},{5,4},{6,7},{7,6},{8,9},{9,8},{10,11... | collective-permute-start | bytes 1572872 | tf_op jit(solution)/shard_map/ppermute | solution.py:527
  2.2 15.1 %collective-permute-start.1 = (bf16[512,512]{1,0:T(8,128)(2,1)S(1)}, bf16[512,512]{1,0:T(8,128)(2,1)S(1)}, u32[]{:S(2)}, u32[]{:S(2)}) collective-permute-start(bf16[512,512]{1,0:T(8,128)(2,1)S(1)} %pad_maximum_fusion), channel_id=1, source_target_pairs={{0,2},{1,3},{2,0},{3,1},{4,6},{5,7},{6,4},{7,5},{8,10},{9,11},{10,... | collective-permute-start | bytes 1572872 | tf_op jit(solution)/shard_map/ppermute | solution.py:527
  4.8 14.0 %collective-permute-start.2 = (bf16[512,512]{1,0:T(8,128)(2,1)S(1)}, bf16[512,512]{1,0:T(8,128)(2,1)S(1)}, u32[]{:S(2)}, u32[]{:S(2)}) collective-permute-start(bf16[512,512]{1,0:T(8,128)(2,1)S(1)} %pad_maximum_fusion), channel_id=1, source_target_pairs={{0,4},{1,5},{2,6},{3,7},{4,0},{5,1},{6,2},{7,3},{8,12},{9,13},{10,... | collective-permute-start | bytes 1572872 | tf_op jit(solution)/shard_map/ppermute | solution.py:527
  6.3 15.1 %copy-start = (bf16[4,1024,512]{2,1,0:T(8,128)(2,1)S(1)}, bf16[4,1024,512]{2,1,0:T(8,128)(2,1)}, u32[]{:S(2)}) copy-start(bf16[4,1024,512]{2,1,0:T(8,128)(2,1)} %refs_1_) | copy-start | bytes 12582916
  18.8 1.9 %collective-permute-start.5 = (bf16[512,512]{1,0:T(8,128)(2,1)S(1)}, bf16[512,512]{1,0:T(8,128)(2,1)S(1)}, u32[]{:S(2)}, u32[]{:S(2)}) collective-permute-start(bf16[512,512]{1,0:T(8,128)(2,1)S(1)} %collective-permute-done.1.refs_3_.refs_7_), channel_id=1, source_target_pairs={{0,1},{1,0},{2,3},{3,2},{4,5},{5,4},{6,7},{7,6},{8,9},{9,8},{10,11... | collective-permute-start | bytes 1572872 | tf_op jit(solution)/shard_map/ppermute | solution.py:527
  18.8 2.7 %collective-permute-start.6 = (bf16[512,512]{1,0:T(8,128)(2,1)S(1)}, bf16[512,512]{1,0:T(8,128)(2,1)S(1)}, u32[]{:S(2)}, u32[]{:S(2)}) collective-permute-start(bf16[512,512]{1,0:T(8,128)(2,1)S(1)} %collective-permute-done.2.refs_4_.refs_8_), channel_id=1, source_target_pairs={{0,1},{1,0},{2,3},{3,2},{4,5},{5,4},{6,7},{7,6},{8,9},{9,8},{10,11... | collective-permute-start | bytes 1572872 | tf_op jit(solution)/shard_map/ppermute | solution.py:527
  21.4 10.1 %collective-permute-start.7 = (bf16[4,1024,512]{2,1,0:T(8,128)(2,1)S(1)}, bf16[4,1024,512]{2,1,0:T(8,128)(2,1)}, u32[]{:S(2)}, u32[]{:S(2)}) collective-permute-start(bf16[4,1024,512]{2,1,0:T(8,128)(2,1)S(1)} %copy-done), channel_id=1, source_target_pairs={{0,1},{1,0},{2,3},{3,2},{4,5},{5,4},{6,7},{7,6},{8,9},{9,8},{10,11... | collective-permute-start | bytes 12582920 | tf_op jit(solution)/shard_map/ppermute | solution.py:527
  21.6 8.7 %collective-permute-start.3 = (bf16[256,512]{1,0:T(8,128)(2,1)S(1)}, bf16[256,512]{1,0:T(8,128)(2,1)S(1)}, u32[]{:S(2)}, u32[]{:S(2)}) collective-permute-start(bf16[256,512]{1,0:T(8,128)(2,1)S(1)} %slice.12), channel_id=1, source_target_pairs={{0,4},{1,5},{2,6},{3,7},{4,0},{5,1},{6,2},{7,3},{8,12},{9,13},{10,... | collective-permute-start | bytes 786440 | tf_op jit(solution)/shard_map/ppermute | solution.py:527
  23.2 8.3 %collective-permute-start.4 = (bf16[256,512]{1,0:T(8,128)(2,1)S(1)}, bf16[256,512]{1,0:T(8,128)(2,1)S(1)}, u32[]{:S(2)}, u32[]{:S(2)}) collective-permute-start(bf16[256,512]{1,0:T(8,128)(2,1)S(1)} %slice.13), channel_id=1, source_target_pairs={{0,2},{1,3},{2,0},{3,1},{4,6},{5,7},{6,4},{7,5},{8,10},{9,11},{10,... | collective-permute-start | bytes 786440 | tf_op jit(solution)/shard_map/ppermute | solution.py:527
  23.8 9.7 %copy-start.1 = (bf16[4,1024,512]{2,1,0:T(8,128)(2,1)S(1)}, bf16[4,1024,512]{2,1,0:T(8,128)(2,1)}, u32[]{:S(2)}) copy-start(bf16[4,1024,512]{2,1,0:T(8,128)(2,1)} %refs_3_.2) | copy-start | bytes 12582916
  31.5 1.5 %collective-permute-start.8 = (bf16[256,512]{1,0:T(8,128)(2,1)S(1)}, bf16[256,512]{1,0:T(8,128)(2,1)S(1)}, u32[]{:S(2)}, u32[]{:S(2)}) collective-permute-start(bf16[256,512]{1,0:T(8,128)(2,1)S(1)} %collective-permute-done.3.refs_3_), channel_id=1, source_target_pairs={{0,1},{1,0},{2,3},{3,2},{4,5},{5,4},{6,7},{7,6},{8,9},{9,8},{10,11... | collective-permute-start | bytes 786440 | tf_op jit(solution)/shard_map/ppermute | solution.py:527
  31.5 1.9 %collective-permute-start.9 = (bf16[256,512]{1,0:T(8,128)(2,1)S(1)}, bf16[256,512]{1,0:T(8,128)(2,1)S(1)}, u32[]{:S(2)}, u32[]{:S(2)}) collective-permute-start(bf16[256,512]{1,0:T(8,128)(2,1)S(1)} %collective-permute-done.4.refs_5_), channel_id=1, source_target_pairs={{0,1},{1,0},{2,3},{3,2},{4,5},{5,4},{6,7},{7,6},{8,9},{9,8},{10,11... | collective-permute-start | bytes 786440 | tf_op jit(solution)/shard_map/ppermute | solution.py:527
  33.4 11.9 %collective-permute-start.12 = (bf16[4,1024,512]{2,1,0:T(8,128)(2,1)S(1)}, bf16[4,1024,512]{2,1,0:T(8,128)(2,1)}, u32[]{:S(2)}, u32[]{:S(2)}) collective-permute-start(bf16[4,1024,512]{2,1,0:T(8,128)(2,1)S(1)} %copy-done.1), channel_id=1, source_target_pairs={{0,1},{1,0},{2,3},{3,2},{4,5},{5,4},{6,7},{7,6},{8,9},{9,8},{10,11... | collective-permute-start | bytes 12582920 | tf_op jit(solution)/shard_map/ppermute | solution.py:527
  33.6 13.4 %collective-permute-start.13 = (bf16[4,512,1024]{2,1,0:T(8,128)(2,1)}, bf16[4,512,1024]{2,1,0:T(8,128)(2,1)}, u32[]{:S(2)}, u32[]{:S(2)}) collective-permute-start(bf16[4,512,1024]{2,1,0:T(8,128)(2,1)} %refs_5_.1), channel_id=1, source_target_pairs={{0,1},{1,0},{2,3},{3,2},{4,5},{5,4},{6,7},{7,6},{8,9},{9,8},{10,11... | collective-permute-start | bytes 12582920 | tf_op jit(solution)/shard_map/ppermute | solution.py:527
  40.2 16.5 %collective-permute-start.10 = (bf16[272,1024]{1,0:T(8,128)(2,1)S(1)}, bf16[272,1024]{1,0:T(8,128)(2,1)S(1)}, u32[]{:S(2)}, u32[]{:S(2)}) collective-permute-start(bf16[272,1024]{1,0:T(8,128)(2,1)S(1)} %get-tuple-element.63.refs_0_), channel_id=1, source_target_pairs={{0,2},{1,3},{2,0},{3,1},{4,6},{5,7},{6,4},{7,5},{8,10},{9,11},{10,... | collective-permute-start | bytes 1671176 | tf_op jit(solution)/shard_map/ppermute | solution.py:527
  40.8 16.0 %collective-permute-start.11 = (bf16[272,1024]{1,0:T(8,128)(2,1)S(1)}, bf16[272,1024]{1,0:T(8,128)(2,1)S(1)}, u32[]{:S(2)}, u32[]{:S(2)}) collective-permute-start(bf16[272,1024]{1,0:T(8,128)(2,1)S(1)} %get-tuple-element.63.refs_0_), channel_id=1, source_target_pairs={{0,4},{1,5},{2,6},{3,7},{4,0},{5,1},{6,2},{7,3},{8,12},{9,13},{10,... | collective-permute-start | bytes 1671176 | tf_op jit(solution)/shard_map/ppermute | solution.py:527
  56.8 10.8 %collective-permute-start.15 = (bf16[144,1024]{1,0:T(8,128)(2,1)S(1)}, bf16[144,1024]{1,0:T(8,128)(2,1)S(1)}, u32[]{:S(2)}, u32[]{:S(2)}) collective-permute-start(bf16[144,1024]{1,0:T(8,128)(2,1)S(1)} %slice.15), channel_id=1, source_target_pairs={{0,2},{1,3},{2,0},{3,1},{4,6},{5,7},{6,4},{7,5},{8,10},{9,11},{10,... | collective-permute-start | bytes 884744 | tf_op jit(solution)/shard_map/ppermute | solution.py:527
  57.4 10.2 %collective-permute-start.14 = (bf16[128,1024]{1,0:T(8,128)(2,1)S(1)}, bf16[128,1024]{1,0:T(8,128)(2,1)S(1)}, u32[]{:S(2)}, u32[]{:S(2)}) collective-permute-start(bf16[128,1024]{1,0:T(8,128)(2,1)S(1)} %slice.14), channel_id=1, source_target_pairs={{0,4},{1,5},{2,6},{3,7},{4,0},{5,1},{6,2},{7,3},{8,12},{9,13},{10,... | collective-permute-start | bytes 786440 | tf_op jit(solution)/shard_map/ppermute | solution.py:527
  67.7 14.7 %collective-permute-start.16 = (bf16[256,1024]{1,0:T(8,128)(2,1)S(1)}, bf16[256,1024]{1,0:T(8,128)(2,1)S(1)}, u32[]{:S(2)}, u32[]{:S(2)}) collective-permute-start(bf16[256,1024]{1,0:T(8,128)(2,1)S(1)} %get-tuple-element.77), channel_id=1, source_target_pairs={{0,2},{1,3},{2,0},{3,1},{4,6},{5,7},{6,4},{7,5},{8,10},{9,11},{10,... | collective-permute-start | bytes 1572872 | tf_op jit(solution)/shard_map/ppermute | solution.py:527
  69.4 24.4 %collective-permute-start.17 = (bf16[256,1024]{1,0:T(8,128)(2,1)S(1)}, bf16[256,1024]{1,0:T(8,128)(2,1)S(1)}, u32[]{:S(2)}, u32[]{:S(2)}) collective-permute-start(bf16[256,1024]{1,0:T(8,128)(2,1)S(1)} %get-tuple-element.78), channel_id=1, source_target_pairs={{0,4},{1,5},{2,6},{3,7},{4,0},{5,1},{6,2},{7,3},{8,12},{9,13},{10,... | collective-permute-start | bytes 1572872 | tf_op jit(solution)/shard_map/ppermute | solution.py:527
  78.2 15.8 %collective-permute-start.18 = (bf16[256,1024]{1,0:T(8,128)(2,1)S(1)}, bf16[256,1024]{1,0:T(8,128)(2,1)S(1)}, u32[]{:S(2)}, u32[]{:S(2)}) collective-permute-start(bf16[256,1024]{1,0:T(8,128)(2,1)S(1)} %experts.5), channel_id=1, source_target_pairs={{0,6},{1,7},{2,4},{3,5},{4,2},{5,3},{6,0},{7,1},{8,14},{9,15},{10,... | collective-permute-start | bytes 1572872 | tf_op jit(solution)/shard_map/ppermute | solution.py:527

commit v5 on v4

--- a/solution.py
+++ b/solution.py
@@ -183,9 +183,11 @@
 BF16 = jnp.bfloat16
 MIB = 1 << 20
 LANES = 128
-VMEM_ATTEND = 48
+VMEM_ATTEND = 54
+VMEM_LAST = 57
+VMEM_NEAR = 54
 NOTE_ROWS = 16
-VMEM_EXPERTS = 30
+VMEM_EXPERTS = 17
 
 
 def dot(lhs, rhs):
@@ -329,7 +331,6 @@
     rows, block = 2 * tok_count, keys.shape[0]
     cosine, sine = rope_tables(prefix_len, tok_count)
     smem = pl.BlockSpec(memory_space=pltpu.SMEM)
-    mate_specs = [pl.BlockSpec((block, KV * HD), lambda i, kind=kind: (kind, 0)) for kind in range(2)]
     queries, *state = pl.pallas_call(
         near_kernel,
         grid=(1,),
@@ -337,21 +338,20 @@
         + [whole_spec(*array.shape) for array in (w_query, w_key, w_value)]
         + [whole_spec(tok_count, LANES)] * 2
         + [smem, smem]
-        + [whole_spec(block, KV * HD)] * 2
-        + mate_specs,
+        + [whole_spec(block, KV * HD)] * 4,
         out_specs=[whole_spec(KV, rows, LANES), whole_spec(KV, 1, rows), whole_spec(KV, HD + SUM_ROWS, rows)],
         out_shape=[
             pltpu.VMEM((KV, rows, LANES), BF16),
             pltpu.VMEM((KV, 1, rows), F32),
             pltpu.VMEM((KV, HD + SUM_ROWS, rows), F32),
         ],
-        compiler_params=pltpu.CompilerParams(vmem_limit_bytes=VMEM_ATTEND * MIB),
+        compiler_params=pltpu.CompilerParams(vmem_limit_bytes=VMEM_NEAR * MIB),
         cost_estimate=pl.CostEstimate(flops=4000 * MIB, bytes_accessed=6 * MIB, transcendentals=0),
         name="attend_near",
     )(
         *held_in_hbm([own_rows, attn_gain.reshape(1, width), w_query, w_key, w_value, cosine, sine]),
         *held_in_hbm([lengths, assignment, keys, values]),
-        *held_in_vmem([mate, mate]),
+        *held_in_vmem(mate),
     )
     return queries, state
 
@@ -414,42 +414,44 @@
         in_specs=in_specs,
         out_specs=out_specs,
         out_shape=out_shape,
-        compiler_params=pltpu.CompilerParams(vmem_limit_bytes=VMEM_ATTEND * MIB),
+        compiler_params=pltpu.CompilerParams(vmem_limit_bytes=(VMEM_LAST if last else VMEM_ATTEND) * MIB),
         cost_estimate=pl.CostEstimate(flops=blocks * 1200 * MIB, bytes_accessed=4 * MIB, transcendentals=0),
         name="attend_far",
     )(*held_in_vmem(args), *tiles, *held_in_hbm(own_args))
 
 
-def experts_kernel(sources, pieces, load, *refs):
+def experts_kernel(sources, pieces, owners, load, *refs):
     refs = list(refs)
     take = lambda n: [refs.pop(0) for _ in range(n)]
     row_refs = [take(pieces) for _ in range(sources)]
-    weight_refs = [take(2) for _ in range(3)] if load else None
-    held = None if load else take(3)
+    weight_refs = [take(3) for _ in owners]
     out_refs = take(sources)
-    held = take(3) if load else held
+    held = [take(3) for _ in owners] if load else weight_refs
     picked_ref, made_ref, combine_ref, *sems = refs
-    chip_experts = held[0].shape[0]
-    local_experts = chip_experts // 2
+    local_experts = held[0][0].shape[0]
+    experts = len(owners) * local_experts
     tok_count, width = out_refs[0].shape
-    slots = chip_experts * CAP
+    slots = experts * CAP
     me = lax.axis_index("req")
-    first_own, first_mate = me * local_experts, (me + 1 - 2 * lax.rem(me, 2)) * local_experts
-
-    def copy(kind, owner, e, expert):
+    firsts = [(me + owner * (1 - 2 * lax.rem(me, 2))) * local_experts for owner in owners]
+
+    def copy(group, kind, e):
         return pltpu.make_async_copy(
-            weight_refs[kind][owner].at[e], held[kind].at[expert], sems[0].at[kind, expert]
+            weight_refs[group][kind].at[e], held[group][kind].at[e], sems[0].at[group, kind, e]
         )
 
-    for expert in range(chip_experts if load else 0):
-        for kind in range(3):
-            copy(kind, expert // local_experts, expert % local_experts, expert).start()
+    for group in range(len(owners) if load else 0):
+        for e in range(local_experts):
+            for kind in range(3):
+                copy(group, kind, e).start()
 
     before = lax.broadcasted_iota(jnp.int32, (tok_count, tok_count), 0)
     after = lane_index((tok_count, tok_count))
     earlier = jnp.where(before < after, 1.0, 0.0).astype(BF16)
     slot = lax.broadcasted_iota(jnp.int32, (slots, EXPERTS), 0) // CAP
-    held_here = jnp.where(slot < local_experts, slot + first_own, slot + (first_mate - local_experts))
+    held_here = slot + firsts[0]
+    if len(owners) > 1:
+        held_here = jnp.where(slot < local_experts, held_here, slot + (firsts[1] - local_experts))
     spread = jnp.where(held_here == lane_index((slots, EXPERTS)), 1.0, 0.0).astype(BF16)
     within = (lax.broadcasted_iota(jnp.int32, (slots, tok_count), 0) % CAP).astype(F32)
     expert_row = lax.broadcasted_iota(jnp.int32, (EXPERTS, tok_count), 0).astype(F32)
@@ -467,51 +469,53 @@
         pick = jnp.where(match, 1.0, 0.0).astype(BF16)
         combine_ref[source] = jnp.where(match, dot(spread, route.astype(BF16)), 0.0).astype(BF16)
         picked = dot(pick, rows).astype(BF16)
-        for e in range(chip_experts):
+        for e in range(experts):
             picked_ref[e, source] = picked[e * CAP : (e + 1) * CAP]
 
-    def one_expert(expert, carry):
+    def one_expert(group, e, carry):
         for kind in range(3 if load else 0):
-            copy(kind, 0, 0, expert).wait()
+            copy(group, kind, e).wait()
+        expert = group * local_experts + e
         rows = picked_ref[expert].reshape(sources * CAP, width)
-        gate = dot(rows, held[0][expert])
-        up = dot(rows, held[1][expert])
+        gate = dot(rows, held[group][0][e])
+        up = dot(rows, held[group][1][e])
         act = (jax.nn.silu(gate) * up).astype(BF16)
-        made = dot(act, held[2][expert]).astype(BF16)
+        made = dot(act, held[group][2][e]).astype(BF16)
         for source in range(sources):
             made_ref[source, pl.ds(pl.multiple_of(expert * CAP, CAP), CAP), :] = made[
                 source * CAP : (source + 1) * CAP
             ]
         return carry
 
-    lax.fori_loop(0, chip_experts, one_expert, 0)
+    for group in range(len(owners)):
+        lax.fori_loop(0, local_experts, functools.partial(one_expert, group), 0)
     for source, ref in enumerate(out_refs):
         ref[...] = dot_tn(combine_ref[source], made_ref[source]).astype(ref.dtype)
 
 
-def run_experts(rows, weights, load=False, out_type=BF16):
+def run_experts(rows, weights, owners=(0, 1), load=False, out_type=BF16):
     sources, pieces = len(rows), len(rows[0])
     tok_count, width = sum(piece.shape[0] for piece in rows[0]) - NOTE_ROWS, rows[0][0].shape[1]
     vmem = pl.BlockSpec(memory_space=pltpu.VMEM)
+    weight_args = [array for owned in weights for array in owned]
+    local_experts = weight_args[0].shape[0]
+    experts = len(owners) * local_experts
     out_shape = [pltpu.VMEM((tok_count, width), out_type)] * sources
     if load:
-        chip_experts = 2 * weights[0][0].shape[0]
-        out_shape = out_shape + [pltpu.VMEM((chip_experts, *own.shape[1:]), BF16) for own, _ in weights]
-        weight_args = [array for pair in weights for array in pair]
-        weight_specs = [pl.BlockSpec(memory_space=pl.ANY)] * 6
-        semaphores = [pltpu.SemaphoreType.DMA((3, chip_experts))]
+        out_shape = out_shape + [pltpu.VMEM(array.shape, BF16) for array in weight_args]
+        weight_args, weight_specs = held_in_hbm(weight_args), [pl.BlockSpec(memory_space=pl.ANY)] * len(weight_args)
+        semaphores = [pltpu.SemaphoreType.DMA((len(owners), 3, local_experts))]
     else:
-        chip_experts = weights[0].shape[0]
-        weight_args, weight_specs, semaphores = held_in_vmem(weights), [vmem] * 3, []
+        weight_args, weight_specs, semaphores = held_in_vmem(weight_args), [vmem] * len(weight_args), []
     return pl.pallas_call(
-        functools.partial(experts_kernel, sources, pieces, load),
+        functools.partial(experts_kernel, sources, pieces, owners, load),
         in_specs=[vmem] * (pieces * sources) + weight_specs,
         out_specs=[vmem] * len(out_shape),
         out_shape=out_shape,
         scratch_shapes=[
-            pltpu.VMEM((chip_experts, sources, CAP, width), BF16),
-            pltpu.VMEM((sources, chip_experts * CAP, width), BF16),
-            pltpu.VMEM((sources, chip_experts * CAP, tok_count), BF16),
+            pltpu.VMEM((experts, sources, CAP, width), BF16),
+            pltpu.VMEM((sources, experts * CAP, width), BF16),
+            pltpu.VMEM((sources, experts * CAP, tok_count), BF16),
             *semaphores,
         ],
         compiler_params=pltpu.CompilerParams(vmem_limit_bytes=VMEM_EXPERTS * MIB),
@@ -555,19 +559,20 @@
     prefix_len = prefix_keys.shape[1] * peer_count
     keys, values = prefix_keys[0], prefix_values[0]
     block = keys.shape[0]
-    cached = jnp.concatenate([keys, values], axis=0)
-    cached_x, cached_y = swap(cached, ACROSS_X), swap(cached, ACROSS_Y)
-    cached_mate = swap(cached, CORE)
+    keys_x, values_y = swap(keys, ACROSS_X), swap(values, ACROSS_Y)
+    values_x, keys_y = swap(values, ACROSS_X), swap(keys, ACROSS_Y)
+    cached_mate = (swap(keys, CORE), swap(values, CORE))
 
     queries, state = attend_near(
         own_rows, attn_gain, w_query, w_key, w_value, prefix_len, lengths, assignment, keys, values, cached_mate
     )
-    cached_x, cached_y, *state = ordered(cached_x, cached_y, *state)
-    far = [swap(cached_x[:block], ACROSS_Y), swap(cached_y[block:], ACROSS_X)]
-    mates = [swap(cached_x, CORE), swap(cached_y, CORE)]
+    keys_x, values_x, keys_y, values_y, *state = ordered(keys_x, values_x, keys_y, values_y, *state)
+    far = [swap(keys_x, ACROSS_Y), swap(values_y, ACROSS_X)]
+    mates = [swap(array, CORE) for array in (keys_x, values_x, keys_y, values_y)]
     *mates, w_gate = ordered(*mates, w_gate)
     gate = (w_gate, swap(w_gate, CORE))
-    state = attend_far(queries, state, [cached_x, cached_y, *mates])
+    near = [(keys_x, values_x), (keys_y, values_y), tuple(mates[:2]), tuple(mates[2:])]
+    state = attend_far(queries, state, near)
     *far, gate, s0, s1 = ordered(*far, gate, *state)
     far_mate = [swap(array, CORE) for array in far]
     *far_mate, w_up, w_down = ordered(*far_mate, w_up, w_down)
@@ -579,18 +584,21 @@
         final=(own_rows, w_out, moe_gain, expert_ids[0], route_weights[0]),
     )
 
-    weights = (gate, up, down)
+    owned, mated = zip(gate, up, down)
     half = tok_count // 2
     rows_x, rows_y = swap(moe_in, ACROSS_X), swap(moe_in, ACROSS_Y)
-    own, *weights = run_experts([[moe_in]], weights, load=True, out_type=F32)
-    rows_x, rows_y, own = ordered(rows_x, rows_y, own)
+    own, *owned = run_experts([[moe_in]], [owned], (0,), load=True, out_type=F32)
+    moe_in, own = ordered(moe_in, own)
+    more, *mated = run_experts([[moe_in]], [mated], (1,), load=True, out_type=F32)
+    rows_x, rows_y, more = ordered(rows_x, rows_y, more)
+    weights = [owned, mated]
     low_xy, high_xy = swap(rows_x[:half], ACROSS_Y), swap(rows_y[half:], ACROSS_X)
     to_x, to_y = run_experts([[rows_x], [rows_y]], weights)
     low_xy, high_xy, to_x, to_y = ordered(low_xy, high_xy, to_x, to_y)
     from_x, from_y = swap(to_x, ACROSS_X), swap(to_y, ACROSS_Y)
     (to_xy,) = run_experts([[low_xy, high_xy]], weights)
     from_xy = swap(to_xy, ACROSS_X | ACROSS_Y)
-    partial, from_xy = ordered(own + from_x.astype(F32) + from_y.astype(F32), from_xy)
+    partial, from_xy = ordered(own + more + from_x.astype(F32) + from_y.astype(F32), from_xy)
     expert_mix = (partial + from_xy.astype(F32)).astype(BF16)
     return (context[None], hidden[None], expert_mix[None])
 

time: 95.1 us -> 92.8 us (0.976)
  waiting for transfers between devices: 30.2 us -> 23.1 us
  starting transfers between devices: 13.9 us -> 17.6 us
  Pallas kernels: 47.7 us -> 49.8 us
    ppermute x19 -> x24, waiting for transfers between devices: 30.2 us -> 23.1 us  [swap(): lax.ppermute(array, 'req', [(i, i ^ mask) for i in range(lax.axis_size('r...]
    ppermute x19 -> x24, starting transfers between devices: 13.9 us -> 17.6 us  [swap(): lax.ppermute(array, 'req', [(i, i ^ mask) for i in range(lax.axis_size('r...]
    pallas_call x3 -> x4, Pallas kernels: 26.9 us -> 29.1 us  [run_experts(): pl.pallas_call(functools.partial(experts_kernel, sources, pieces, owners,...]
    concatenate x1 -> x0, other arithmetic: 1.07 us -> none  [local_chips(): cached = jnp.concatenate([keys, values], axis=0)]
  transfers between devices with their start and end apart: 19 -> 24, of which waited for: 12 -> 13; matrix products, arithmetic and copies ran while one was open for 0% -> 0% of each run, Pallas kernels for 50% -> 54%
where the time goes in v5:
time: 92.8 us; the launch traced here: 92.6 us
  Pallas kernels  49.8 us (54%)
  waiting for transfers between devices  23.1 us (25%)
  starting transfers between devices  17.6 us (19%)
  other arithmetic  1.3 us (1%)
    pallas_call x4, Pallas kernels, run_experts(): pl.pallas_call(functools.partial(experts_kernel, sources, pieces, owners,...  29.1 us
    ppermute x24, waiting for transfers between devices, swap(): lax.ppermute(array, 'req', [(i, i ^ mask) for i in range(lax.axis_size('r...  23.1 us
    ppermute x24, starting transfers between devices, swap(): lax.ppermute(array, 'req', [(i, i ^ mask) for i in range(lax.axis_size('r...  17.6 us
    pallas_call x2, Pallas kernels, attend_far(): pl.pallas_call(functools.partial(far_kernel, blocks, last), grid=(1,), in...  12.2 us
    pallas_call x1, Pallas kernels, attend_near(): pl.pallas_call(near_kernel, grid=(1,), in_specs=[whole_spec(tok_count, wi...  8.5 us
  transfers between devices with their start and end apart: 24, of which 13 were waited for; matrix products, arithmetic and copies ran while one was open for 0% of the time, Pallas kernels for 54%

profile of v5, /device:TPU:0, one launch (start us, length us, event | category | flops | bytes accessed | tf_op | source)
XLA Modules:
  0.0 92.6 jit_solution(512792705299031866)
XLA Ops:
  0.6 0.5 collective-permute-start
  1.2 2.9 %collective-permute-start.2 = (bf16[256,512]{1,0:T(8,128)(2,1)}, bf16[256,512]{1,0:T(8,128)(2,1)S(1)}, u32[]{:S(2)}, u32[]{:S(2)}) collective-permute-start(bf16[256,512]{1,0:T(8,128)(2,1)} %bitcast.18), channel_id=1, source_target_pairs={{0,2},{1,3},{2,0},{3,1},{4,6},{5,7},{6,4},{7,5},{8,10},{9,11},{10,... | collective-permute-start | bytes 786440 | tf_op jit(solution)/shard_map/ppermute | solution.py:531
  4.2 2.0 %collective-permute-start.4 = (bf16[256,512]{1,0:T(8,128)(2,1)}, bf16[256,512]{1,0:T(8,128)(2,1)S(1)}, u32[]{:S(2)}, u32[]{:S(2)}) collective-permute-start(bf16[256,512]{1,0:T(8,128)(2,1)} %bitcast.19), channel_id=1, source_target_pairs={{0,4},{1,5},{2,6},{3,7},{4,0},{5,1},{6,2},{7,3},{8,12},{9,13},{10,... | collective-permute-start | bytes 786440 | tf_op jit(solution)/shard_map/ppermute | solution.py:531
  6.2 8.5 %attend_near.1 = (bf16[8,512,128]{2,1,0:T(8,128)(2,1)S(1)}, f32[8,1,512]{2,1,0:T(1,128)S(1)}, f32[8,80,512]{2,1,0:T(8,128)S(1)}) custom-call(bf16[256,1024]{1,0:T(8,128)(2,1)} %bitcast.15, f32[1,1024]{1,0:T(1,128)} %bitcast.27, bf16[1024,1024]{1,0:T(8,128)(2,1)} %refs_2_.1, bf16[1024,512]{1,0:T(8,128)(2,1)} %refs_3_.1, bf16[1024,512]{1,0:T(8,128)(2,1)} %refs_4_.1, ...), custom_call_target="tpu_custom_call" | custom-call | flops 4194304000 | bytes 6291456 | tf_op jit(solution)/shard_map/attend_near/pallas_call | solution.py:334
  14.8 1.8 %collective-permute-done.3.refs_7_ = bf16[256,512]{1,0:T(8,128)(2,1)S(1)} collective-permute-done((bf16[256,512]{1,0:T(8,128)(2,1)}, bf16[256,512]{1,0:T(8,128)(2,1)S(1)}, u32[]{:S(2)}, u32[]{:S(2)}) %collective-permute-start.3) | collective-permute-done | bytes 262176 | tf_op jit(solution)/shard_map/ppermute | solution.py:531
  16.5 1.5 %collective-permute-done.5.refs_8_ = bf16[256,512]{1,0:T(8,128)(2,1)S(1)} collective-permute-done((bf16[256,512]{1,0:T(8,128)(2,1)}, bf16[256,512]{1,0:T(8,128)(2,1)S(1)}, u32[]{:S(2)}, u32[]{:S(2)}) %collective-permute-start.5) | collective-permute-done | bytes 262176 | tf_op jit(solution)/shard_map/ppermute | solution.py:531
  18.0 0.5 collective-permute-start.8
  18.5 0.5 collective-permute-start.9
  19.0 0.5 collective-permute-done.11.refs_10_
  19.9 0.4 collective-permute-done.10.refs_6_
  20.8 1.8 %collective-permute-start.6 = (bf16[256,512]{1,0:T(8,128)(2,1)S(1)}, bf16[256,512]{1,0:T(8,128)(2,1)S(1)}, u32[]{:S(2)}, u32[]{:S(2)}) collective-permute-start(bf16[256,512]{1,0:T(8,128)(2,1)S(1)} %collective-permute-done.2.refs_3_), channel_id=1, source_target_pairs={{0,4},{1,5},{2,6},{3,7},{4,0},{5,1},{6,2},{7,3},{8,12},{9,13},{10,... | collective-permute-start | bytes 786440 | tf_op jit(solution)/shard_map/ppermute | solution.py:531
  22.6 1.5 %collective-permute-start.7 = (bf16[256,512]{1,0:T(8,128)(2,1)S(1)}, bf16[256,512]{1,0:T(8,128)(2,1)S(1)}, u32[]{:S(2)}, u32[]{:S(2)}) collective-permute-start(bf16[256,512]{1,0:T(8,128)(2,1)S(1)} %collective-permute-done.5.refs_8_), channel_id=1, source_target_pairs={{0,2},{1,3},{2,0},{3,1},{4,6},{5,7},{6,4},{7,5},{8,10},{9,11},{10,... | collective-permute-start | bytes 786440 | tf_op jit(solution)/shard_map/ppermute | solution.py:531
  24.1 5.9 %attend_far.2 = (f32[8,1,512]{2,1,0:T(1,128)S(1)}, f32[8,80,512]{2,1,0:T(8,128)S(1)}) custom-call(bf16[8,512,128]{2,1,0:T(8,128)(2,1)S(1)} %get-tuple-element.53.refs_0_, f32[8,1,512]{2,1,0:T(1,128)S(1)} %get-tuple-element.61.refs_1_, f32[8,80,512]{2,1,0:T(8,128)S(1)} %get-tuple-element.62.refs_2_, bf16[256,512]{1,0:T(8,128)(2,1)S(1)} %collective-permute-done.2.refs_3_, ...), custom_call_target="tpu_custom_call" | custom-call | flops 5033164800 | bytes 4194304 | tf_op jit(solution)/shard_map/attend_far/pallas_call | solution.py:411
  30.0 0.9 collective-permute-done.7.refs_5_
  30.9 0.5 collective-permute-start.14
  31.4 1.0 %collective-permute-done.13.refs_4_ = bf16[256,512]{1,0:T(8,128)(2,1)S(1)} collective-permute-done((bf16[256,512]{1,0:T(8,128)(2,1)S(1)}, bf16[256,512]{1,0:T(8,128)(2,1)S(1)}, u32[]{:S(2)}, u32[]{:S(2)}) %collective-permute-start.13) | collective-permute-done | bytes 262176 | tf_op jit(solution)/shard_map/ppermute | solution.py:531
  32.4 0.4 collective-permute-done.14.refs_6_
  33.3 6.3 %attend_far.3 = (bf16[256,1024]{1,0:T(8,128)(2,1)}, bf16[256,1024]{1,0:T(8,128)(2,1)}, bf16[272,1024]{1,0:T(8,128)(2,1)S(1)}) custom-call(bf16[8,512,128]{2,1,0:T(8,128)(2,1)S(1)} %get-tuple-element.53.refs_0_, f32[8,1,512]{2,1,0:T(1,128)S(1)} %get-tuple-element.69.refs_1_, f32[8,80,512]{2,1,0:T(8,128)S(1)} %get-tuple-element.70.refs_2_, ...), custom_call_target="tpu_custom_call" | custom-call | flops 2516582400 | bytes 4194304 | tf_op jit(solution)/shard_map/attend_far/pallas_call | solution.py:411
  39.6 1.5 %collective-permute-start.15 = (bf16[272,1024]{1,0:T(8,128)(2,1)S(1)}, bf16[272,1024]{1,0:T(8,128)(2,1)S(1)}, u32[]{:S(2)}, u32[]{:S(2)}) collective-permute-start(bf16[272,1024]{1,0:T(8,128)(2,1)S(1)} %get-tuple-element.83.refs_0_), channel_id=1, source_target_pairs={{0,2},{1,3},{2,0},{3,1},{4,6},{5,7},{6,4},{7,5},{8,10},{9,11},{10,... | collective-permute-start | bytes 1671176 | tf_op jit(solution)/shard_map/ppermute | solution.py:531
  41.1 0.5 collective-permute-start.16
  41.6 6.0 %experts.4 = (f32[256,1024]{1,0:T(8,128)S(1)}, bf16[4,1024,512]{2,1,0:T(8,128)(2,1)S(1)}, bf16[4,1024,512]{2,1,0:T(8,128)(2,1)S(1)}, bf16[4,512,1024]{2,1,0:T(8,128)(2,1)S(1)}) custom-call(bf16[272,1024]{1,0:T(8,128)(2,1)S(1)} %get-tuple-element.83.refs_0_, bf16[4,1024,512]{2,1,0:T(8,128)(2,1)} %refs_1_, bf16[4,1024,512]{2,1,0:T(8,128)(2,1)} %refs_2_.2, ...), custom_call_target="tpu_custom_call" | custom-call | flops 12582912000 | bytes 31457280 | tf_op jit(solution)/shard_map/experts/pallas_call | solution.py:510
  47.6 6.0 %experts.5 = (f32[256,1024]{1,0:T(8,128)S(1)}, bf16[4,1024,512]{2,1,0:T(8,128)(2,1)S(1)}, bf16[4,1024,512]{2,1,0:T(8,128)(2,1)S(1)}, bf16[4,512,1024]{2,1,0:T(8,128)(2,1)S(1)}) custom-call(bf16[272,1024]{1,0:T(8,128)(2,1)S(1)} %get-tuple-element.83.refs_0_, bf16[4,1024,512]{2,1,0:T(8,128)(2,1)} %collective-permute-done.12.refs_1_, ...), custom_call_target="tpu_custom_call" | custom-call | flops 12582912000 | bytes 31457280 | tf_op jit(solution)/shard_map/experts/pallas_call | solution.py:510
  53.5 0.7 collective-permute-done.15.refs_0_
  54.3 1.2 %collective-permute-done.16.refs_1_ = bf16[272,1024]{1,0:T(8,128)(2,1)S(1)} collective-permute-done((bf16[272,1024]{1,0:T(8,128)(2,1)S(1)}, bf16[272,1024]{1,0:T(8,128)(2,1)S(1)}, u32[]{:S(2)}, u32[]{:S(2)}) %collective-permute-start.16) | collective-permute-done | bytes 557088 | tf_op jit(solution)/shard_map/ppermute | solution.py:531
  55.5 0.6 collective-permute-start.20
  56.5 9.8 %experts.6 = (bf16[256,1024]{1,0:T(8,128)(2,1)S(1)}, bf16[256,1024]{1,0:T(8,128)(2,1)S(1)}) custom-call(bf16[272,1024]{1,0:T(8,128)(2,1)S(1)} %collective-permute-done.15.refs_0_, bf16[272,1024]{1,0:T(8,128)(2,1)S(1)} %collective-permute-done.16.refs_1_, bf16[4,1024,512]{2,1,0:T(8,128)(2,1)S(1)} %get-tuple-element.89.refs_2_, ...), custom_call_target="tpu_custom_call" | custom-call | flops 12582912000 | bytes 31457280 | tf_op jit(solution)/shard_map/experts/pallas_call | solution.py:510
  66.3 1.8 %collective-permute-start.21 = (bf16[256,1024]{1,0:T(8,128)(2,1)S(1)}, bf16[256,1024]{1,0:T(8,128)(2,1)S(1)}, u32[]{:S(2)}, u32[]{:S(2)}) collective-permute-start(bf16[256,1024]{1,0:T(8,128)(2,1)S(1)} %get-tuple-element.97), channel_id=1, source_target_pairs={{0,2},{1,3},{2,0},{3,1},{4,6},{5,7},{6,4},{7,5},{8,10},{9,11},{10,... | collective-permute-start | bytes 1572872 | tf_op jit(solution)/shard_map/ppermute | solution.py:531
  68.1 1.5 %collective-permute-start.22 = (bf16[256,1024]{1,0:T(8,128)(2,1)S(1)}, bf16[256,1024]{1,0:T(8,128)(2,1)S(1)}, u32[]{:S(2)}, u32[]{:S(2)}) collective-permute-start(bf16[256,1024]{1,0:T(8,128)(2,1)S(1)} %get-tuple-element.98), channel_id=1, source_target_pairs={{0,4},{1,5},{2,6},{3,7},{4,0},{5,1},{6,2},{7,3},{8,12},{9,13},{10,... | collective-permute-start | bytes 1572872 | tf_op jit(solution)/shard_map/ppermute | solution.py:531
  69.6 7.4 %experts.7 = bf16[256,1024]{1,0:T(8,128)(2,1)S(1)} custom-call(bf16[128,1024]{1,0:T(8,128)(2,1)S(1)} %collective-permute-done.19.refs_0_, bf16[144,1024]{1,0:T(8,128)(2,1)S(1)} %collective-permute-done.20.refs_1_, bf16[4,1024,512]{2,1,0:T(8,128)(2,1)S(1)} %get-tuple-element.89.refs_2_, bf16[4,1024,512]{2,1,0:T(8,128)(2,1)S(1)} %get-tuple-element.90.refs_3_, ...), custom_call_target="tpu_custom_call" | custom-call | flops 12582912000 | bytes 31457280 | tf_op jit(solution)/shard_map/experts/pallas_call | solution.py:510
  77.3 3.0 %collective-permute-done.21 = bf16[256,1024]{1,0:T(8,128)(2,1)S(1)} collective-permute-done((bf16[256,1024]{1,0:T(8,128)(2,1)S(1)}, bf16[256,1024]{1,0:T(8,128)(2,1)S(1)}, u32[]{:S(2)}, u32[]{:S(2)}) %collective-permute-start.21) | collective-permute-done | bytes 524320 | tf_op jit(solution)/shard_map/ppermute | solution.py:531
  80.3 11.0 %collective-permute-done.22 = bf16[256,1024]{1,0:T(8,128)(2,1)S(1)} collective-permute-done((bf16[256,1024]{1,0:T(8,128)(2,1)S(1)}, bf16[256,1024]{1,0:T(8,128)(2,1)S(1)}, u32[]{:S(2)}, u32[]{:S(2)}) %collective-permute-start.22) | collective-permute-done | bytes 524320 | tf_op jit(solution)/shard_map/ppermute | solution.py:531
  91.7 0.9 %fusion = bf16[1,256,1024]{2,1,0:T(8,128)(2,1)} fusion(f32[256,1024]{1,0:T(8,128)S(1)} %convert_add_fusion, bf16[256,1024]{1,0:T(8,128)(2,1)S(1)} %collective-permute-done.23), kind=kLoop, calls=%fused_computation.2 | loop fusion | flops 786432 | bytes 2097152 | tf_op jit(solution)/shard_map/broadcast_in_dim | solution.py:603
  (27 shorter events, 2.6 us)
Async XLA Ops:
  0.6 5.6 %collective-permute-start = (bf16[256,512]{1,0:T(8,128)(2,1)}, bf16[256,512]{1,0:T(8,128)(2,1)S(1)}, u32[]{:S(2)}, u32[]{:S(2)}) collective-permute-start(bf16[256,512]{1,0:T(8,128)(2,1)} %bitcast.17), channel_id=1, source_target_pairs={{0,1},{1,0},{2,3},{3,2},{4,5},{5,4},{6,7},{7,6},{8,9},{9,8},{10,11... | collective-permute-start | bytes 786440 | tf_op jit(solution)/shard_map/ppermute | solution.py:531
  1.2 5.1 %collective-permute-start.1 = (bf16[256,512]{1,0:T(8,128)(2,1)}, bf16[256,512]{1,0:T(8,128)(2,1)S(1)}, u32[]{:S(2)}, u32[]{:S(2)}) collective-permute-start(bf16[256,512]{1,0:T(8,128)(2,1)} %bitcast.21), channel_id=1, source_target_pairs={{0,1},{1,0},{2,3},{3,2},{4,5},{5,4},{6,7},{7,6},{8,9},{9,8},{10,11... | collective-permute-start | bytes 786440 | tf_op jit(solution)/shard_map/ppermute | solution.py:531
  1.2 13.5 %collective-permute-start.2 = (bf16[256,512]{1,0:T(8,128)(2,1)}, bf16[256,512]{1,0:T(8,128)(2,1)S(1)}, u32[]{:S(2)}, u32[]{:S(2)}) collective-permute-start(bf16[256,512]{1,0:T(8,128)(2,1)} %bitcast.18), channel_id=1, source_target_pairs={{0,2},{1,3},{2,0},{3,1},{4,6},{5,7},{6,4},{7,5},{8,10},{9,11},{10,... | collective-permute-start | bytes 786440 | tf_op jit(solution)/shard_map/ppermute | solution.py:531
  4.1 12.4 %collective-permute-start.3 = (bf16[256,512]{1,0:T(8,128)(2,1)}, bf16[256,512]{1,0:T(8,128)(2,1)S(1)}, u32[]{:S(2)}, u32[]{:S(2)}) collective-permute-start(bf16[256,512]{1,0:T(8,128)(2,1)} %bitcast.22), channel_id=1, source_target_pairs={{0,2},{1,3},{2,0},{3,1},{4,6},{5,7},{6,4},{7,5},{8,10},{9,11},{10,... | collective-permute-start | bytes 786440 | tf_op jit(solution)/shard_map/ppermute | solution.py:531
  4.2 12.3 %collective-permute-start.4 = (bf16[256,512]{1,0:T(8,128)(2,1)}, bf16[256,512]{1,0:T(8,128)(2,1)S(1)}, u32[]{:S(2)}, u32[]{:S(2)}) collective-permute-start(bf16[256,512]{1,0:T(8,128)(2,1)} %bitcast.19), channel_id=1, source_target_pairs={{0,4},{1,5},{2,6},{3,7},{4,0},{5,1},{6,2},{7,3},{8,12},{9,13},{10,... | collective-permute-start | bytes 786440 | tf_op jit(solution)/shard_map/ppermute | solution.py:531
  6.2 11.8 %collective-permute-start.5 = (bf16[256,512]{1,0:T(8,128)(2,1)}, bf16[256,512]{1,0:T(8,128)(2,1)S(1)}, u32[]{:S(2)}, u32[]{:S(2)}) collective-permute-start(bf16[256,512]{1,0:T(8,128)(2,1)} %bitcast.23), channel_id=1, source_target_pairs={{0,4},{1,5},{2,6},{3,7},{4,0},{5,1},{6,2},{7,3},{8,12},{9,13},{10,... | collective-permute-start | bytes 786440 | tf_op jit(solution)/shard_map/ppermute | solution.py:531
  18.0 1.5 %collective-permute-start.11 = (bf16[256,512]{1,0:T(8,128)(2,1)S(1)}, bf16[256,512]{1,0:T(8,128)(2,1)S(1)}, u32[]{:S(2)}, u32[]{:S(2)}) collective-permute-start(bf16[256,512]{1,0:T(8,128)(2,1)S(1)} %collective-permute-done.5.refs_8_), channel_id=1, source_target_pairs={{0,1},{1,0},{2,3},{3,2},{4,5},{5,4},{6,7},{7,6},{8,9},{9,8},{10,11... | collective-permute-start | bytes 786440 | tf_op jit(solution)/shard_map/ppermute | solution.py:531
  18.0 1.9 %collective-permute-start.8 = (bf16[256,512]{1,0:T(8,128)(2,1)S(1)}, bf16[256,512]{1,0:T(8,128)(2,1)S(1)}, u32[]{:S(2)}, u32[]{:S(2)}) collective-permute-start(bf16[256,512]{1,0:T(8,128)(2,1)S(1)} %collective-permute-done.2.refs_3_), channel_id=1, source_target_pairs={{0,1},{1,0},{2,3},{3,2},{4,5},{5,4},{6,7},{7,6},{8,9},{9,8},{10,11... | collective-permute-start | bytes 786440 | tf_op jit(solution)/shard_map/ppermute | solution.py:531
  18.5 1.8 %collective-permute-start.10 = (bf16[256,512]{1,0:T(8,128)(2,1)S(1)}, bf16[256,512]{1,0:T(8,128)(2,1)S(1)}, u32[]{:S(2)}, u32[]{:S(2)}) collective-permute-start(bf16[256,512]{1,0:T(8,128)(2,1)S(1)} %collective-permute-done.4.refs_4_), channel_id=1, source_target_pairs={{0,1},{1,0},{2,3},{3,2},{4,5},{5,4},{6,7},{7,6},{8,9},{9,8},{10,11... | collective-permute-start | bytes 786440 | tf_op jit(solution)/shard_map/ppermute | solution.py:531
  18.5 2.1 %collective-permute-start.9 = (bf16[256,512]{1,0:T(8,128)(2,1)S(1)}, bf16[256,512]{1,0:T(8,128)(2,1)S(1)}, u32[]{:S(2)}, u32[]{:S(2)}) collective-permute-start(bf16[256,512]{1,0:T(8,128)(2,1)S(1)} %collective-permute-done.3.refs_7_), channel_id=1, source_target_pairs={{0,1},{1,0},{2,3},{3,2},{4,5},{5,4},{6,7},{7,6},{8,9},{9,8},{10,11... | collective-permute-start | bytes 786440 | tf_op jit(solution)/shard_map/ppermute | solution.py:531
  20.7 10.2 %collective-permute-start.12 = (bf16[4,1024,512]{2,1,0:T(8,128)(2,1)}, bf16[4,1024,512]{2,1,0:T(8,128)(2,1)}, u32[]{:S(2)}, u32[]{:S(2)}) collective-permute-start(bf16[4,1024,512]{2,1,0:T(8,128)(2,1)} %refs_1_), channel_id=1, source_target_pairs={{0,1},{1,0},{2,3},{3,2},{4,5},{5,4},{6,7},{7,6},{8,9},{9,8},{10,11... | collective-permute-start | bytes 12582920 | tf_op jit(solution)/shard_map/ppermute | solution.py:531
  20.8 9.2 %collective-permute-start.6 = (bf16[256,512]{1,0:T(8,128)(2,1)S(1)}, bf16[256,512]{1,0:T(8,128)(2,1)S(1)}, u32[]{:S(2)}, u32[]{:S(2)}) collective-permute-start(bf16[256,512]{1,0:T(8,128)(2,1)S(1)} %collective-permute-done.2.refs_3_), channel_id=1, source_target_pairs={{0,4},{1,5},{2,6},{3,7},{4,0},{5,1},{6,2},{7,3},{8,12},{9,13},{10,... | collective-permute-start | bytes 786440 | tf_op jit(solution)/shard_map/ppermute | solution.py:531
  22.6 8.3 %collective-permute-start.7 = (bf16[256,512]{1,0:T(8,128)(2,1)S(1)}, bf16[256,512]{1,0:T(8,128)(2,1)S(1)}, u32[]{:S(2)}, u32[]{:S(2)}) collective-permute-start(bf16[256,512]{1,0:T(8,128)(2,1)S(1)} %collective-permute-done.5.refs_8_), channel_id=1, source_target_pairs={{0,2},{1,3},{2,0},{3,1},{4,6},{5,7},{6,4},{7,5},{8,10},{9,11},{10,... | collective-permute-start | bytes 786440 | tf_op jit(solution)/shard_map/ppermute | solution.py:531
  30.9 1.5 %collective-permute-start.13 = (bf16[256,512]{1,0:T(8,128)(2,1)S(1)}, bf16[256,512]{1,0:T(8,128)(2,1)S(1)}, u32[]{:S(2)}, u32[]{:S(2)}) collective-permute-start(bf16[256,512]{1,0:T(8,128)(2,1)S(1)} %collective-permute-done.6.refs_3_), channel_id=1, source_target_pairs={{0,1},{1,0},{2,3},{3,2},{4,5},{5,4},{6,7},{7,6},{8,9},{9,8},{10,11... | collective-permute-start | bytes 786440 | tf_op jit(solution)/shard_map/ppermute | solution.py:531
  30.9 1.9 %collective-permute-start.14 = (bf16[256,512]{1,0:T(8,128)(2,1)S(1)}, bf16[256,512]{1,0:T(8,128)(2,1)S(1)}, u32[]{:S(2)}, u32[]{:S(2)}) collective-permute-start(bf16[256,512]{1,0:T(8,128)(2,1)S(1)} %collective-permute-done.7.refs_5_), channel_id=1, source_target_pairs={{0,1},{1,0},{2,3},{3,2},{4,5},{5,4},{6,7},{7,6},{8,9},{9,8},{10,11... | collective-permute-start | bytes 786440 | tf_op jit(solution)/shard_map/ppermute | solution.py:531
  32.8 14.8 %collective-permute-start.17 = (bf16[4,1024,512]{2,1,0:T(8,128)(2,1)}, bf16[4,1024,512]{2,1,0:T(8,128)(2,1)}, u32[]{:S(2)}, u32[]{:S(2)}) collective-permute-start(bf16[4,1024,512]{2,1,0:T(8,128)(2,1)} %refs_2_.2), channel_id=1, source_target_pairs={{0,1},{1,0},{2,3},{3,2},{4,5},{5,4},{6,7},{7,6},{8,9},{9,8},{10,11... | collective-permute-start | bytes 12582920 | tf_op jit(solution)/shard_map/ppermute | solution.py:531
  32.9 14.6 %collective-permute-start.18 = (bf16[4,512,1024]{2,1,0:T(8,128)(2,1)}, bf16[4,512,1024]{2,1,0:T(8,128)(2,1)}, u32[]{:S(2)}, u32[]{:S(2)}) collective-permute-start(bf16[4,512,1024]{2,1,0:T(8,128)(2,1)} %refs_3_.2), channel_id=1, source_target_pairs={{0,1},{1,0},{2,3},{3,2},{4,5},{5,4},{6,7},{7,6},{8,9},{9,8},{10,11... | collective-permute-start | bytes 12582920 | tf_op jit(solution)/shard_map/ppermute | solution.py:531
  39.6 14.7 %collective-permute-start.15 = (bf16[272,1024]{1,0:T(8,128)(2,1)S(1)}, bf16[272,1024]{1,0:T(8,128)(2,1)S(1)}, u32[]{:S(2)}, u32[]{:S(2)}) collective-permute-start(bf16[272,1024]{1,0:T(8,128)(2,1)S(1)} %get-tuple-element.83.refs_0_), channel_id=1, source_target_pairs={{0,2},{1,3},{2,0},{3,1},{4,6},{5,7},{6,4},{7,5},{8,10},{9,11},{10,... | collective-permute-start | bytes 1671176 | tf_op jit(solution)/shard_map/ppermute | solution.py:531
  41.1 14.4 %collective-permute-start.16 = (bf16[272,1024]{1,0:T(8,128)(2,1)S(1)}, bf16[272,1024]{1,0:T(8,128)(2,1)S(1)}, u32[]{:S(2)}, u32[]{:S(2)}) collective-permute-start(bf16[272,1024]{1,0:T(8,128)(2,1)S(1)} %get-tuple-element.83.refs_0_), channel_id=1, source_target_pairs={{0,4},{1,5},{2,6},{3,7},{4,0},{5,1},{6,2},{7,3},{8,12},{9,13},{10,... | collective-permute-start | bytes 1671176 | tf_op jit(solution)/shard_map/ppermute | solution.py:531
  55.5 10.8 %collective-permute-start.20 = (bf16[144,1024]{1,0:T(8,128)(2,1)S(1)}, bf16[144,1024]{1,0:T(8,128)(2,1)S(1)}, u32[]{:S(2)}, u32[]{:S(2)}) collective-permute-start(bf16[144,1024]{1,0:T(8,128)(2,1)S(1)} %slice.7), channel_id=1, source_target_pairs={{0,2},{1,3},{2,0},{3,1},{4,6},{5,7},{6,4},{7,5},{8,10},{9,11},{10,... | collective-permute-start | bytes 884744 | tf_op jit(solution)/shard_map/ppermute | solution.py:531
  56.1 10.2 %collective-permute-start.19 = (bf16[128,1024]{1,0:T(8,128)(2,1)S(1)}, bf16[128,1024]{1,0:T(8,128)(2,1)S(1)}, u32[]{:S(2)}, u32[]{:S(2)}) collective-permute-start(bf16[128,1024]{1,0:T(8,128)(2,1)S(1)} %slice.6), channel_id=1, source_target_pairs={{0,4},{1,5},{2,6},{3,7},{4,0},{5,1},{6,2},{7,3},{8,12},{9,13},{10,... | collective-permute-start | bytes 786440 | tf_op jit(solution)/shard_map/ppermute | solution.py:531
  66.3 14.0 %collective-permute-start.21 = (bf16[256,1024]{1,0:T(8,128)(2,1)S(1)}, bf16[256,1024]{1,0:T(8,128)(2,1)S(1)}, u32[]{:S(2)}, u32[]{:S(2)}) collective-permute-start(bf16[256,1024]{1,0:T(8,128)(2,1)S(1)} %get-tuple-element.97), channel_id=1, source_target_pairs={{0,2},{1,3},{2,0},{3,1},{4,6},{5,7},{6,4},{7,5},{8,10},{9,11},{10,... | collective-permute-start | bytes 1572872 | tf_op jit(solution)/shard_map/ppermute | solution.py:531
  68.1 23.2 %collective-permute-start.22 = (bf16[256,1024]{1,0:T(8,128)(2,1)S(1)}, bf16[256,1024]{1,0:T(8,128)(2,1)S(1)}, u32[]{:S(2)}, u32[]{:S(2)}) collective-permute-start(bf16[256,1024]{1,0:T(8,128)(2,1)S(1)} %get-tuple-element.98), channel_id=1, source_target_pairs={{0,4},{1,5},{2,6},{3,7},{4,0},{5,1},{6,2},{7,3},{8,12},{9,13},{10,... | collective-permute-start | bytes 1572872 | tf_op jit(solution)/shard_map/ppermute | solution.py:531
  77.0 14.7 %collective-permute-start.23 = (bf16[256,1024]{1,0:T(8,128)(2,1)S(1)}, bf16[256,1024]{1,0:T(8,128)(2,1)S(1)}, u32[]{:S(2)}, u32[]{:S(2)}) collective-permute-start(bf16[256,1024]{1,0:T(8,128)(2,1)S(1)} %experts.7), channel_id=1, source_target_pairs={{0,6},{1,7},{2,4},{3,5},{4,2},{5,3},{6,0},{7,1},{8,14},{9,15},{10,... | collective-permute-start | bytes 1572872 | tf_op jit(solution)/shard_map/ppermute | solution.py:531

commit v6 on v5

--- a/solution.py
+++ b/solution.py
@@ -183,9 +183,9 @@
 BF16 = jnp.bfloat16
 MIB = 1 << 20
 LANES = 128
-VMEM_ATTEND = 54
-VMEM_LAST = 57
-VMEM_NEAR = 54
+VMEM_ATTEND = 30
+VMEM_LAST = 26
+VMEM_NEAR = 30
 NOTE_ROWS = 16
 VMEM_EXPERTS = 17
 
@@ -587,18 +587,16 @@
     owned, mated = zip(gate, up, down)
     half = tok_count // 2
     rows_x, rows_y = swap(moe_in, ACROSS_X), swap(moe_in, ACROSS_Y)
-    own, *owned = run_experts([[moe_in]], [owned], (0,), load=True, out_type=F32)
-    moe_in, own = ordered(moe_in, own)
-    more, *mated = run_experts([[moe_in]], [mated], (1,), load=True, out_type=F32)
-    rows_x, rows_y, more = ordered(rows_x, rows_y, more)
-    weights = [owned, mated]
+    weights = [list(owned), list(mated)]
+    (own,) = run_experts([[moe_in]], weights, out_type=F32)
+    rows_x, rows_y, own = ordered(rows_x, rows_y, own)
     low_xy, high_xy = swap(rows_x[:half], ACROSS_Y), swap(rows_y[half:], ACROSS_X)
     to_x, to_y = run_experts([[rows_x], [rows_y]], weights)
     low_xy, high_xy, to_x, to_y = ordered(low_xy, high_xy, to_x, to_y)
     from_x, from_y = swap(to_x, ACROSS_X), swap(to_y, ACROSS_Y)
     (to_xy,) = run_experts([[low_xy, high_xy]], weights)
     from_xy = swap(to_xy, ACROSS_X | ACROSS_Y)
-    partial, from_xy = ordered(own + more + from_x.astype(F32) + from_y.astype(F32), from_xy)
+    partial, from_xy = ordered(own + from_x.astype(F32) + from_y.astype(F32), from_xy)
     expert_mix = (partial + from_xy.astype(F32)).astype(BF16)
     return (context[None], hidden[None], expert_mix[None])
 

time: 92.8 us -> 91.8 us (0.989)
  Pallas kernels: 49.8 us -> 45.2 us
  waiting for transfers between devices: 23.1 us -> 25.8 us
  starting transfers between devices: 17.6 us -> 18.7 us
    pallas_call x4 -> x3, Pallas kernels: 29.1 us -> 24.4 us  [run_experts(): pl.pallas_call(functools.partial(experts_kernel, sources, pieces, owners,...]
    ppermute x24, waiting for transfers between devices: 23.1 us -> 25.8 us  [swap(): lax.ppermute(array, 'req', [(i, i ^ mask) for i in range(lax.axis_size('r...]
    ppermute x24, starting transfers between devices: 17.6 us -> 18.7 us  [swap(): lax.ppermute(array, 'req', [(i, i ^ mask) for i in range(lax.axis_size('r...]
  transfers between devices with their start and end apart: 24 -> 24, of which waited for: 13 -> 14; matrix products, arithmetic and copies ran while one was open for 0% -> 0% of each run, Pallas kernels for 54% -> 49%
where the time goes in v6:
time: 91.8 us; the launch traced here: 91.7 us
  Pallas kernels  45.2 us (49%)
  waiting for transfers between devices  25.8 us (28%)
  starting transfers between devices  18.7 us (20%)
  other arithmetic  1.18 us (1%)
    ppermute x24, waiting for transfers between devices, swap(): lax.ppermute(array, 'req', [(i, i ^ mask) for i in range(lax.axis_size('r...  25.8 us
    pallas_call x3, Pallas kernels, run_experts(): pl.pallas_call(functools.partial(experts_kernel, sources, pieces, owners,...  24.4 us
    ppermute x24, starting transfers between devices, swap(): lax.ppermute(array, 'req', [(i, i ^ mask) for i in range(lax.axis_size('r...  18.7 us
    pallas_call x2, Pallas kernels, attend_far(): pl.pallas_call(functools.partial(far_kernel, blocks, last), grid=(1,), in...  12.2 us
    pallas_call x1, Pallas kernels, attend_near(): pl.pallas_call(near_kernel, grid=(1,), in_specs=[whole_spec(tok_count, wi...  8.65 us
  transfers between devices with their start and end apart: 24, of which 14 were waited for; matrix products, arithmetic and copies ran while one was open for 0% of the time, Pallas kernels for 49%

profile of v6, /device:TPU:0, one launch (start us, length us, event | category | flops | bytes accessed | tf_op | source)
XLA Modules:
  0.0 91.7 jit_solution(7198476910577472403)
XLA Ops:
  0.6 0.5 collective-permute-start
  1.2 2.9 %collective-permute-start.4 = (bf16[256,512]{1,0:T(8,128)(2,1)}, bf16[256,512]{1,0:T(8,128)(2,1)S(1)}, u32[]{:S(2)}, u32[]{:S(2)}) collective-permute-start(bf16[256,512]{1,0:T(8,128)(2,1)} %bitcast.18), channel_id=1, source_target_pairs={{0,4},{1,5},{2,6},{3,7},{4,0},{5,1},{6,2},{7,3},{8,12},{9,13},{10,... | collective-permute-start | bytes 786440 | tf_op jit(solution)/shard_map/ppermute | solution.py:531
  4.2 1.5 %collective-permute-start.2 = (bf16[256,512]{1,0:T(8,128)(2,1)}, bf16[256,512]{1,0:T(8,128)(2,1)S(1)}, u32[]{:S(2)}, u32[]{:S(2)}) collective-permute-start(bf16[256,512]{1,0:T(8,128)(2,1)} %bitcast.19), channel_id=1, source_target_pairs={{0,2},{1,3},{2,0},{3,1},{4,6},{5,7},{6,4},{7,5},{8,10},{9,11},{10,... | collective-permute-start | bytes 786440 | tf_op jit(solution)/shard_map/ppermute | solution.py:531
  5.7 0.5 collective-permute-start.5
  6.2 8.6 %attend_near.1 = (bf16[8,512,128]{2,1,0:T(8,128)(2,1)S(1)}, f32[8,1,512]{2,1,0:T(1,128)S(1)}, f32[8,80,512]{2,1,0:T(8,128)S(1)}) custom-call(bf16[256,1024]{1,0:T(8,128)(2,1)} %bitcast.15, f32[1,1024]{1,0:T(1,128)} %bitcast.27, bf16[1024,1024]{1,0:T(8,128)(2,1)} %refs_2_.1, bf16[1024,512]{1,0:T(8,128)(2,1)} %refs_3_.1, bf16[1024,512]{1,0:T(8,128)(2,1)} %refs_4_.1, ...), custom_call_target="tpu_custom_call" | custom-call | flops 4194304000 | bytes 6291456 | tf_op jit(solution)/shard_map/attend_near/pallas_call | solution.py:334
  14.9 1.7 %collective-permute-done.5.refs_8_ = bf16[256,512]{1,0:T(8,128)(2,1)S(1)} collective-permute-done((bf16[256,512]{1,0:T(8,128)(2,1)}, bf16[256,512]{1,0:T(8,128)(2,1)S(1)}, u32[]{:S(2)}, u32[]{:S(2)}) %collective-permute-start.5) | collective-permute-done | bytes 262176 | tf_op jit(solution)/shard_map/ppermute | solution.py:531
  16.6 1.5 %collective-permute-done.3.refs_7_ = bf16[256,512]{1,0:T(8,128)(2,1)S(1)} collective-permute-done((bf16[256,512]{1,0:T(8,128)(2,1)}, bf16[256,512]{1,0:T(8,128)(2,1)S(1)}, u32[]{:S(2)}, u32[]{:S(2)}) %collective-permute-start.3) | collective-permute-done | bytes 262176 | tf_op jit(solution)/shard_map/ppermute | solution.py:531
  18.0 0.5 collective-permute-start.10
  18.5 0.5 collective-permute-start.11
  19.0 0.5 collective-permute-done.9.refs_9_
  19.9 0.4 collective-permute-done.8.refs_5_
  21.1 1.7 %collective-permute-start.7 = (bf16[256,512]{1,0:T(8,128)(2,1)S(1)}, bf16[256,512]{1,0:T(8,128)(2,1)S(1)}, u32[]{:S(2)}, u32[]{:S(2)}) collective-permute-start(bf16[256,512]{1,0:T(8,128)(2,1)S(1)} %collective-permute-done.5.refs_8_), channel_id=1, source_target_pairs={{0,2},{1,3},{2,0},{3,1},{4,6},{5,7},{6,4},{7,5},{8,10},{9,11},{10,... | collective-permute-start | bytes 786440 | tf_op jit(solution)/shard_map/ppermute | solution.py:531
  22.8 5.9 %attend_far.2 = (f32[8,1,512]{2,1,0:T(1,128)S(1)}, f32[8,80,512]{2,1,0:T(8,128)S(1)}) custom-call(bf16[8,512,128]{2,1,0:T(8,128)(2,1)S(1)} %get-tuple-element.43.refs_0_, f32[8,1,512]{2,1,0:T(1,128)S(1)} %get-tuple-element.51.refs_1_, f32[8,80,512]{2,1,0:T(8,128)S(1)} %get-tuple-element.52.refs_2_, bf16[256,512]{1,0:T(8,128)(2,1)S(1)} %collective-permute-done.2.refs_3_, ...), custom_call_target="tpu_custom_call" | custom-call | flops 5033164800 | bytes 4194304 | tf_op jit(solution)/shard_map/attend_far/pallas_call | solution.py:411
  28.8 0.6 collective-permute-done.6.refs_3_
  29.4 0.5 collective-permute-start.14
  29.9 1.0 %collective-permute-done.13.refs_4_ = bf16[256,512]{1,0:T(8,128)(2,1)S(1)} collective-permute-done((bf16[256,512]{1,0:T(8,128)(2,1)S(1)}, bf16[256,512]{1,0:T(8,128)(2,1)S(1)}, u32[]{:S(2)}, u32[]{:S(2)}) %collective-permute-start.13) | collective-permute-done | bytes 262176 | tf_op jit(solution)/shard_map/ppermute | solution.py:531
  31.8 6.3 %attend_far.3 = (bf16[256,1024]{1,0:T(8,128)(2,1)}, bf16[256,1024]{1,0:T(8,128)(2,1)}, bf16[272,1024]{1,0:T(8,128)(2,1)S(1)}) custom-call(bf16[8,512,128]{2,1,0:T(8,128)(2,1)S(1)} %get-tuple-element.43.refs_0_, f32[8,1,512]{2,1,0:T(1,128)S(1)} %get-tuple-element.59.refs_1_, f32[8,80,512]{2,1,0:T(8,128)S(1)} %get-tuple-element.60.refs_2_, ...), custom_call_target="tpu_custom_call" | custom-call | flops 2516582400 | bytes 4194304 | tf_op jit(solution)/shard_map/attend_far/pallas_call | solution.py:411
  38.1 1.7 %collective-permute-start.16 = (bf16[272,1024]{1,0:T(8,128)(2,1)S(1)}, bf16[272,1024]{1,0:T(8,128)(2,1)S(1)}, u32[]{:S(2)}, u32[]{:S(2)}) collective-permute-start(bf16[272,1024]{1,0:T(8,128)(2,1)S(1)} %get-tuple-element.67.refs_0_), channel_id=1, source_target_pairs={{0,4},{1,5},{2,6},{3,7},{4,0},{5,1},{6,2},{7,3},{8,12},{9,13},{10,... | collective-permute-start | bytes 1671176 | tf_op jit(solution)/shard_map/ppermute | solution.py:531
  39.9 1.5 %collective-permute-start.15 = (bf16[272,1024]{1,0:T(8,128)(2,1)S(1)}, bf16[272,1024]{1,0:T(8,128)(2,1)S(1)}, u32[]{:S(2)}, u32[]{:S(2)}) collective-permute-start(bf16[272,1024]{1,0:T(8,128)(2,1)S(1)} %get-tuple-element.67.refs_0_), channel_id=1, source_target_pairs={{0,2},{1,3},{2,0},{3,1},{4,6},{5,7},{6,4},{7,5},{8,10},{9,11},{10,... | collective-permute-start | bytes 1671176 | tf_op jit(solution)/shard_map/ppermute | solution.py:531
  41.4 3.1 %collective-permute-done.18.refs_6_.refs_7_ = bf16[4,512,1024]{2,1,0:T(8,128)(2,1)S(1)} collective-permute-done((bf16[4,512,1024]{2,1,0:T(8,128)(2,1)S(1)}, bf16[4,512,1024]{2,1,0:T(8,128)(2,1)S(1)}, u32[]{:S(2)}, u32[]{:S(2)}) %collective-permute-start.18) | collective-permute-done | bytes 4194336 | tf_op jit(solution)/shard_map/ppermute | solution.py:531
  44.5 7.3 %experts.3 = f32[256,1024]{1,0:T(8,128)S(1)} custom-call(bf16[272,1024]{1,0:T(8,128)(2,1)S(1)} %get-tuple-element.67.refs_0_, bf16[4,1024,512]{2,1,0:T(8,128)(2,1)S(1)} %copy-done, bf16[4,1024,512]{2,1,0:T(8,128)(2,1)S(1)} %copy-done.1, bf16[4,512,1024]{2,1,0:T(8,128)(2,1)S(1)} %copy-done.2, ...), custom_call_target="tpu_custom_call" | custom-call | flops 12582912000 | bytes 31457280 | tf_op jit(solution)/shard_map/experts/pallas_call | solution.py:510
  51.8 1.0 %collective-permute-done.16.refs_1_ = bf16[272,1024]{1,0:T(8,128)(2,1)S(1)} collective-permute-done((bf16[272,1024]{1,0:T(8,128)(2,1)S(1)}, bf16[272,1024]{1,0:T(8,128)(2,1)S(1)}, u32[]{:S(2)}, u32[]{:S(2)}) %collective-permute-start.16) | collective-permute-done | bytes 557088 | tf_op jit(solution)/shard_map/ppermute | solution.py:531
  52.8 1.5 %collective-permute-done.15.refs_0_ = bf16[272,1024]{1,0:T(8,128)(2,1)S(1)} collective-permute-done((bf16[272,1024]{1,0:T(8,128)(2,1)S(1)}, bf16[272,1024]{1,0:T(8,128)(2,1)S(1)}, u32[]{:S(2)}, u32[]{:S(2)}) %collective-permute-start.15) | collective-permute-done | bytes 557088 | tf_op jit(solution)/shard_map/ppermute | solution.py:531
  54.7 1.8 %collective-permute-start.20 = (bf16[144,1024]{1,0:T(8,128)(2,1)S(1)}, bf16[144,1024]{1,0:T(8,128)(2,1)S(1)}, u32[]{:S(2)}, u32[]{:S(2)}) collective-permute-start(bf16[144,1024]{1,0:T(8,128)(2,1)S(1)} %slice.7), channel_id=1, source_target_pairs={{0,2},{1,3},{2,0},{3,1},{4,6},{5,7},{6,4},{7,5},{8,10},{9,11},{10,... | collective-permute-start | bytes 884744 | tf_op jit(solution)/shard_map/ppermute | solution.py:531
  56.4 9.8 %experts.4 = (bf16[256,1024]{1,0:T(8,128)(2,1)S(1)}, bf16[256,1024]{1,0:T(8,128)(2,1)S(1)}) custom-call(bf16[272,1024]{1,0:T(8,128)(2,1)S(1)} %collective-permute-done.15.refs_0_, bf16[272,1024]{1,0:T(8,128)(2,1)S(1)} %collective-permute-done.16.refs_1_, bf16[4,1024,512]{2,1,0:T(8,128)(2,1)S(1)} %copy-done, bf16[4,1024,512]{2,1,0:T(8,128)(2,1)S(1)} %copy-done.1, ...), custom_call_target="tpu_custom_call" | custom-call | flops 12582912000 | bytes 31457280 | tf_op jit(solution)/shard_map/experts/pallas_call | solution.py:510
  66.2 0.4 collective-permute-start.21
  66.6 1.7 %collective-permute-start.22 = (bf16[256,1024]{1,0:T(8,128)(2,1)S(1)}, bf16[256,1024]{1,0:T(8,128)(2,1)S(1)}, u32[]{:S(2)}, u32[]{:S(2)}) collective-permute-start(bf16[256,1024]{1,0:T(8,128)(2,1)S(1)} %get-tuple-element.78), channel_id=1, source_target_pairs={{0,4},{1,5},{2,6},{3,7},{4,0},{5,1},{6,2},{7,3},{8,12},{9,13},{10,... | collective-permute-start | bytes 1572872 | tf_op jit(solution)/shard_map/ppermute | solution.py:531
  68.3 7.3 %experts.5 = bf16[256,1024]{1,0:T(8,128)(2,1)S(1)} custom-call(bf16[128,1024]{1,0:T(8,128)(2,1)S(1)} %collective-permute-done.19.refs_0_, bf16[144,1024]{1,0:T(8,128)(2,1)S(1)} %collective-permute-done.20.refs_1_, bf16[4,1024,512]{2,1,0:T(8,128)(2,1)S(1)} %copy-done, bf16[4,1024,512]{2,1,0:T(8,128)(2,1)S(1)} %copy-done.1, ...), custom_call_target="tpu_custom_call" | custom-call | flops 12582912000 | bytes 31457280 | tf_op jit(solution)/shard_map/experts/pallas_call | solution.py:510
  75.7 1.5 %collective-permute-start.23 = (bf16[256,1024]{1,0:T(8,128)(2,1)S(1)}, bf16[256,1024]{1,0:T(8,128)(2,1)S(1)}, u32[]{:S(2)}, u32[]{:S(2)}) collective-permute-start(bf16[256,1024]{1,0:T(8,128)(2,1)S(1)} %experts.5), channel_id=1, source_target_pairs={{0,6},{1,7},{2,4},{3,5},{4,2},{5,3},{6,0},{7,1},{8,14},{9,15},{10,... | collective-permute-start | bytes 1572872 | tf_op jit(solution)/shard_map/ppermute | solution.py:531
  77.2 3.8 %collective-permute-done.21 = bf16[256,1024]{1,0:T(8,128)(2,1)S(1)} collective-permute-done((bf16[256,1024]{1,0:T(8,128)(2,1)S(1)}, bf16[256,1024]{1,0:T(8,128)(2,1)S(1)}, u32[]{:S(2)}, u32[]{:S(2)}) %collective-permute-start.21) | collective-permute-done | bytes 524320 | tf_op jit(solution)/shard_map/ppermute | solution.py:531
  81.2 9.5 %collective-permute-done.23 = bf16[256,1024]{1,0:T(8,128)(2,1)S(1)} collective-permute-done((bf16[256,1024]{1,0:T(8,128)(2,1)S(1)}, bf16[256,1024]{1,0:T(8,128)(2,1)S(1)}, u32[]{:S(2)}, u32[]{:S(2)}) %collective-permute-start.23) | collective-permute-done | bytes 524320 | tf_op jit(solution)/shard_map/ppermute | solution.py:531
  90.7 0.9 %fusion = bf16[1,256,1024]{2,1,0:T(8,128)(2,1)} fusion(f32[256,1024]{1,0:T(8,128)S(1)} %convert_add_fusion, bf16[256,1024]{1,0:T(8,128)(2,1)S(1)} %collective-permute-done.23), kind=kLoop, calls=%fused_computation.2 | loop fusion | flops 786432 | bytes 2097152 | tf_op jit(solution)/shard_map/broadcast_in_dim | solution.py:601
  (32 shorter events, 2.9 us)
Async XLA Ops:
  0.6 5.5 %collective-permute-start = (bf16[256,512]{1,0:T(8,128)(2,1)}, bf16[256,512]{1,0:T(8,128)(2,1)S(1)}, u32[]{:S(2)}, u32[]{:S(2)}) collective-permute-start(bf16[256,512]{1,0:T(8,128)(2,1)} %bitcast.17), channel_id=1, source_target_pairs={{0,1},{1,0},{2,3},{3,2},{4,5},{5,4},{6,7},{7,6},{8,9},{9,8},{10,11... | collective-permute-start | bytes 786440 | tf_op jit(solution)/shard_map/ppermute | solution.py:531
  1.2 5.1 %collective-permute-start.1 = (bf16[256,512]{1,0:T(8,128)(2,1)}, bf16[256,512]{1,0:T(8,128)(2,1)S(1)}, u32[]{:S(2)}, u32[]{:S(2)}) collective-permute-start(bf16[256,512]{1,0:T(8,128)(2,1)} %bitcast.21), channel_id=1, source_target_pairs={{0,1},{1,0},{2,3},{3,2},{4,5},{5,4},{6,7},{7,6},{8,9},{9,8},{10,11... | collective-permute-start | bytes 786440 | tf_op jit(solution)/shard_map/ppermute | solution.py:531
  1.2 13.6 %collective-permute-start.4 = (bf16[256,512]{1,0:T(8,128)(2,1)}, bf16[256,512]{1,0:T(8,128)(2,1)S(1)}, u32[]{:S(2)}, u32[]{:S(2)}) collective-permute-start(bf16[256,512]{1,0:T(8,128)(2,1)} %bitcast.18), channel_id=1, source_target_pairs={{0,4},{1,5},{2,6},{3,7},{4,0},{5,1},{6,2},{7,3},{8,12},{9,13},{10,... | collective-permute-start | bytes 786440 | tf_op jit(solution)/shard_map/ppermute | solution.py:531
  4.2 10.7 %collective-permute-start.2 = (bf16[256,512]{1,0:T(8,128)(2,1)}, bf16[256,512]{1,0:T(8,128)(2,1)S(1)}, u32[]{:S(2)}, u32[]{:S(2)}) collective-permute-start(bf16[256,512]{1,0:T(8,128)(2,1)} %bitcast.19), channel_id=1, source_target_pairs={{0,2},{1,3},{2,0},{3,1},{4,6},{5,7},{6,4},{7,5},{8,10},{9,11},{10,... | collective-permute-start | bytes 786440 | tf_op jit(solution)/shard_map/ppermute | solution.py:531
  5.7 10.9 %collective-permute-start.5 = (bf16[256,512]{1,0:T(8,128)(2,1)}, bf16[256,512]{1,0:T(8,128)(2,1)S(1)}, u32[]{:S(2)}, u32[]{:S(2)}) collective-permute-start(bf16[256,512]{1,0:T(8,128)(2,1)} %bitcast.22), channel_id=1, source_target_pairs={{0,4},{1,5},{2,6},{3,7},{4,0},{5,1},{6,2},{7,3},{8,12},{9,13},{10,... | collective-permute-start | bytes 786440 | tf_op jit(solution)/shard_map/ppermute | solution.py:531
  6.2 11.8 %collective-permute-start.3 = (bf16[256,512]{1,0:T(8,128)(2,1)}, bf16[256,512]{1,0:T(8,128)(2,1)S(1)}, u32[]{:S(2)}, u32[]{:S(2)}) collective-permute-start(bf16[256,512]{1,0:T(8,128)(2,1)} %bitcast.23), channel_id=1, source_target_pairs={{0,2},{1,3},{2,0},{3,1},{4,6},{5,7},{6,4},{7,5},{8,10},{9,11},{10,... | collective-permute-start | bytes 786440 | tf_op jit(solution)/shard_map/ppermute | solution.py:531
  6.2 14.5 %copy-start = (bf16[4,1024,512]{2,1,0:T(8,128)(2,1)S(1)}, bf16[4,1024,512]{2,1,0:T(8,128)(2,1)}, u32[]{:S(2)}) copy-start(bf16[4,1024,512]{2,1,0:T(8,128)(2,1)} %refs_2_.4) | copy-start | bytes 12582916
  18.0 1.5 %collective-permute-start.9 = (bf16[256,512]{1,0:T(8,128)(2,1)S(1)}, bf16[256,512]{1,0:T(8,128)(2,1)S(1)}, u32[]{:S(2)}, u32[]{:S(2)}) collective-permute-start(bf16[256,512]{1,0:T(8,128)(2,1)S(1)} %collective-permute-done.3.refs_7_), channel_id=1, source_target_pairs={{0,1},{1,0},{2,3},{3,2},{4,5},{5,4},{6,7},{7,6},{8,9},{9,8},{10,11... | collective-permute-start | bytes 786440 | tf_op jit(solution)/shard_map/ppermute | solution.py:531
  18.0 1.9 %collective-permute-start.10 = (bf16[256,512]{1,0:T(8,128)(2,1)S(1)}, bf16[256,512]{1,0:T(8,128)(2,1)S(1)}, u32[]{:S(2)}, u32[]{:S(2)}) collective-permute-start(bf16[256,512]{1,0:T(8,128)(2,1)S(1)} %collective-permute-done.4.refs_4_), channel_id=1, source_target_pairs={{0,1},{1,0},{2,3},{3,2},{4,5},{5,4},{6,7},{7,6},{8,9},{9,8},{10,11... | collective-permute-start | bytes 786440 | tf_op jit(solution)/shard_map/ppermute | solution.py:531
  18.5 1.8 %collective-permute-start.8 = (bf16[256,512]{1,0:T(8,128)(2,1)S(1)}, bf16[256,512]{1,0:T(8,128)(2,1)S(1)}, u32[]{:S(2)}, u32[]{:S(2)}) collective-permute-start(bf16[256,512]{1,0:T(8,128)(2,1)S(1)} %collective-permute-done.2.refs_3_), channel_id=1, source_target_pairs={{0,1},{1,0},{2,3},{3,2},{4,5},{5,4},{6,7},{7,6},{8,9},{9,8},{10,11... | collective-permute-start | bytes 786440 | tf_op jit(solution)/shard_map/ppermute | solution.py:531
  18.5 2.1 %collective-permute-start.11 = (bf16[256,512]{1,0:T(8,128)(2,1)S(1)}, bf16[256,512]{1,0:T(8,128)(2,1)S(1)}, u32[]{:S(2)}, u32[]{:S(2)}) collective-permute-start(bf16[256,512]{1,0:T(8,128)(2,1)S(1)} %collective-permute-done.5.refs_8_), channel_id=1, source_target_pairs={{0,1},{1,0},{2,3},{3,2},{4,5},{5,4},{6,7},{7,6},{8,9},{9,8},{10,11... | collective-permute-start | bytes 786440 | tf_op jit(solution)/shard_map/ppermute | solution.py:531
  20.7 8.7 %collective-permute-start.12 = (bf16[4,1024,512]{2,1,0:T(8,128)(2,1)S(1)}, bf16[4,1024,512]{2,1,0:T(8,128)(2,1)S(1)}, u32[]{:S(2)}, u32[]{:S(2)}) collective-permute-start(bf16[4,1024,512]{2,1,0:T(8,128)(2,1)S(1)} %copy-done), channel_id=1, source_target_pairs={{0,1},{1,0},{2,3},{3,2},{4,5},{5,4},{6,7},{7,6},{8,9},{9,8},{10,11... | collective-permute-start | bytes 12582920 | tf_op jit(solution)/shard_map/ppermute | solution.py:531
  20.8 8.6 %collective-permute-start.6 = (bf16[256,512]{1,0:T(8,128)(2,1)S(1)}, bf16[256,512]{1,0:T(8,128)(2,1)S(1)}, u32[]{:S(2)}, u32[]{:S(2)}) collective-permute-start(bf16[256,512]{1,0:T(8,128)(2,1)S(1)} %collective-permute-done.2.refs_3_), channel_id=1, source_target_pairs={{0,4},{1,5},{2,6},{3,7},{4,0},{5,1},{6,2},{7,3},{8,12},{9,13},{10,... | collective-permute-start | bytes 786440 | tf_op jit(solution)/shard_map/ppermute | solution.py:531
  21.1 8.3 %collective-permute-start.7 = (bf16[256,512]{1,0:T(8,128)(2,1)S(1)}, bf16[256,512]{1,0:T(8,128)(2,1)S(1)}, u32[]{:S(2)}, u32[]{:S(2)}) collective-permute-start(bf16[256,512]{1,0:T(8,128)(2,1)S(1)} %collective-permute-done.5.refs_8_), channel_id=1, source_target_pairs={{0,2},{1,3},{2,0},{3,1},{4,6},{5,7},{6,4},{7,5},{8,10},{9,11},{10,... | collective-permute-start | bytes 786440 | tf_op jit(solution)/shard_map/ppermute | solution.py:531
  22.8 8.5 %copy-start.1 = (bf16[4,1024,512]{2,1,0:T(8,128)(2,1)S(1)}, bf16[4,1024,512]{2,1,0:T(8,128)(2,1)}, u32[]{:S(2)}) copy-start(bf16[4,1024,512]{2,1,0:T(8,128)(2,1)} %refs_3_.4) | copy-start | bytes 12582916
  22.8 8.6 %copy-start.2 = (bf16[4,512,1024]{2,1,0:T(8,128)(2,1)S(1)}, bf16[4,512,1024]{2,1,0:T(8,128)(2,1)}, u32[]{:S(2)}) copy-start(bf16[4,512,1024]{2,1,0:T(8,128)(2,1)} %refs_4_.3) | copy-start | bytes 12582916
  29.4 1.5 %collective-permute-start.13 = (bf16[256,512]{1,0:T(8,128)(2,1)S(1)}, bf16[256,512]{1,0:T(8,128)(2,1)S(1)}, u32[]{:S(2)}, u32[]{:S(2)}) collective-permute-start(bf16[256,512]{1,0:T(8,128)(2,1)S(1)} %collective-permute-done.6.refs_3_), channel_id=1, source_target_pairs={{0,1},{1,0},{2,3},{3,2},{4,5},{5,4},{6,7},{7,6},{8,9},{9,8},{10,11... | collective-permute-start | bytes 786440 | tf_op jit(solution)/shard_map/ppermute | solution.py:531
  29.4 1.9 %collective-permute-start.14 = (bf16[256,512]{1,0:T(8,128)(2,1)S(1)}, bf16[256,512]{1,0:T(8,128)(2,1)S(1)}, u32[]{:S(2)}, u32[]{:S(2)}) collective-permute-start(bf16[256,512]{1,0:T(8,128)(2,1)S(1)} %collective-permute-done.7.refs_5_), channel_id=1, source_target_pairs={{0,1},{1,0},{2,3},{3,2},{4,5},{5,4},{6,7},{7,6},{8,9},{9,8},{10,11... | collective-permute-start | bytes 786440 | tf_op jit(solution)/shard_map/ppermute | solution.py:531
  31.3 10.0 %collective-permute-start.17 = (bf16[4,1024,512]{2,1,0:T(8,128)(2,1)S(1)}, bf16[4,1024,512]{2,1,0:T(8,128)(2,1)S(1)}, u32[]{:S(2)}, u32[]{:S(2)}) collective-permute-start(bf16[4,1024,512]{2,1,0:T(8,128)(2,1)S(1)} %copy-done.1), channel_id=1, source_target_pairs={{0,1},{1,0},{2,3},{3,2},{4,5},{5,4},{6,7},{7,6},{8,9},{9,8},{10,11... | collective-permute-start | bytes 12582920 | tf_op jit(solution)/shard_map/ppermute | solution.py:531
  31.5 13.0 %collective-permute-start.18 = (bf16[4,512,1024]{2,1,0:T(8,128)(2,1)S(1)}, bf16[4,512,1024]{2,1,0:T(8,128)(2,1)S(1)}, u32[]{:S(2)}, u32[]{:S(2)}) collective-permute-start(bf16[4,512,1024]{2,1,0:T(8,128)(2,1)S(1)} %copy-done.2), channel_id=1, source_target_pairs={{0,1},{1,0},{2,3},{3,2},{4,5},{5,4},{6,7},{7,6},{8,9},{9,8},{10,11... | collective-permute-start | bytes 12582920 | tf_op jit(solution)/shard_map/ppermute | solution.py:531
  38.1 14.7 %collective-permute-start.16 = (bf16[272,1024]{1,0:T(8,128)(2,1)S(1)}, bf16[272,1024]{1,0:T(8,128)(2,1)S(1)}, u32[]{:S(2)}, u32[]{:S(2)}) collective-permute-start(bf16[272,1024]{1,0:T(8,128)(2,1)S(1)} %get-tuple-element.67.refs_0_), channel_id=1, source_target_pairs={{0,4},{1,5},{2,6},{3,7},{4,0},{5,1},{6,2},{7,3},{8,12},{9,13},{10,... | collective-permute-start | bytes 1671176 | tf_op jit(solution)/shard_map/ppermute | solution.py:531
  39.9 14.4 %collective-permute-start.15 = (bf16[272,1024]{1,0:T(8,128)(2,1)S(1)}, bf16[272,1024]{1,0:T(8,128)(2,1)S(1)}, u32[]{:S(2)}, u32[]{:S(2)}) collective-permute-start(bf16[272,1024]{1,0:T(8,128)(2,1)S(1)} %get-tuple-element.67.refs_0_), channel_id=1, source_target_pairs={{0,2},{1,3},{2,0},{3,1},{4,6},{5,7},{6,4},{7,5},{8,10},{9,11},{10,... | collective-permute-start | bytes 1671176 | tf_op jit(solution)/shard_map/ppermute | solution.py:531
  54.3 11.9 %collective-permute-start.19 = (bf16[128,1024]{1,0:T(8,128)(2,1)S(1)}, bf16[128,1024]{1,0:T(8,128)(2,1)S(1)}, u32[]{:S(2)}, u32[]{:S(2)}) collective-permute-start(bf16[128,1024]{1,0:T(8,128)(2,1)S(1)} %slice.6), channel_id=1, source_target_pairs={{0,4},{1,5},{2,6},{3,7},{4,0},{5,1},{6,2},{7,3},{8,12},{9,13},{10,... | collective-permute-start | bytes 786440 | tf_op jit(solution)/shard_map/ppermute | solution.py:531
  54.7 11.6 %collective-permute-start.20 = (bf16[144,1024]{1,0:T(8,128)(2,1)S(1)}, bf16[144,1024]{1,0:T(8,128)(2,1)S(1)}, u32[]{:S(2)}, u32[]{:S(2)}) collective-permute-start(bf16[144,1024]{1,0:T(8,128)(2,1)S(1)} %slice.7), channel_id=1, source_target_pairs={{0,2},{1,3},{2,0},{3,1},{4,6},{5,7},{6,4},{7,5},{8,10},{9,11},{10,... | collective-permute-start | bytes 884744 | tf_op jit(solution)/shard_map/ppermute | solution.py:531
  66.2 14.8 %collective-permute-start.21 = (bf16[256,1024]{1,0:T(8,128)(2,1)S(1)}, bf16[256,1024]{1,0:T(8,128)(2,1)S(1)}, u32[]{:S(2)}, u32[]{:S(2)}) collective-permute-start(bf16[256,1024]{1,0:T(8,128)(2,1)S(1)} %get-tuple-element.77), channel_id=1, source_target_pairs={{0,2},{1,3},{2,0},{3,1},{4,6},{5,7},{6,4},{7,5},{8,10},{9,11},{10,... | collective-permute-start | bytes 1572872 | tf_op jit(solution)/shard_map/ppermute | solution.py:531
  66.6 14.4 %collective-permute-start.22 = (bf16[256,1024]{1,0:T(8,128)(2,1)S(1)}, bf16[256,1024]{1,0:T(8,128)(2,1)S(1)}, u32[]{:S(2)}, u32[]{:S(2)}) collective-permute-start(bf16[256,1024]{1,0:T(8,128)(2,1)S(1)} %get-tuple-element.78), channel_id=1, source_target_pairs={{0,4},{1,5},{2,6},{3,7},{4,0},{5,1},{6,2},{7,3},{8,12},{9,13},{10,... | collective-permute-start | bytes 1572872 | tf_op jit(solution)/shard_map/ppermute | solution.py:531
  75.7 15.1 %collective-permute-start.23 = (bf16[256,1024]{1,0:T(8,128)(2,1)S(1)}, bf16[256,1024]{1,0:T(8,128)(2,1)S(1)}, u32[]{:S(2)}, u32[]{:S(2)}) collective-permute-start(bf16[256,1024]{1,0:T(8,128)(2,1)S(1)} %experts.5), channel_id=1, source_target_pairs={{0,6},{1,7},{2,4},{3,5},{4,2},{5,3},{6,0},{7,1},{8,14},{9,15},{10,... | collective-permute-start | bytes 1572872 | tf_op jit(solution)/shard_map/ppermute | solution.py:531

commit v7 on v6

--- a/solution.py
+++ b/solution.py
@@ -488,7 +488,7 @@
         return carry
 
     for group in range(len(owners)):
-        lax.fori_loop(0, local_experts, functools.partial(one_expert, group), 0)
+        lax.fori_loop(0, local_experts, functools.partial(one_expert, group), 0, unroll=4)
     for source, ref in enumerate(out_refs):
         ref[...] = dot_tn(combine_ref[source], made_ref[source]).astype(ref.dtype)
 

time: 91.8 us -> 90.5 us (0.986)
  Pallas kernels: 45.2 us -> 41.2 us
  waiting for transfers between devices: 25.8 us -> 28.4 us
    pallas_call x3, Pallas kernels: 24.4 us -> 20.3 us  [run_experts(): pl.pallas_call(functools.partial(experts_kernel, sources, pieces, owners,...]
    ppermute x24, waiting for transfers between devices: 25.8 us -> 28.4 us  [swap(): lax.ppermute(array, 'req', [(i, i ^ mask) for i in range(lax.axis_size('r...]
  transfers between devices with their start and end apart: 24 -> 24, of which waited for: 14 -> 14; matrix products, arithmetic and copies ran while one was open for 0% -> 0% of each run, Pallas kernels for 49% -> 46%
where the time goes in v7:
time: 90.5 us; the launch traced here: 90.3 us
  Pallas kernels  41.2 us (46%)
  waiting for transfers between devices  28.4 us (31%)
  starting transfers between devices  18.7 us (21%)
  other arithmetic  1.18 us (1%)
    ppermute x24, waiting for transfers between devices, swap(): lax.ppermute(array, 'req', [(i, i ^ mask) for i in range(lax.axis_size('r...  28.4 us
    pallas_call x3, Pallas kernels, run_experts(): pl.pallas_call(functools.partial(experts_kernel, sources, pieces, owners,...  20.3 us
    ppermute x24, starting transfers between devices, swap(): lax.ppermute(array, 'req', [(i, i ^ mask) for i in range(lax.axis_size('r...  18.7 us
    pallas_call x2, Pallas kernels, attend_far(): pl.pallas_call(functools.partial(far_kernel, blocks, last), grid=(1,), in...  12.2 us
    pallas_call x1, Pallas kernels, attend_near(): pl.pallas_call(near_kernel, grid=(1,), in_specs=[whole_spec(tok_count, wi...  8.65 us
  transfers between devices with their start and end apart: 24, of which 14 were waited for; matrix products, arithmetic and copies ran while one was open for 0% of the time, Pallas kernels for 46%

profile of v7, /device:TPU:0, one launch (start us, length us, event | category | flops | bytes accessed | tf_op | source)
XLA Modules:
  0.0 90.3 jit_solution(11298615240630514243)
XLA Ops:
  0.6 0.5 collective-permute-start
  1.2 2.9 %collective-permute-start.4 = (bf16[256,512]{1,0:T(8,128)(2,1)}, bf16[256,512]{1,0:T(8,128)(2,1)S(1)}, u32[]{:S(2)}, u32[]{:S(2)}) collective-permute-start(bf16[256,512]{1,0:T(8,128)(2,1)} %bitcast.18), channel_id=1, source_target_pairs={{0,4},{1,5},{2,6},{3,7},{4,0},{5,1},{6,2},{7,3},{8,12},{9,13},{10,... | collective-permute-start | bytes 786440 | tf_op jit(solution)/shard_map/ppermute | solution.py:531
  4.2 1.5 %collective-permute-start.2 = (bf16[256,512]{1,0:T(8,128)(2,1)}, bf16[256,512]{1,0:T(8,128)(2,1)S(1)}, u32[]{:S(2)}, u32[]{:S(2)}) collective-permute-start(bf16[256,512]{1,0:T(8,128)(2,1)} %bitcast.19), channel_id=1, source_target_pairs={{0,2},{1,3},{2,0},{3,1},{4,6},{5,7},{6,4},{7,5},{8,10},{9,11},{10,... | collective-permute-start | bytes 786440 | tf_op jit(solution)/shard_map/ppermute | solution.py:531
  5.7 0.5 collective-permute-start.5
  6.2 8.6 %attend_near.1 = (bf16[8,512,128]{2,1,0:T(8,128)(2,1)S(1)}, f32[8,1,512]{2,1,0:T(1,128)S(1)}, f32[8,80,512]{2,1,0:T(8,128)S(1)}) custom-call(bf16[256,1024]{1,0:T(8,128)(2,1)} %bitcast.15, f32[1,1024]{1,0:T(1,128)} %bitcast.27, bf16[1024,1024]{1,0:T(8,128)(2,1)} %refs_2_.1, bf16[1024,512]{1,0:T(8,128)(2,1)} %refs_3_.1, bf16[1024,512]{1,0:T(8,128)(2,1)} %refs_4_.1, ...), custom_call_target="tpu_custom_call" | custom-call | flops 4194304000 | bytes 6291456 | tf_op jit(solution)/shard_map/attend_near/pallas_call | solution.py:334
  14.9 1.7 %collective-permute-done.5.refs_8_ = bf16[256,512]{1,0:T(8,128)(2,1)S(1)} collective-permute-done((bf16[256,512]{1,0:T(8,128)(2,1)}, bf16[256,512]{1,0:T(8,128)(2,1)S(1)}, u32[]{:S(2)}, u32[]{:S(2)}) %collective-permute-start.5) | collective-permute-done | bytes 262176 | tf_op jit(solution)/shard_map/ppermute | solution.py:531
  16.6 1.5 %collective-permute-done.3.refs_7_ = bf16[256,512]{1,0:T(8,128)(2,1)S(1)} collective-permute-done((bf16[256,512]{1,0:T(8,128)(2,1)}, bf16[256,512]{1,0:T(8,128)(2,1)S(1)}, u32[]{:S(2)}, u32[]{:S(2)}) %collective-permute-start.3) | collective-permute-done | bytes 262176 | tf_op jit(solution)/shard_map/ppermute | solution.py:531
  18.0 0.5 collective-permute-start.10
  18.5 0.5 collective-permute-start.11
  19.0 0.5 collective-permute-done.9.refs_9_
  19.9 0.4 collective-permute-done.8.refs_5_
  21.1 1.7 %collective-permute-start.7 = (bf16[256,512]{1,0:T(8,128)(2,1)S(1)}, bf16[256,512]{1,0:T(8,128)(2,1)S(1)}, u32[]{:S(2)}, u32[]{:S(2)}) collective-permute-start(bf16[256,512]{1,0:T(8,128)(2,1)S(1)} %collective-permute-done.5.refs_8_), channel_id=1, source_target_pairs={{0,2},{1,3},{2,0},{3,1},{4,6},{5,7},{6,4},{7,5},{8,10},{9,11},{10,... | collective-permute-start | bytes 786440 | tf_op jit(solution)/shard_map/ppermute | solution.py:531
  22.8 5.9 %attend_far.2 = (f32[8,1,512]{2,1,0:T(1,128)S(1)}, f32[8,80,512]{2,1,0:T(8,128)S(1)}) custom-call(bf16[8,512,128]{2,1,0:T(8,128)(2,1)S(1)} %get-tuple-element.43.refs_0_, f32[8,1,512]{2,1,0:T(1,128)S(1)} %get-tuple-element.51.refs_1_, f32[8,80,512]{2,1,0:T(8,128)S(1)} %get-tuple-element.52.refs_2_, bf16[256,512]{1,0:T(8,128)(2,1)S(1)} %collective-permute-done.2.refs_3_, ...), custom_call_target="tpu_custom_call" | custom-call | flops 5033164800 | bytes 4194304 | tf_op jit(solution)/shard_map/attend_far/pallas_call | solution.py:411
  28.8 0.6 collective-permute-done.6.refs_3_
  29.4 0.5 collective-permute-start.14
  29.9 1.0 %collective-permute-done.13.refs_4_ = bf16[256,512]{1,0:T(8,128)(2,1)S(1)} collective-permute-done((bf16[256,512]{1,0:T(8,128)(2,1)S(1)}, bf16[256,512]{1,0:T(8,128)(2,1)S(1)}, u32[]{:S(2)}, u32[]{:S(2)}) %collective-permute-start.13) | collective-permute-done | bytes 262176 | tf_op jit(solution)/shard_map/ppermute | solution.py:531
  31.8 6.3 %attend_far.3 = (bf16[256,1024]{1,0:T(8,128)(2,1)}, bf16[256,1024]{1,0:T(8,128)(2,1)}, bf16[272,1024]{1,0:T(8,128)(2,1)S(1)}) custom-call(bf16[8,512,128]{2,1,0:T(8,128)(2,1)S(1)} %get-tuple-element.43.refs_0_, f32[8,1,512]{2,1,0:T(1,128)S(1)} %get-tuple-element.59.refs_1_, f32[8,80,512]{2,1,0:T(8,128)S(1)} %get-tuple-element.60.refs_2_, ...), custom_call_target="tpu_custom_call" | custom-call | flops 2516582400 | bytes 4194304 | tf_op jit(solution)/shard_map/attend_far/pallas_call | solution.py:411
  38.1 1.7 %collective-permute-start.16 = (bf16[272,1024]{1,0:T(8,128)(2,1)S(1)}, bf16[272,1024]{1,0:T(8,128)(2,1)S(1)}, u32[]{:S(2)}, u32[]{:S(2)}) collective-permute-start(bf16[272,1024]{1,0:T(8,128)(2,1)S(1)} %get-tuple-element.67.refs_0_), channel_id=1, source_target_pairs={{0,4},{1,5},{2,6},{3,7},{4,0},{5,1},{6,2},{7,3},{8,12},{9,13},{10,... | collective-permute-start | bytes 1671176 | tf_op jit(solution)/shard_map/ppermute | solution.py:531
  39.9 1.5 %collective-permute-start.15 = (bf16[272,1024]{1,0:T(8,128)(2,1)S(1)}, bf16[272,1024]{1,0:T(8,128)(2,1)S(1)}, u32[]{:S(2)}, u32[]{:S(2)}) collective-permute-start(bf16[272,1024]{1,0:T(8,128)(2,1)S(1)} %get-tuple-element.67.refs_0_), channel_id=1, source_target_pairs={{0,2},{1,3},{2,0},{3,1},{4,6},{5,7},{6,4},{7,5},{8,10},{9,11},{10,... | collective-permute-start | bytes 1671176 | tf_op jit(solution)/shard_map/ppermute | solution.py:531
  41.4 3.1 %collective-permute-done.18.refs_6_.refs_7_ = bf16[4,512,1024]{2,1,0:T(8,128)(2,1)S(1)} collective-permute-done((bf16[4,512,1024]{2,1,0:T(8,128)(2,1)S(1)}, bf16[4,512,1024]{2,1,0:T(8,128)(2,1)S(1)}, u32[]{:S(2)}, u32[]{:S(2)}) %collective-permute-start.18) | collective-permute-done | bytes 4194336 | tf_op jit(solution)/shard_map/ppermute | solution.py:531
  44.5 6.0 %experts.3 = f32[256,1024]{1,0:T(8,128)S(1)} custom-call(bf16[272,1024]{1,0:T(8,128)(2,1)S(1)} %get-tuple-element.67.refs_0_, bf16[4,1024,512]{2,1,0:T(8,128)(2,1)S(1)} %copy-done, bf16[4,1024,512]{2,1,0:T(8,128)(2,1)S(1)} %copy-done.1, bf16[4,512,1024]{2,1,0:T(8,128)(2,1)S(1)} %copy-done.2, ...), custom_call_target="tpu_custom_call" | custom-call | flops 12582912000 | bytes 31457280 | tf_op jit(solution)/shard_map/experts/pallas_call | solution.py:510
  50.5 2.3 %collective-permute-done.16.refs_1_ = bf16[272,1024]{1,0:T(8,128)(2,1)S(1)} collective-permute-done((bf16[272,1024]{1,0:T(8,128)(2,1)S(1)}, bf16[272,1024]{1,0:T(8,128)(2,1)S(1)}, u32[]{:S(2)}, u32[]{:S(2)}) %collective-permute-start.16) | collective-permute-done | bytes 557088 | tf_op jit(solution)/shard_map/ppermute | solution.py:531
  52.8 1.5 %collective-permute-done.15.refs_0_ = bf16[272,1024]{1,0:T(8,128)(2,1)S(1)} collective-permute-done((bf16[272,1024]{1,0:T(8,128)(2,1)S(1)}, bf16[272,1024]{1,0:T(8,128)(2,1)S(1)}, u32[]{:S(2)}, u32[]{:S(2)}) %collective-permute-start.15) | collective-permute-done | bytes 557088 | tf_op jit(solution)/shard_map/ppermute | solution.py:531
  54.7 1.8 %collective-permute-start.20 = (bf16[144,1024]{1,0:T(8,128)(2,1)S(1)}, bf16[144,1024]{1,0:T(8,128)(2,1)S(1)}, u32[]{:S(2)}, u32[]{:S(2)}) collective-permute-start(bf16[144,1024]{1,0:T(8,128)(2,1)S(1)} %slice.7), channel_id=1, source_target_pairs={{0,2},{1,3},{2,0},{3,1},{4,6},{5,7},{6,4},{7,5},{8,10},{9,11},{10,... | collective-permute-start | bytes 884744 | tf_op jit(solution)/shard_map/ppermute | solution.py:531
  56.4 8.4 %experts.4 = (bf16[256,1024]{1,0:T(8,128)(2,1)S(1)}, bf16[256,1024]{1,0:T(8,128)(2,1)S(1)}) custom-call(bf16[272,1024]{1,0:T(8,128)(2,1)S(1)} %collective-permute-done.15.refs_0_, bf16[272,1024]{1,0:T(8,128)(2,1)S(1)} %collective-permute-done.16.refs_1_, bf16[4,1024,512]{2,1,0:T(8,128)(2,1)S(1)} %copy-done, bf16[4,1024,512]{2,1,0:T(8,128)(2,1)S(1)} %copy-done.1, ...), custom_call_target="tpu_custom_call" | custom-call | flops 12582912000 | bytes 31457280 | tf_op jit(solution)/shard_map/experts/pallas_call | solution.py:510
  64.8 0.4 collective-permute-start.21
  65.2 1.7 %collective-permute-start.22 = (bf16[256,1024]{1,0:T(8,128)(2,1)S(1)}, bf16[256,1024]{1,0:T(8,128)(2,1)S(1)}, u32[]{:S(2)}, u32[]{:S(2)}) collective-permute-start(bf16[256,1024]{1,0:T(8,128)(2,1)S(1)} %get-tuple-element.78), channel_id=1, source_target_pairs={{0,4},{1,5},{2,6},{3,7},{4,0},{5,1},{6,2},{7,3},{8,12},{9,13},{10,... | collective-permute-start | bytes 1572872 | tf_op jit(solution)/shard_map/ppermute | solution.py:531
  67.0 6.0 %experts.5 = bf16[256,1024]{1,0:T(8,128)(2,1)S(1)} custom-call(bf16[128,1024]{1,0:T(8,128)(2,1)S(1)} %collective-permute-done.19.refs_0_, bf16[144,1024]{1,0:T(8,128)(2,1)S(1)} %collective-permute-done.20.refs_1_, bf16[4,1024,512]{2,1,0:T(8,128)(2,1)S(1)} %copy-done, bf16[4,1024,512]{2,1,0:T(8,128)(2,1)S(1)} %copy-done.1, ...), custom_call_target="tpu_custom_call" | custom-call | flops 12582912000 | bytes 31457280 | tf_op jit(solution)/shard_map/experts/pallas_call | solution.py:510
  72.9 1.5 %collective-permute-start.23 = (bf16[256,1024]{1,0:T(8,128)(2,1)S(1)}, bf16[256,1024]{1,0:T(8,128)(2,1)S(1)}, u32[]{:S(2)}, u32[]{:S(2)}) collective-permute-start(bf16[256,1024]{1,0:T(8,128)(2,1)S(1)} %experts.5), channel_id=1, source_target_pairs={{0,6},{1,7},{2,4},{3,5},{4,2},{5,3},{6,0},{7,1},{8,14},{9,15},{10,... | collective-permute-start | bytes 1572872 | tf_op jit(solution)/shard_map/ppermute | solution.py:531
  74.4 5.3 %collective-permute-done.21 = bf16[256,1024]{1,0:T(8,128)(2,1)S(1)} collective-permute-done((bf16[256,1024]{1,0:T(8,128)(2,1)S(1)}, bf16[256,1024]{1,0:T(8,128)(2,1)S(1)}, u32[]{:S(2)}, u32[]{:S(2)}) %collective-permute-start.21) | collective-permute-done | bytes 524320 | tf_op jit(solution)/shard_map/ppermute | solution.py:531
  80.0 9.3 %collective-permute-done.23 = bf16[256,1024]{1,0:T(8,128)(2,1)S(1)} collective-permute-done((bf16[256,1024]{1,0:T(8,128)(2,1)S(1)}, bf16[256,1024]{1,0:T(8,128)(2,1)S(1)}, u32[]{:S(2)}, u32[]{:S(2)}) %collective-permute-start.23) | collective-permute-done | bytes 524320 | tf_op jit(solution)/shard_map/ppermute | solution.py:531
  89.4 0.9 %fusion = bf16[1,256,1024]{2,1,0:T(8,128)(2,1)} fusion(f32[256,1024]{1,0:T(8,128)S(1)} %convert_add_fusion, bf16[256,1024]{1,0:T(8,128)(2,1)S(1)} %collective-permute-done.23), kind=kLoop, calls=%fused_computation.2 | loop fusion | flops 786432 | bytes 2097152 | tf_op jit(solution)/shard_map/broadcast_in_dim | solution.py:601
  (32 shorter events, 2.9 us)
Async XLA Ops:
  0.6 5.5 %collective-permute-start = (bf16[256,512]{1,0:T(8,128)(2,1)}, bf16[256,512]{1,0:T(8,128)(2,1)S(1)}, u32[]{:S(2)}, u32[]{:S(2)}) collective-permute-start(bf16[256,512]{1,0:T(8,128)(2,1)} %bitcast.17), channel_id=1, source_target_pairs={{0,1},{1,0},{2,3},{3,2},{4,5},{5,4},{6,7},{7,6},{8,9},{9,8},{10,11... | collective-permute-start | bytes 786440 | tf_op jit(solution)/shard_map/ppermute | solution.py:531
  1.2 5.1 %collective-permute-start.1 = (bf16[256,512]{1,0:T(8,128)(2,1)}, bf16[256,512]{1,0:T(8,128)(2,1)S(1)}, u32[]{:S(2)}, u32[]{:S(2)}) collective-permute-start(bf16[256,512]{1,0:T(8,128)(2,1)} %bitcast.21), channel_id=1, source_target_pairs={{0,1},{1,0},{2,3},{3,2},{4,5},{5,4},{6,7},{7,6},{8,9},{9,8},{10,11... | collective-permute-start | bytes 786440 | tf_op jit(solution)/shard_map/ppermute | solution.py:531
  1.2 13.6 %collective-permute-start.4 = (bf16[256,512]{1,0:T(8,128)(2,1)}, bf16[256,512]{1,0:T(8,128)(2,1)S(1)}, u32[]{:S(2)}, u32[]{:S(2)}) collective-permute-start(bf16[256,512]{1,0:T(8,128)(2,1)} %bitcast.18), channel_id=1, source_target_pairs={{0,4},{1,5},{2,6},{3,7},{4,0},{5,1},{6,2},{7,3},{8,12},{9,13},{10,... | collective-permute-start | bytes 786440 | tf_op jit(solution)/shard_map/ppermute | solution.py:531
  4.2 10.7 %collective-permute-start.2 = (bf16[256,512]{1,0:T(8,128)(2,1)}, bf16[256,512]{1,0:T(8,128)(2,1)S(1)}, u32[]{:S(2)}, u32[]{:S(2)}) collective-permute-start(bf16[256,512]{1,0:T(8,128)(2,1)} %bitcast.19), channel_id=1, source_target_pairs={{0,2},{1,3},{2,0},{3,1},{4,6},{5,7},{6,4},{7,5},{8,10},{9,11},{10,... | collective-permute-start | bytes 786440 | tf_op jit(solution)/shard_map/ppermute | solution.py:531
  5.7 10.9 %collective-permute-start.5 = (bf16[256,512]{1,0:T(8,128)(2,1)}, bf16[256,512]{1,0:T(8,128)(2,1)S(1)}, u32[]{:S(2)}, u32[]{:S(2)}) collective-permute-start(bf16[256,512]{1,0:T(8,128)(2,1)} %bitcast.22), channel_id=1, source_target_pairs={{0,4},{1,5},{2,6},{3,7},{4,0},{5,1},{6,2},{7,3},{8,12},{9,13},{10,... | collective-permute-start | bytes 786440 | tf_op jit(solution)/shard_map/ppermute | solution.py:531
  6.2 11.8 %collective-permute-start.3 = (bf16[256,512]{1,0:T(8,128)(2,1)}, bf16[256,512]{1,0:T(8,128)(2,1)S(1)}, u32[]{:S(2)}, u32[]{:S(2)}) collective-permute-start(bf16[256,512]{1,0:T(8,128)(2,1)} %bitcast.23), channel_id=1, source_target_pairs={{0,2},{1,3},{2,0},{3,1},{4,6},{5,7},{6,4},{7,5},{8,10},{9,11},{10,... | collective-permute-start | bytes 786440 | tf_op jit(solution)/shard_map/ppermute | solution.py:531
  6.2 14.5 %copy-start = (bf16[4,1024,512]{2,1,0:T(8,128)(2,1)S(1)}, bf16[4,1024,512]{2,1,0:T(8,128)(2,1)}, u32[]{:S(2)}) copy-start(bf16[4,1024,512]{2,1,0:T(8,128)(2,1)} %refs_2_.4) | copy-start | bytes 12582916
  18.0 1.5 %collective-permute-start.9 = (bf16[256,512]{1,0:T(8,128)(2,1)S(1)}, bf16[256,512]{1,0:T(8,128)(2,1)S(1)}, u32[]{:S(2)}, u32[]{:S(2)}) collective-permute-start(bf16[256,512]{1,0:T(8,128)(2,1)S(1)} %collective-permute-done.3.refs_7_), channel_id=1, source_target_pairs={{0,1},{1,0},{2,3},{3,2},{4,5},{5,4},{6,7},{7,6},{8,9},{9,8},{10,11... | collective-permute-start | bytes 786440 | tf_op jit(solution)/shard_map/ppermute | solution.py:531
  18.0 1.9 %collective-permute-start.10 = (bf16[256,512]{1,0:T(8,128)(2,1)S(1)}, bf16[256,512]{1,0:T(8,128)(2,1)S(1)}, u32[]{:S(2)}, u32[]{:S(2)}) collective-permute-start(bf16[256,512]{1,0:T(8,128)(2,1)S(1)} %collective-permute-done.4.refs_4_), channel_id=1, source_target_pairs={{0,1},{1,0},{2,3},{3,2},{4,5},{5,4},{6,7},{7,6},{8,9},{9,8},{10,11... | collective-permute-start | bytes 786440 | tf_op jit(solution)/shard_map/ppermute | solution.py:531
  18.5 1.8 %collective-permute-start.8 = (bf16[256,512]{1,0:T(8,128)(2,1)S(1)}, bf16[256,512]{1,0:T(8,128)(2,1)S(1)}, u32[]{:S(2)}, u32[]{:S(2)}) collective-permute-start(bf16[256,512]{1,0:T(8,128)(2,1)S(1)} %collective-permute-done.2.refs_3_), channel_id=1, source_target_pairs={{0,1},{1,0},{2,3},{3,2},{4,5},{5,4},{6,7},{7,6},{8,9},{9,8},{10,11... | collective-permute-start | bytes 786440 | tf_op jit(solution)/shard_map/ppermute | solution.py:531
  18.5 2.1 %collective-permute-start.11 = (bf16[256,512]{1,0:T(8,128)(2,1)S(1)}, bf16[256,512]{1,0:T(8,128)(2,1)S(1)}, u32[]{:S(2)}, u32[]{:S(2)}) collective-permute-start(bf16[256,512]{1,0:T(8,128)(2,1)S(1)} %collective-permute-done.5.refs_8_), channel_id=1, source_target_pairs={{0,1},{1,0},{2,3},{3,2},{4,5},{5,4},{6,7},{7,6},{8,9},{9,8},{10,11... | collective-permute-start | bytes 786440 | tf_op jit(solution)/shard_map/ppermute | solution.py:531
  20.7 8.7 %collective-permute-start.12 = (bf16[4,1024,512]{2,1,0:T(8,128)(2,1)S(1)}, bf16[4,1024,512]{2,1,0:T(8,128)(2,1)S(1)}, u32[]{:S(2)}, u32[]{:S(2)}) collective-permute-start(bf16[4,1024,512]{2,1,0:T(8,128)(2,1)S(1)} %copy-done), channel_id=1, source_target_pairs={{0,1},{1,0},{2,3},{3,2},{4,5},{5,4},{6,7},{7,6},{8,9},{9,8},{10,11... | collective-permute-start | bytes 12582920 | tf_op jit(solution)/shard_map/ppermute | solution.py:531
  20.8 8.6 %collective-permute-start.6 = (bf16[256,512]{1,0:T(8,128)(2,1)S(1)}, bf16[256,512]{1,0:T(8,128)(2,1)S(1)}, u32[]{:S(2)}, u32[]{:S(2)}) collective-permute-start(bf16[256,512]{1,0:T(8,128)(2,1)S(1)} %collective-permute-done.2.refs_3_), channel_id=1, source_target_pairs={{0,4},{1,5},{2,6},{3,7},{4,0},{5,1},{6,2},{7,3},{8,12},{9,13},{10,... | collective-permute-start | bytes 786440 | tf_op jit(solution)/shard_map/ppermute | solution.py:531
  21.1 8.3 %collective-permute-start.7 = (bf16[256,512]{1,0:T(8,128)(2,1)S(1)}, bf16[256,512]{1,0:T(8,128)(2,1)S(1)}, u32[]{:S(2)}, u32[]{:S(2)}) collective-permute-start(bf16[256,512]{1,0:T(8,128)(2,1)S(1)} %collective-permute-done.5.refs_8_), channel_id=1, source_target_pairs={{0,2},{1,3},{2,0},{3,1},{4,6},{5,7},{6,4},{7,5},{8,10},{9,11},{10,... | collective-permute-start | bytes 786440 | tf_op jit(solution)/shard_map/ppermute | solution.py:531
  22.8 8.5 %copy-start.1 = (bf16[4,1024,512]{2,1,0:T(8,128)(2,1)S(1)}, bf16[4,1024,512]{2,1,0:T(8,128)(2,1)}, u32[]{:S(2)}) copy-start(bf16[4,1024,512]{2,1,0:T(8,128)(2,1)} %refs_3_.4) | copy-start | bytes 12582916
  22.8 8.6 %copy-start.2 = (bf16[4,512,1024]{2,1,0:T(8,128)(2,1)S(1)}, bf16[4,512,1024]{2,1,0:T(8,128)(2,1)}, u32[]{:S(2)}) copy-start(bf16[4,512,1024]{2,1,0:T(8,128)(2,1)} %refs_4_.3) | copy-start | bytes 12582916
  29.4 1.5 %collective-permute-start.13 = (bf16[256,512]{1,0:T(8,128)(2,1)S(1)}, bf16[256,512]{1,0:T(8,128)(2,1)S(1)}, u32[]{:S(2)}, u32[]{:S(2)}) collective-permute-start(bf16[256,512]{1,0:T(8,128)(2,1)S(1)} %collective-permute-done.6.refs_3_), channel_id=1, source_target_pairs={{0,1},{1,0},{2,3},{3,2},{4,5},{5,4},{6,7},{7,6},{8,9},{9,8},{10,11... | collective-permute-start | bytes 786440 | tf_op jit(solution)/shard_map/ppermute | solution.py:531
  29.4 1.9 %collective-permute-start.14 = (bf16[256,512]{1,0:T(8,128)(2,1)S(1)}, bf16[256,512]{1,0:T(8,128)(2,1)S(1)}, u32[]{:S(2)}, u32[]{:S(2)}) collective-permute-start(bf16[256,512]{1,0:T(8,128)(2,1)S(1)} %collective-permute-done.7.refs_5_), channel_id=1, source_target_pairs={{0,1},{1,0},{2,3},{3,2},{4,5},{5,4},{6,7},{7,6},{8,9},{9,8},{10,11... | collective-permute-start | bytes 786440 | tf_op jit(solution)/shard_map/ppermute | solution.py:531
  31.3 10.0 %collective-permute-start.17 = (bf16[4,1024,512]{2,1,0:T(8,128)(2,1)S(1)}, bf16[4,1024,512]{2,1,0:T(8,128)(2,1)S(1)}, u32[]{:S(2)}, u32[]{:S(2)}) collective-permute-start(bf16[4,1024,512]{2,1,0:T(8,128)(2,1)S(1)} %copy-done.1), channel_id=1, source_target_pairs={{0,1},{1,0},{2,3},{3,2},{4,5},{5,4},{6,7},{7,6},{8,9},{9,8},{10,11... | collective-permute-start | bytes 12582920 | tf_op jit(solution)/shard_map/ppermute | solution.py:531
  31.5 13.0 %collective-permute-start.18 = (bf16[4,512,1024]{2,1,0:T(8,128)(2,1)S(1)}, bf16[4,512,1024]{2,1,0:T(8,128)(2,1)S(1)}, u32[]{:S(2)}, u32[]{:S(2)}) collective-permute-start(bf16[4,512,1024]{2,1,0:T(8,128)(2,1)S(1)} %copy-done.2), channel_id=1, source_target_pairs={{0,1},{1,0},{2,3},{3,2},{4,5},{5,4},{6,7},{7,6},{8,9},{9,8},{10,11... | collective-permute-start | bytes 12582920 | tf_op jit(solution)/shard_map/ppermute | solution.py:531
  38.1 14.7 %collective-permute-start.16 = (bf16[272,1024]{1,0:T(8,128)(2,1)S(1)}, bf16[272,1024]{1,0:T(8,128)(2,1)S(1)}, u32[]{:S(2)}, u32[]{:S(2)}) collective-permute-start(bf16[272,1024]{1,0:T(8,128)(2,1)S(1)} %get-tuple-element.67.refs_0_), channel_id=1, source_target_pairs={{0,4},{1,5},{2,6},{3,7},{4,0},{5,1},{6,2},{7,3},{8,12},{9,13},{10,... | collective-permute-start | bytes 1671176 | tf_op jit(solution)/shard_map/ppermute | solution.py:531
  39.9 14.4 %collective-permute-start.15 = (bf16[272,1024]{1,0:T(8,128)(2,1)S(1)}, bf16[272,1024]{1,0:T(8,128)(2,1)S(1)}, u32[]{:S(2)}, u32[]{:S(2)}) collective-permute-start(bf16[272,1024]{1,0:T(8,128)(2,1)S(1)} %get-tuple-element.67.refs_0_), channel_id=1, source_target_pairs={{0,2},{1,3},{2,0},{3,1},{4,6},{5,7},{6,4},{7,5},{8,10},{9,11},{10,... | collective-permute-start | bytes 1671176 | tf_op jit(solution)/shard_map/ppermute | solution.py:531
  54.3 10.5 %collective-permute-start.19 = (bf16[128,1024]{1,0:T(8,128)(2,1)S(1)}, bf16[128,1024]{1,0:T(8,128)(2,1)S(1)}, u32[]{:S(2)}, u32[]{:S(2)}) collective-permute-start(bf16[128,1024]{1,0:T(8,128)(2,1)S(1)} %slice.6), channel_id=1, source_target_pairs={{0,4},{1,5},{2,6},{3,7},{4,0},{5,1},{6,2},{7,3},{8,12},{9,13},{10,... | collective-permute-start | bytes 786440 | tf_op jit(solution)/shard_map/ppermute | solution.py:531
  54.7 10.2 %collective-permute-start.20 = (bf16[144,1024]{1,0:T(8,128)(2,1)S(1)}, bf16[144,1024]{1,0:T(8,128)(2,1)S(1)}, u32[]{:S(2)}, u32[]{:S(2)}) collective-permute-start(bf16[144,1024]{1,0:T(8,128)(2,1)S(1)} %slice.7), channel_id=1, source_target_pairs={{0,2},{1,3},{2,0},{3,1},{4,6},{5,7},{6,4},{7,5},{8,10},{9,11},{10,... | collective-permute-start | bytes 884744 | tf_op jit(solution)/shard_map/ppermute | solution.py:531
  64.8 14.9 %collective-permute-start.21 = (bf16[256,1024]{1,0:T(8,128)(2,1)S(1)}, bf16[256,1024]{1,0:T(8,128)(2,1)S(1)}, u32[]{:S(2)}, u32[]{:S(2)}) collective-permute-start(bf16[256,1024]{1,0:T(8,128)(2,1)S(1)} %get-tuple-element.77), channel_id=1, source_target_pairs={{0,2},{1,3},{2,0},{3,1},{4,6},{5,7},{6,4},{7,5},{8,10},{9,11},{10,... | collective-permute-start | bytes 1572872 | tf_op jit(solution)/shard_map/ppermute | solution.py:531
  65.2 14.6 %collective-permute-start.22 = (bf16[256,1024]{1,0:T(8,128)(2,1)S(1)}, bf16[256,1024]{1,0:T(8,128)(2,1)S(1)}, u32[]{:S(2)}, u32[]{:S(2)}) collective-permute-start(bf16[256,1024]{1,0:T(8,128)(2,1)S(1)} %get-tuple-element.78), channel_id=1, source_target_pairs={{0,4},{1,5},{2,6},{3,7},{4,0},{5,1},{6,2},{7,3},{8,12},{9,13},{10,... | collective-permute-start | bytes 1572872 | tf_op jit(solution)/shard_map/ppermute | solution.py:531
  72.9 16.4 %collective-permute-start.23 = (bf16[256,1024]{1,0:T(8,128)(2,1)S(1)}, bf16[256,1024]{1,0:T(8,128)(2,1)S(1)}, u32[]{:S(2)}, u32[]{:S(2)}) collective-permute-start(bf16[256,1024]{1,0:T(8,128)(2,1)S(1)} %experts.5), channel_id=1, source_target_pairs={{0,6},{1,7},{2,4},{3,5},{4,2},{5,3},{6,0},{7,1},{8,14},{9,15},{10,... | collective-permute-start | bytes 1572872 | tf_op jit(solution)/shard_map/ppermute | solution.py:531

commit v8 on v7

--- a/solution.py
+++ b/solution.py
@@ -589,8 +589,10 @@
     rows_x, rows_y = swap(moe_in, ACROSS_X), swap(moe_in, ACROSS_Y)
     weights = [list(owned), list(mated)]
     (own,) = run_experts([[moe_in]], weights, out_type=F32)
+    rows_y, own = ordered(rows_y, own)
+    high_xy = swap(rows_y[half:], ACROSS_X)
     rows_x, rows_y, own = ordered(rows_x, rows_y, own)
-    low_xy, high_xy = swap(rows_x[:half], ACROSS_Y), swap(rows_y[half:], ACROSS_X)
+    low_xy = swap(rows_x[:half], ACROSS_Y)
     to_x, to_y = run_experts([[rows_x], [rows_y]], weights)
     low_xy, high_xy, to_x, to_y = ordered(low_xy, high_xy, to_x, to_y)
     from_x, from_y = swap(to_x, ACROSS_X), swap(to_y, ACROSS_Y)

time: 90.5 us -> 90.4 us (level)
  no operation moved by 1% of the time
where the time goes in v8:
time: 90.4 us; the launch traced here: 90.2 us
  Pallas kernels  41.2 us (46%)
  waiting for transfers between devices  28.4 us (31%)
  starting transfers between devices  18.7 us (21%)
  other arithmetic  1.18 us (1%)
    ppermute x24, waiting for transfers between devices, swap(): lax.ppermute(array, 'req', [(i, i ^ mask) for i in range(lax.axis_size('r...  28.4 us
    pallas_call x3, Pallas kernels, run_experts(): pl.pallas_call(functools.partial(experts_kernel, sources, pieces, owners,...  20.3 us
    ppermute x24, starting transfers between devices, swap(): lax.ppermute(array, 'req', [(i, i ^ mask) for i in range(lax.axis_size('r...  18.7 us
    pallas_call x2, Pallas kernels, attend_far(): pl.pallas_call(functools.partial(far_kernel, blocks, last), grid=(1,), in...  12.2 us
    pallas_call x1, Pallas kernels, attend_near(): pl.pallas_call(near_kernel, grid=(1,), in_specs=[whole_spec(tok_count, wi...  8.65 us
  transfers between devices with their start and end apart: 24, of which 14 were waited for; matrix products, arithmetic and copies ran while one was open for 0% of the time, Pallas kernels for 46%

profile of v8, /device:TPU:0, one launch (start us, length us, event | category | flops | bytes accessed | tf_op | source)
XLA Modules:
  0.0 90.2 jit_solution(7740416798578081955)
XLA Ops:
  0.6 0.5 collective-permute-start
  1.2 2.9 %collective-permute-start.4 = (bf16[256,512]{1,0:T(8,128)(2,1)}, bf16[256,512]{1,0:T(8,128)(2,1)S(1)}, u32[]{:S(2)}, u32[]{:S(2)}) collective-permute-start(bf16[256,512]{1,0:T(8,128)(2,1)} %bitcast.18), channel_id=1, source_target_pairs={{0,4},{1,5},{2,6},{3,7},{4,0},{5,1},{6,2},{7,3},{8,12},{9,13},{10,... | collective-permute-start | bytes 786440 | tf_op jit(solution)/shard_map/ppermute | solution.py:531
  4.2 1.5 %collective-permute-start.2 = (bf16[256,512]{1,0:T(8,128)(2,1)}, bf16[256,512]{1,0:T(8,128)(2,1)S(1)}, u32[]{:S(2)}, u32[]{:S(2)}) collective-permute-start(bf16[256,512]{1,0:T(8,128)(2,1)} %bitcast.19), channel_id=1, source_target_pairs={{0,2},{1,3},{2,0},{3,1},{4,6},{5,7},{6,4},{7,5},{8,10},{9,11},{10,... | collective-permute-start | bytes 786440 | tf_op jit(solution)/shard_map/ppermute | solution.py:531
  5.7 0.5 collective-permute-start.5
  6.2 8.6 %attend_near.1 = (bf16[8,512,128]{2,1,0:T(8,128)(2,1)S(1)}, f32[8,1,512]{2,1,0:T(1,128)S(1)}, f32[8,80,512]{2,1,0:T(8,128)S(1)}) custom-call(bf16[256,1024]{1,0:T(8,128)(2,1)} %bitcast.15, f32[1,1024]{1,0:T(1,128)} %bitcast.27, bf16[1024,1024]{1,0:T(8,128)(2,1)} %refs_2_.1, bf16[1024,512]{1,0:T(8,128)(2,1)} %refs_3_.1, bf16[1024,512]{1,0:T(8,128)(2,1)} %refs_4_.1, ...), custom_call_target="tpu_custom_call" | custom-call | flops 4194304000 | bytes 6291456 | tf_op jit(solution)/shard_map/attend_near/pallas_call | solution.py:334
  14.9 1.7 %collective-permute-done.5.refs_8_ = bf16[256,512]{1,0:T(8,128)(2,1)S(1)} collective-permute-done((bf16[256,512]{1,0:T(8,128)(2,1)}, bf16[256,512]{1,0:T(8,128)(2,1)S(1)}, u32[]{:S(2)}, u32[]{:S(2)}) %collective-permute-start.5) | collective-permute-done | bytes 262176 | tf_op jit(solution)/shard_map/ppermute | solution.py:531
  16.6 1.5 %collective-permute-done.3.refs_7_ = bf16[256,512]{1,0:T(8,128)(2,1)S(1)} collective-permute-done((bf16[256,512]{1,0:T(8,128)(2,1)}, bf16[256,512]{1,0:T(8,128)(2,1)S(1)}, u32[]{:S(2)}, u32[]{:S(2)}) %collective-permute-start.3) | collective-permute-done | bytes 262176 | tf_op jit(solution)/shard_map/ppermute | solution.py:531
  18.0 0.5 collective-permute-start.10
  18.5 0.5 collective-permute-start.11
  19.0 0.5 collective-permute-done.9.refs_9_
  21.1 1.7 %collective-permute-start.7 = (bf16[256,512]{1,0:T(8,128)(2,1)S(1)}, bf16[256,512]{1,0:T(8,128)(2,1)S(1)}, u32[]{:S(2)}, u32[]{:S(2)}) collective-permute-start(bf16[256,512]{1,0:T(8,128)(2,1)S(1)} %collective-permute-done.5.refs_8_), channel_id=1, source_target_pairs={{0,2},{1,3},{2,0},{3,1},{4,6},{5,7},{6,4},{7,5},{8,10},{9,11},{10,... | collective-permute-start | bytes 786440 | tf_op jit(solution)/shard_map/ppermute | solution.py:531
  22.8 5.9 %attend_far.2 = (f32[8,1,512]{2,1,0:T(1,128)S(1)}, f32[8,80,512]{2,1,0:T(8,128)S(1)}) custom-call(bf16[8,512,128]{2,1,0:T(8,128)(2,1)S(1)} %get-tuple-element.45.refs_0_, f32[8,1,512]{2,1,0:T(1,128)S(1)} %get-tuple-element.53.refs_1_, f32[8,80,512]{2,1,0:T(8,128)S(1)} %get-tuple-element.54.refs_2_, bf16[256,512]{1,0:T(8,128)(2,1)S(1)} %collective-permute-done.2.refs_3_, ...), custom_call_target="tpu_custom_call" | custom-call | flops 5033164800 | bytes 4194304 | tf_op jit(solution)/shard_map/attend_far/pallas_call | solution.py:411
  28.8 0.6 collective-permute-done.6.refs_3_
  29.4 0.5 collective-permute-start.14
  29.9 1.0 %collective-permute-done.13.refs_4_ = bf16[256,512]{1,0:T(8,128)(2,1)S(1)} collective-permute-done((bf16[256,512]{1,0:T(8,128)(2,1)S(1)}, bf16[256,512]{1,0:T(8,128)(2,1)S(1)}, u32[]{:S(2)}, u32[]{:S(2)}) %collective-permute-start.13) | collective-permute-done | bytes 262176 | tf_op jit(solution)/shard_map/ppermute | solution.py:531
  31.8 6.3 %attend_far.3 = (bf16[256,1024]{1,0:T(8,128)(2,1)}, bf16[256,1024]{1,0:T(8,128)(2,1)}, bf16[272,1024]{1,0:T(8,128)(2,1)S(1)}) custom-call(bf16[8,512,128]{2,1,0:T(8,128)(2,1)S(1)} %get-tuple-element.45.refs_0_, f32[8,1,512]{2,1,0:T(1,128)S(1)} %get-tuple-element.61.refs_1_, f32[8,80,512]{2,1,0:T(8,128)S(1)} %get-tuple-element.62.refs_2_, ...), custom_call_target="tpu_custom_call" | custom-call | flops 2516582400 | bytes 4194304 | tf_op jit(solution)/shard_map/attend_far/pallas_call | solution.py:411
  38.1 1.7 %collective-permute-start.16 = (bf16[272,1024]{1,0:T(8,128)(2,1)S(1)}, bf16[272,1024]{1,0:T(8,128)(2,1)S(1)}, u32[]{:S(2)}, u32[]{:S(2)}) collective-permute-start(bf16[272,1024]{1,0:T(8,128)(2,1)S(1)} %get-tuple-element.69.refs_0_), channel_id=1, source_target_pairs={{0,4},{1,5},{2,6},{3,7},{4,0},{5,1},{6,2},{7,3},{8,12},{9,13},{10,... | collective-permute-start | bytes 1671176 | tf_op jit(solution)/shard_map/ppermute | solution.py:531
  39.9 1.5 %collective-permute-start.15 = (bf16[272,1024]{1,0:T(8,128)(2,1)S(1)}, bf16[272,1024]{1,0:T(8,128)(2,1)S(1)}, u32[]{:S(2)}, u32[]{:S(2)}) collective-permute-start(bf16[272,1024]{1,0:T(8,128)(2,1)S(1)} %get-tuple-element.69.refs_0_), channel_id=1, source_target_pairs={{0,2},{1,3},{2,0},{3,1},{4,6},{5,7},{6,4},{7,5},{8,10},{9,11},{10,... | collective-permute-start | bytes 1671176 | tf_op jit(solution)/shard_map/ppermute | solution.py:531
  41.4 3.1 %collective-permute-done.18.refs_6_.refs_7_ = bf16[4,512,1024]{2,1,0:T(8,128)(2,1)S(1)} collective-permute-done((bf16[4,512,1024]{2,1,0:T(8,128)(2,1)S(1)}, bf16[4,512,1024]{2,1,0:T(8,128)(2,1)S(1)}, u32[]{:S(2)}, u32[]{:S(2)}) %collective-permute-start.18) | collective-permute-done | bytes 4194336 | tf_op jit(solution)/shard_map/ppermute | solution.py:531
  44.5 6.0 %experts.3 = f32[256,1024]{1,0:T(8,128)S(1)} custom-call(bf16[272,1024]{1,0:T(8,128)(2,1)S(1)} %get-tuple-element.69.refs_0_, bf16[4,1024,512]{2,1,0:T(8,128)(2,1)S(1)} %copy-done, bf16[4,1024,512]{2,1,0:T(8,128)(2,1)S(1)} %copy-done.1, bf16[4,512,1024]{2,1,0:T(8,128)(2,1)S(1)} %copy-done.2, ...), custom_call_target="tpu_custom_call" | custom-call | flops 12582912000 | bytes 31457280 | tf_op jit(solution)/shard_map/experts/pallas_call | solution.py:510
  50.5 2.3 %collective-permute-done.16.refs_1_ = bf16[272,1024]{1,0:T(8,128)(2,1)S(1)} collective-permute-done((bf16[272,1024]{1,0:T(8,128)(2,1)S(1)}, bf16[272,1024]{1,0:T(8,128)(2,1)S(1)}, u32[]{:S(2)}, u32[]{:S(2)}) %collective-permute-start.16) | collective-permute-done | bytes 557088 | tf_op jit(solution)/shard_map/ppermute | solution.py:531
  52.8 1.4 %collective-permute-done.15.refs_0_ = bf16[272,1024]{1,0:T(8,128)(2,1)S(1)} collective-permute-done((bf16[272,1024]{1,0:T(8,128)(2,1)S(1)}, bf16[272,1024]{1,0:T(8,128)(2,1)S(1)}, u32[]{:S(2)}, u32[]{:S(2)}) %collective-permute-start.15) | collective-permute-done | bytes 557088 | tf_op jit(solution)/shard_map/ppermute | solution.py:531
  54.3 0.4 collective-permute-start.19
  54.7 1.7 %collective-permute-start.20 = (bf16[144,1024]{1,0:T(8,128)(2,1)S(1)}, bf16[144,1024]{1,0:T(8,128)(2,1)S(1)}, u32[]{:S(2)}, u32[]{:S(2)}) collective-permute-start(bf16[144,1024]{1,0:T(8,128)(2,1)S(1)} %slice.7), channel_id=1, source_target_pairs={{0,2},{1,3},{2,0},{3,1},{4,6},{5,7},{6,4},{7,5},{8,10},{9,11},{10,... | collective-permute-start | bytes 884744 | tf_op jit(solution)/shard_map/ppermute | solution.py:531
  56.3 8.4 %experts.4 = (bf16[256,1024]{1,0:T(8,128)(2,1)S(1)}, bf16[256,1024]{1,0:T(8,128)(2,1)S(1)}) custom-call(bf16[272,1024]{1,0:T(8,128)(2,1)S(1)} %collective-permute-done.15.refs_0_, bf16[272,1024]{1,0:T(8,128)(2,1)S(1)} %collective-permute-done.16.refs_1_, bf16[4,1024,512]{2,1,0:T(8,128)(2,1)S(1)} %copy-done, bf16[4,1024,512]{2,1,0:T(8,128)(2,1)S(1)} %copy-done.1, ...), custom_call_target="tpu_custom_call" | custom-call | flops 12582912000 | bytes 31457280 | tf_op jit(solution)/shard_map/experts/pallas_call | solution.py:510
  64.8 0.4 collective-permute-start.21
  65.2 1.7 %collective-permute-start.22 = (bf16[256,1024]{1,0:T(8,128)(2,1)S(1)}, bf16[256,1024]{1,0:T(8,128)(2,1)S(1)}, u32[]{:S(2)}, u32[]{:S(2)}) collective-permute-start(bf16[256,1024]{1,0:T(8,128)(2,1)S(1)} %get-tuple-element.82), channel_id=1, source_target_pairs={{0,4},{1,5},{2,6},{3,7},{4,0},{5,1},{6,2},{7,3},{8,12},{9,13},{10,... | collective-permute-start | bytes 1572872 | tf_op jit(solution)/shard_map/ppermute | solution.py:531
  66.9 6.0 %experts.5 = bf16[256,1024]{1,0:T(8,128)(2,1)S(1)} custom-call(bf16[128,1024]{1,0:T(8,128)(2,1)S(1)} %collective-permute-done.19.refs_0_, bf16[144,1024]{1,0:T(8,128)(2,1)S(1)} %collective-permute-done.20.refs_1_, bf16[4,1024,512]{2,1,0:T(8,128)(2,1)S(1)} %copy-done, bf16[4,1024,512]{2,1,0:T(8,128)(2,1)S(1)} %copy-done.1, ...), custom_call_target="tpu_custom_call" | custom-call | flops 12582912000 | bytes 31457280 | tf_op jit(solution)/shard_map/experts/pallas_call | solution.py:510
  72.8 1.5 %collective-permute-start.23 = (bf16[256,1024]{1,0:T(8,128)(2,1)S(1)}, bf16[256,1024]{1,0:T(8,128)(2,1)S(1)}, u32[]{:S(2)}, u32[]{:S(2)}) collective-permute-start(bf16[256,1024]{1,0:T(8,128)(2,1)S(1)} %experts.5), channel_id=1, source_target_pairs={{0,6},{1,7},{2,4},{3,5},{4,2},{5,3},{6,0},{7,1},{8,14},{9,15},{10,... | collective-permute-start | bytes 1572872 | tf_op jit(solution)/shard_map/ppermute | solution.py:531
  74.4 5.3 %collective-permute-done.21 = bf16[256,1024]{1,0:T(8,128)(2,1)S(1)} collective-permute-done((bf16[256,1024]{1,0:T(8,128)(2,1)S(1)}, bf16[256,1024]{1,0:T(8,128)(2,1)S(1)}, u32[]{:S(2)}, u32[]{:S(2)}) %collective-permute-start.21) | collective-permute-done | bytes 524320 | tf_op jit(solution)/shard_map/ppermute | solution.py:531
  79.9 9.3 %collective-permute-done.23 = bf16[256,1024]{1,0:T(8,128)(2,1)S(1)} collective-permute-done((bf16[256,1024]{1,0:T(8,128)(2,1)S(1)}, bf16[256,1024]{1,0:T(8,128)(2,1)S(1)}, u32[]{:S(2)}, u32[]{:S(2)}) %collective-permute-start.23) | collective-permute-done | bytes 524320 | tf_op jit(solution)/shard_map/ppermute | solution.py:531
  89.3 0.9 %fusion = bf16[1,256,1024]{2,1,0:T(8,128)(2,1)} fusion(f32[256,1024]{1,0:T(8,128)S(1)} %convert_add_fusion, bf16[256,1024]{1,0:T(8,128)(2,1)S(1)} %collective-permute-done.23), kind=kLoop, calls=%fused_computation.2 | loop fusion | flops 786432 | bytes 2097152 | tf_op jit(solution)/shard_map/broadcast_in_dim | solution.py:603
  (32 shorter events, 2.9 us)
Async XLA Ops:
  0.6 5.5 %collective-permute-start = (bf16[256,512]{1,0:T(8,128)(2,1)}, bf16[256,512]{1,0:T(8,128)(2,1)S(1)}, u32[]{:S(2)}, u32[]{:S(2)}) collective-permute-start(bf16[256,512]{1,0:T(8,128)(2,1)} %bitcast.17), channel_id=1, source_target_pairs={{0,1},{1,0},{2,3},{3,2},{4,5},{5,4},{6,7},{7,6},{8,9},{9,8},{10,11... | collective-permute-start | bytes 786440 | tf_op jit(solution)/shard_map/ppermute | solution.py:531
  1.2 5.1 %collective-permute-start.1 = (bf16[256,512]{1,0:T(8,128)(2,1)}, bf16[256,512]{1,0:T(8,128)(2,1)S(1)}, u32[]{:S(2)}, u32[]{:S(2)}) collective-permute-start(bf16[256,512]{1,0:T(8,128)(2,1)} %bitcast.21), channel_id=1, source_target_pairs={{0,1},{1,0},{2,3},{3,2},{4,5},{5,4},{6,7},{7,6},{8,9},{9,8},{10,11... | collective-permute-start | bytes 786440 | tf_op jit(solution)/shard_map/ppermute | solution.py:531
  1.2 13.6 %collective-permute-start.4 = (bf16[256,512]{1,0:T(8,128)(2,1)}, bf16[256,512]{1,0:T(8,128)(2,1)S(1)}, u32[]{:S(2)}, u32[]{:S(2)}) collective-permute-start(bf16[256,512]{1,0:T(8,128)(2,1)} %bitcast.18), channel_id=1, source_target_pairs={{0,4},{1,5},{2,6},{3,7},{4,0},{5,1},{6,2},{7,3},{8,12},{9,13},{10,... | collective-permute-start | bytes 786440 | tf_op jit(solution)/shard_map/ppermute | solution.py:531
  4.2 10.7 %collective-permute-start.2 = (bf16[256,512]{1,0:T(8,128)(2,1)}, bf16[256,512]{1,0:T(8,128)(2,1)S(1)}, u32[]{:S(2)}, u32[]{:S(2)}) collective-permute-start(bf16[256,512]{1,0:T(8,128)(2,1)} %bitcast.19), channel_id=1, source_target_pairs={{0,2},{1,3},{2,0},{3,1},{4,6},{5,7},{6,4},{7,5},{8,10},{9,11},{10,... | collective-permute-start | bytes 786440 | tf_op jit(solution)/shard_map/ppermute | solution.py:531
  5.7 10.9 %collective-permute-start.5 = (bf16[256,512]{1,0:T(8,128)(2,1)}, bf16[256,512]{1,0:T(8,128)(2,1)S(1)}, u32[]{:S(2)}, u32[]{:S(2)}) collective-permute-start(bf16[256,512]{1,0:T(8,128)(2,1)} %bitcast.22), channel_id=1, source_target_pairs={{0,4},{1,5},{2,6},{3,7},{4,0},{5,1},{6,2},{7,3},{8,12},{9,13},{10,... | collective-permute-start | bytes 786440 | tf_op jit(solution)/shard_map/ppermute | solution.py:531
  6.2 11.8 %collective-permute-start.3 = (bf16[256,512]{1,0:T(8,128)(2,1)}, bf16[256,512]{1,0:T(8,128)(2,1)S(1)}, u32[]{:S(2)}, u32[]{:S(2)}) collective-permute-start(bf16[256,512]{1,0:T(8,128)(2,1)} %bitcast.23), channel_id=1, source_target_pairs={{0,2},{1,3},{2,0},{3,1},{4,6},{5,7},{6,4},{7,5},{8,10},{9,11},{10,... | collective-permute-start | bytes 786440 | tf_op jit(solution)/shard_map/ppermute | solution.py:531
  6.2 14.5 %copy-start = (bf16[4,1024,512]{2,1,0:T(8,128)(2,1)S(1)}, bf16[4,1024,512]{2,1,0:T(8,128)(2,1)}, u32[]{:S(2)}) copy-start(bf16[4,1024,512]{2,1,0:T(8,128)(2,1)} %refs_2_.4) | copy-start | bytes 12582916
  18.0 1.5 %collective-permute-start.9 = (bf16[256,512]{1,0:T(8,128)(2,1)S(1)}, bf16[256,512]{1,0:T(8,128)(2,1)S(1)}, u32[]{:S(2)}, u32[]{:S(2)}) collective-permute-start(bf16[256,512]{1,0:T(8,128)(2,1)S(1)} %collective-permute-done.3.refs_7_), channel_id=1, source_target_pairs={{0,1},{1,0},{2,3},{3,2},{4,5},{5,4},{6,7},{7,6},{8,9},{9,8},{10,11... | collective-permute-start | bytes 786440 | tf_op jit(solution)/shard_map/ppermute | solution.py:531
  18.0 1.9 %collective-permute-start.10 = (bf16[256,512]{1,0:T(8,128)(2,1)S(1)}, bf16[256,512]{1,0:T(8,128)(2,1)S(1)}, u32[]{:S(2)}, u32[]{:S(2)}) collective-permute-start(bf16[256,512]{1,0:T(8,128)(2,1)S(1)} %collective-permute-done.4.refs_4_), channel_id=1, source_target_pairs={{0,1},{1,0},{2,3},{3,2},{4,5},{5,4},{6,7},{7,6},{8,9},{9,8},{10,11... | collective-permute-start | bytes 786440 | tf_op jit(solution)/shard_map/ppermute | solution.py:531
  18.5 1.8 %collective-permute-start.8 = (bf16[256,512]{1,0:T(8,128)(2,1)S(1)}, bf16[256,512]{1,0:T(8,128)(2,1)S(1)}, u32[]{:S(2)}, u32[]{:S(2)}) collective-permute-start(bf16[256,512]{1,0:T(8,128)(2,1)S(1)} %collective-permute-done.2.refs_3_), channel_id=1, source_target_pairs={{0,1},{1,0},{2,3},{3,2},{4,5},{5,4},{6,7},{7,6},{8,9},{9,8},{10,11... | collective-permute-start | bytes 786440 | tf_op jit(solution)/shard_map/ppermute | solution.py:531
  18.5 2.1 %collective-permute-start.11 = (bf16[256,512]{1,0:T(8,128)(2,1)S(1)}, bf16[256,512]{1,0:T(8,128)(2,1)S(1)}, u32[]{:S(2)}, u32[]{:S(2)}) collective-permute-start(bf16[256,512]{1,0:T(8,128)(2,1)S(1)} %collective-permute-done.5.refs_8_), channel_id=1, source_target_pairs={{0,1},{1,0},{2,3},{3,2},{4,5},{5,4},{6,7},{7,6},{8,9},{9,8},{10,11... | collective-permute-start | bytes 786440 | tf_op jit(solution)/shard_map/ppermute | solution.py:531
  20.7 8.7 %collective-permute-start.12 = (bf16[4,1024,512]{2,1,0:T(8,128)(2,1)S(1)}, bf16[4,1024,512]{2,1,0:T(8,128)(2,1)S(1)}, u32[]{:S(2)}, u32[]{:S(2)}) collective-permute-start(bf16[4,1024,512]{2,1,0:T(8,128)(2,1)S(1)} %copy-done), channel_id=1, source_target_pairs={{0,1},{1,0},{2,3},{3,2},{4,5},{5,4},{6,7},{7,6},{8,9},{9,8},{10,11... | collective-permute-start | bytes 12582920 | tf_op jit(solution)/shard_map/ppermute | solution.py:531
  20.8 8.6 %collective-permute-start.6 = (bf16[256,512]{1,0:T(8,128)(2,1)S(1)}, bf16[256,512]{1,0:T(8,128)(2,1)S(1)}, u32[]{:S(2)}, u32[]{:S(2)}) collective-permute-start(bf16[256,512]{1,0:T(8,128)(2,1)S(1)} %collective-permute-done.2.refs_3_), channel_id=1, source_target_pairs={{0,4},{1,5},{2,6},{3,7},{4,0},{5,1},{6,2},{7,3},{8,12},{9,13},{10,... | collective-permute-start | bytes 786440 | tf_op jit(solution)/shard_map/ppermute | solution.py:531
  21.1 8.3 %collective-permute-start.7 = (bf16[256,512]{1,0:T(8,128)(2,1)S(1)}, bf16[256,512]{1,0:T(8,128)(2,1)S(1)}, u32[]{:S(2)}, u32[]{:S(2)}) collective-permute-start(bf16[256,512]{1,0:T(8,128)(2,1)S(1)} %collective-permute-done.5.refs_8_), channel_id=1, source_target_pairs={{0,2},{1,3},{2,0},{3,1},{4,6},{5,7},{6,4},{7,5},{8,10},{9,11},{10,... | collective-permute-start | bytes 786440 | tf_op jit(solution)/shard_map/ppermute | solution.py:531
  22.8 8.5 %copy-start.1 = (bf16[4,1024,512]{2,1,0:T(8,128)(2,1)S(1)}, bf16[4,1024,512]{2,1,0:T(8,128)(2,1)}, u32[]{:S(2)}) copy-start(bf16[4,1024,512]{2,1,0:T(8,128)(2,1)} %refs_3_.4) | copy-start | bytes 12582916
  22.8 8.6 %copy-start.2 = (bf16[4,512,1024]{2,1,0:T(8,128)(2,1)S(1)}, bf16[4,512,1024]{2,1,0:T(8,128)(2,1)}, u32[]{:S(2)}) copy-start(bf16[4,512,1024]{2,1,0:T(8,128)(2,1)} %refs_4_.3) | copy-start | bytes 12582916
  29.4 1.5 %collective-permute-start.13 = (bf16[256,512]{1,0:T(8,128)(2,1)S(1)}, bf16[256,512]{1,0:T(8,128)(2,1)S(1)}, u32[]{:S(2)}, u32[]{:S(2)}) collective-permute-start(bf16[256,512]{1,0:T(8,128)(2,1)S(1)} %collective-permute-done.6.refs_3_), channel_id=1, source_target_pairs={{0,1},{1,0},{2,3},{3,2},{4,5},{5,4},{6,7},{7,6},{8,9},{9,8},{10,11... | collective-permute-start | bytes 786440 | tf_op jit(solution)/shard_map/ppermute | solution.py:531
  29.4 1.9 %collective-permute-start.14 = (bf16[256,512]{1,0:T(8,128)(2,1)S(1)}, bf16[256,512]{1,0:T(8,128)(2,1)S(1)}, u32[]{:S(2)}, u32[]{:S(2)}) collective-permute-start(bf16[256,512]{1,0:T(8,128)(2,1)S(1)} %collective-permute-done.7.refs_5_), channel_id=1, source_target_pairs={{0,1},{1,0},{2,3},{3,2},{4,5},{5,4},{6,7},{7,6},{8,9},{9,8},{10,11... | collective-permute-start | bytes 786440 | tf_op jit(solution)/shard_map/ppermute | solution.py:531
  31.3 10.0 %collective-permute-start.17 = (bf16[4,1024,512]{2,1,0:T(8,128)(2,1)S(1)}, bf16[4,1024,512]{2,1,0:T(8,128)(2,1)S(1)}, u32[]{:S(2)}, u32[]{:S(2)}) collective-permute-start(bf16[4,1024,512]{2,1,0:T(8,128)(2,1)S(1)} %copy-done.1), channel_id=1, source_target_pairs={{0,1},{1,0},{2,3},{3,2},{4,5},{5,4},{6,7},{7,6},{8,9},{9,8},{10,11... | collective-permute-start | bytes 12582920 | tf_op jit(solution)/shard_map/ppermute | solution.py:531
  31.5 13.0 %collective-permute-start.18 = (bf16[4,512,1024]{2,1,0:T(8,128)(2,1)S(1)}, bf16[4,512,1024]{2,1,0:T(8,128)(2,1)S(1)}, u32[]{:S(2)}, u32[]{:S(2)}) collective-permute-start(bf16[4,512,1024]{2,1,0:T(8,128)(2,1)S(1)} %copy-done.2), channel_id=1, source_target_pairs={{0,1},{1,0},{2,3},{3,2},{4,5},{5,4},{6,7},{7,6},{8,9},{9,8},{10,11... | collective-permute-start | bytes 12582920 | tf_op jit(solution)/shard_map/ppermute | solution.py:531
  38.1 14.7 %collective-permute-start.16 = (bf16[272,1024]{1,0:T(8,128)(2,1)S(1)}, bf16[272,1024]{1,0:T(8,128)(2,1)S(1)}, u32[]{:S(2)}, u32[]{:S(2)}) collective-permute-start(bf16[272,1024]{1,0:T(8,128)(2,1)S(1)} %get-tuple-element.69.refs_0_), channel_id=1, source_target_pairs={{0,4},{1,5},{2,6},{3,7},{4,0},{5,1},{6,2},{7,3},{8,12},{9,13},{10,... | collective-permute-start | bytes 1671176 | tf_op jit(solution)/shard_map/ppermute | solution.py:531
  39.9 14.4 %collective-permute-start.15 = (bf16[272,1024]{1,0:T(8,128)(2,1)S(1)}, bf16[272,1024]{1,0:T(8,128)(2,1)S(1)}, u32[]{:S(2)}, u32[]{:S(2)}) collective-permute-start(bf16[272,1024]{1,0:T(8,128)(2,1)S(1)} %get-tuple-element.69.refs_0_), channel_id=1, source_target_pairs={{0,2},{1,3},{2,0},{3,1},{4,6},{5,7},{6,4},{7,5},{8,10},{9,11},{10,... | collective-permute-start | bytes 1671176 | tf_op jit(solution)/shard_map/ppermute | solution.py:531
  54.3 10.5 %collective-permute-start.19 = (bf16[128,1024]{1,0:T(8,128)(2,1)S(1)}, bf16[128,1024]{1,0:T(8,128)(2,1)S(1)}, u32[]{:S(2)}, u32[]{:S(2)}) collective-permute-start(bf16[128,1024]{1,0:T(8,128)(2,1)S(1)} %slice.6), channel_id=1, source_target_pairs={{0,4},{1,5},{2,6},{3,7},{4,0},{5,1},{6,2},{7,3},{8,12},{9,13},{10,... | collective-permute-start | bytes 786440 | tf_op jit(solution)/shard_map/ppermute | solution.py:531
  54.7 10.1 %collective-permute-start.20 = (bf16[144,1024]{1,0:T(8,128)(2,1)S(1)}, bf16[144,1024]{1,0:T(8,128)(2,1)S(1)}, u32[]{:S(2)}, u32[]{:S(2)}) collective-permute-start(bf16[144,1024]{1,0:T(8,128)(2,1)S(1)} %slice.7), channel_id=1, source_target_pairs={{0,2},{1,3},{2,0},{3,1},{4,6},{5,7},{6,4},{7,5},{8,10},{9,11},{10,... | collective-permute-start | bytes 884744 | tf_op jit(solution)/shard_map/ppermute | solution.py:531
  64.8 14.9 %collective-permute-start.21 = (bf16[256,1024]{1,0:T(8,128)(2,1)S(1)}, bf16[256,1024]{1,0:T(8,128)(2,1)S(1)}, u32[]{:S(2)}, u32[]{:S(2)}) collective-permute-start(bf16[256,1024]{1,0:T(8,128)(2,1)S(1)} %get-tuple-element.81), channel_id=1, source_target_pairs={{0,2},{1,3},{2,0},{3,1},{4,6},{5,7},{6,4},{7,5},{8,10},{9,11},{10,... | collective-permute-start | bytes 1572872 | tf_op jit(solution)/shard_map/ppermute | solution.py:531
  65.2 14.5 %collective-permute-start.22 = (bf16[256,1024]{1,0:T(8,128)(2,1)S(1)}, bf16[256,1024]{1,0:T(8,128)(2,1)S(1)}, u32[]{:S(2)}, u32[]{:S(2)}) collective-permute-start(bf16[256,1024]{1,0:T(8,128)(2,1)S(1)} %get-tuple-element.82), channel_id=1, source_target_pairs={{0,4},{1,5},{2,6},{3,7},{4,0},{5,1},{6,2},{7,3},{8,12},{9,13},{10,... | collective-permute-start | bytes 1572872 | tf_op jit(solution)/shard_map/ppermute | solution.py:531
  72.8 16.4 %collective-permute-start.23 = (bf16[256,1024]{1,0:T(8,128)(2,1)S(1)}, bf16[256,1024]{1,0:T(8,128)(2,1)S(1)}, u32[]{:S(2)}, u32[]{:S(2)}) collective-permute-start(bf16[256,1024]{1,0:T(8,128)(2,1)S(1)} %experts.5), channel_id=1, source_target_pairs={{0,6},{1,7},{2,4},{3,5},{4,2},{5,3},{6,0},{7,1},{8,14},{9,15},{10,... | collective-permute-start | bytes 1572872 | tf_op jit(solution)/shard_map/ppermute | solution.py:531
